TPU v7x, 32 devices: a whole 2x2x4 slice. The times are simulated.
32 devices in a mesh: rep: 2 (over y), dp: 4 (over z), fsdp: 2 (over x), tp: 2 (over core).
Axes of the slice: x: 2, y: 2, z: 4, core: 2. Of those that a mesh axis runs over, the one named last changes fastest.
Arguments:
- tokens: bfloat16 [4096, 8192], P(('rep', 'dp', 'fsdp'), 'tp'), parts along dimension 0, may hold values from -6 to 6
- output_gradient: bfloat16 [4096, 512], P(('rep', 'dp', 'fsdp')), parts along dimension 0, may hold values from -6 to 6
- frozen_value_weight: bfloat16 [8192, 512], P('tp', 'fsdp'), may hold values from -0.0625 to 0.0625
- adapter_down_weight: bfloat16 [32, 16, 8192], P(('rep', 'dp'), None, 'tp'), parts along dimension 0, may hold values from -0.0625 to 0.0625
- adapter_up_weight: bfloat16 [32, 16, 512], P(('rep', 'dp'), None, 'tp'), parts along dimension 0, may hold values from -0.25 to 0.25
- deal: int32 [4096, 1], P(('rep', 'dp', 'fsdp')), parts along dimension 0, may hold values from 0 to 3; in each aligned block of 256 rows (0 to 255, 256 to 511, ...) at most 80 rows name the same one
- row_local_job: int32 [4096], P(('rep', 'dp', 'fsdp')), parts along dimension 0, may hold values from 0 to 3
Outputs:
- value_output: bfloat16 [4096, 512], P(('rep', 'dp', 'fsdp'), 'tp'), parts along dimension 0
- input_gradient: bfloat16 [4096, 8192], P(('rep', 'dp', 'fsdp'), 'tp'), parts along dimension 0
- down_weight_gradient: float32 [32, 16, 8192], P(('rep', 'dp'), 'fsdp', 'tp'), parts along dimension 0
- up_weight_gradient: float32 [32, 16, 512], P(('rep', 'dp'), 'fsdp', 'tp'), parts along dimension 0
There are 2 independent parts, one for each index of `rep`. A program takes and returns all parts, laid end to end along the dimension named above; an argument that names none is the same for every part. Nothing has to cross between parts.
Inputs may be any that keep to these rules, and one draw needn't show every extreme that they name: `deal`: within the rows of one device (aligned blocks of 256 rows) no index is named by more than 80 rows, and in some block one index is named exactly 80 times.
All inputs are finite; a program needn't handle non-finite values.
Results may differ from a plain program's by a relative error of at most 0.0034.
Values may be sent and summed in bfloat16 or wider, within the bound.
No kernel may reach another device: no remote copies, remote signals or barrier semaphores. Data moves between devices by JAX's collectives and lax.ppermute only.
A program may use at most 64 MiB of HBM per device.

v0:
```python
import jax
import jax.numpy as jnp
from jax import lax
from jax.sharding import PartitionSpec as P

ADAPTER_SCALE = 2.0


def local(
    tokens,
    output_gradient,
    frozen_value_weight,
    adapter_down_weight,
    adapter_up_weight,
    deal,
    row_local_job,
):
    row_count = tokens.shape[0]
    width_half = tokens.shape[1]
    jobs_owned_here = adapter_down_weight.shape[0]
    rank_extent = adapter_down_weight.shape[1]
    partial_value_rows = adapter_up_weight.shape[2]
    partner_count = lax.axis_size("dp")
    job_slot_count = 5 * row_count // (4 * partner_count)
    slot_total = partner_count * job_slot_count
    tp_index = lax.axis_index("tp")
    grad_part = lax.dynamic_slice_in_dim(
        output_gradient, tp_index * partial_value_rows, partial_value_rows, 1
    )
    contract_last = (((1,), (1,)), ((), ()))
    full_weight = lax.all_gather(frozen_value_weight, "fsdp", axis=1, tiled=True)
    frozen_output = jnp.dot(tokens, full_weight, preferred_element_type=jnp.float32)
    frozen_gradient = lax.dot_general(
        output_gradient, full_weight, contract_last, preferred_element_type=jnp.float32
    )
    value_share = lax.psum_scatter(frozen_output, "tp", scatter_dimension=1, tiled=True)
    row_dest = deal[:, 0]
    dest_onehot = (row_dest[:, None] == jnp.arange(partner_count, dtype=jnp.int32)[None, :]).astype(
        jnp.int32
    )
    earlier = jnp.cumsum(dest_onehot, axis=0) - dest_onehot
    slot_rank = jnp.sum(earlier * dest_onehot, axis=1)
    row_slot = row_dest * job_slot_count + slot_rank
    row_ids = jnp.arange(row_count, dtype=jnp.int32)
    slot_full = jnp.zeros((slot_total,), jnp.int32).at[row_slot].set(1)
    source_row = jnp.zeros((slot_total,), jnp.int32).at[row_slot].set(row_ids)
    is_full = slot_full > 0
    send_tokens = jnp.where(is_full[:, None], tokens[source_row], jnp.zeros((), jnp.bfloat16))
    send_grads = jnp.where(is_full[:, None], grad_part[source_row], jnp.zeros((), jnp.bfloat16))
    send_jobs = jnp.where(is_full, row_local_job[source_row], -1)
    got_tokens, got_grads, got_jobs = (
        lax.all_to_all(
            send_tokens.reshape(partner_count, job_slot_count, width_half),
            "dp",
            split_axis=0,
            concat_axis=0,
            tiled=True,
        ),
        lax.all_to_all(
            send_grads.reshape(partner_count, job_slot_count, partial_value_rows),
            "dp",
            split_axis=0,
            concat_axis=0,
            tiled=True,
        ),
        lax.all_to_all(
            send_jobs.reshape(partner_count, job_slot_count),
            "dp",
            split_axis=0,
            concat_axis=0,
            tiled=True,
        ),
    )
    got_tokens = got_tokens.reshape(slot_total, width_half)
    got_grads = got_grads.reshape(slot_total, partial_value_rows)
    got_jobs = got_jobs.reshape(slot_total)
    job_pick = got_jobs[:, None] == jnp.arange(jobs_owned_here, dtype=jnp.int32)[None, :]
    flat_down_weight = adapter_down_weight.reshape(jobs_owned_here * rank_extent, width_half)
    flat_up_weight = adapter_up_weight.reshape(jobs_owned_here * rank_extent, partial_value_rows)
    every_down = lax.dot_general(
        got_tokens, flat_down_weight, contract_last, preferred_element_type=jnp.float32
    )
    every_up = lax.dot_general(
        got_grads, flat_up_weight, contract_last, preferred_element_type=jnp.float32
    )
    pick_mask = job_pick.astype(jnp.float32)[:, :, None]
    low_partial = jnp.sum(
        every_down.reshape(slot_total, jobs_owned_here, rank_extent) * pick_mask, axis=1
    )
    grad_partial = jnp.sum(
        every_up.reshape(slot_total, jobs_owned_here, rank_extent) * pick_mask, axis=1
    )
    low_rank, grad_rank = lax.psum((low_partial, grad_partial), "tp")
    pick_narrow = job_pick.astype(jnp.bfloat16)[:, :, None]
    wide_rank_rows = (pick_narrow * low_rank.astype(jnp.bfloat16)[:, None, :]).reshape(
        slot_total, jobs_owned_here * rank_extent
    )
    wide_gradient = (pick_narrow * grad_rank.astype(jnp.bfloat16)[:, None, :]).reshape(
        slot_total, jobs_owned_here * rank_extent
    )
    adapter_output = (
        ADAPTER_SCALE * jnp.dot(wide_rank_rows, flat_up_weight, preferred_element_type=jnp.float32)
    ).astype(jnp.bfloat16)
    adapter_gradient = (
        ADAPTER_SCALE * jnp.dot(wide_gradient, flat_down_weight, preferred_element_type=jnp.float32)
    ).astype(jnp.bfloat16)
    contract_first = (((0,), (0,)), ((), ()))
    down_product = ADAPTER_SCALE * lax.dot_general(
        wide_gradient, got_tokens, contract_first, preferred_element_type=jnp.float32
    )
    up_product = ADAPTER_SCALE * lax.dot_general(
        wide_rank_rows, got_grads, contract_first, preferred_element_type=jnp.float32
    )
    down_share, up_share = (
        lax.psum_scatter(
            down_product.reshape(jobs_owned_here, rank_extent, width_half),
            "fsdp",
            scatter_dimension=1,
            tiled=True,
        ),
        lax.psum_scatter(
            up_product.reshape(jobs_owned_here, rank_extent, partial_value_rows),
            "fsdp",
            scatter_dimension=1,
            tiled=True,
        ),
    )
    back_out, back_grad = (
        lax.all_to_all(
            adapter_output.reshape(partner_count, job_slot_count, partial_value_rows),
            "dp",
            split_axis=0,
            concat_axis=0,
            tiled=True,
        ),
        lax.all_to_all(
            adapter_gradient.reshape(partner_count, job_slot_count, width_half),
            "dp",
            split_axis=0,
            concat_axis=0,
            tiled=True,
        ),
    )
    row_out = back_out.reshape(slot_total, partial_value_rows)[row_slot]
    row_grad = back_grad.reshape(slot_total, width_half)[row_slot]
    value_output = (value_share + row_out.astype(jnp.float32)).astype(jnp.bfloat16)
    input_gradient = (frozen_gradient + row_grad.astype(jnp.float32)).astype(jnp.bfloat16)
    return (value_output, input_gradient, down_share, up_share)


def solution(mesh):
    in_specs = (
        P(("rep", "dp", "fsdp"), "tp"),
        P(("rep", "dp", "fsdp"), None),
        P("tp", "fsdp"),
        P(("rep", "dp"), None, "tp"),
        P(("rep", "dp"), None, "tp"),
        P(("rep", "dp", "fsdp"), None),
        P(("rep", "dp", "fsdp")),
    )
    out_specs = (
        P(("rep", "dp", "fsdp"), "tp"),
        P(("rep", "dp", "fsdp"), "tp"),
        P(("rep", "dp"), "fsdp", "tp"),
        P(("rep", "dp"), "fsdp", "tp"),
    )
    return jax.shard_map(local, mesh=mesh, in_specs=in_specs, out_specs=out_specs, check_vma=False)
```

profile of v0, /device:TPU:0, one launch (start us, length us, event | category | flops | bytes accessed | tf_op | source)
XLA Modules:
  0.0 205.7 jit_solution(3009427540645369944)
XLA Ops:
  7.2 0.0 copy-start
  7.2 0.8 compare_convert_fusion
  8.0 1.2 reduce-window.6
  9.2 0.1 slice.18
  9.3 0.1 copy.13
  9.4 0.1 copy.14
  9.5 0.1 add_bitcast_fusion
  9.6 0.7 fusion.11
  10.3 0.7 compare_select_fusion
  11.0 1.4 scatter_custom_fusion.1
  12.4 1.4 scatter_custom_fusion
  13.8 3.6 %gather_fusion = s32[320]{0:T(512)S(1)} fusion(s32[256]{0:T(256)} %param.13, s32[1024]{0:T(1024)S(1)} %pad_clamp_fusion.1), kind=kCustom, calls=%fused_computation | custom fusion | bytes 3840 | tf_op jit(solution)/shard_map/gather | solution.py:50
  17.5 0.7 all_to_all.18
  18.1 6.3 %all-to-all-start = ((s32[4,1,80]{2,1,0:T(1,128)}), s32[4,1,80]{2,1,0:T(1,128)S(1)}, u32[]{:S(2)}, u32[]{:S(2)}) async-start(s32[4,1,80]{2,1,0:T(1,128)} %all_to_all.18), calls=%async_computation.1 | async-start | bytes 4096 | tf_op jit(solution)/shard_map/all_to_all | solution.py:66
  24.5 0.9 constant_dynamic-slice_fusion
  25.4 2.0 gather_fusion.3
  27.4 0.1 broadcast_in_dim.53
  27.5 0.8 broadcast_select_fusion.1
  28.3 0.0 copy-done
  28.3 3.8 %gather_fusion.1 = bf16[320,4096]{1,0:T(8,128)(2,1)} fusion(bf16[256,4096]{1,0:T(8,128)(2,1)S(1)} %copy-done, s32[1024]{0:T(1024)S(1)} %pad_clamp_fusion.1), kind=kCustom, calls=%fused_computation.1 | custom fusion | bytes 5244160 | tf_op jit(solution)/shard_map/gather | solution.py:48
  32.1 0.0 all-to-all-done
  32.1 5.1 %all-to-all-start.3 = ((bf16[4,80,256]{2,1,0:T(8,128)(2,1)}), bf16[4,80,256]{2,1,0:T(8,128)(2,1)S(1)}, u32[]{:S(2)}, u32[]{:S(2)}) async-start(bf16[4,80,256]{2,1,0:T(8,128)(2,1)} %broadcast_select_fusion.1), calls=%async_computation.4 | async-start | bytes 327680 | tf_op jit(solution)/shard_map/all_to_all | solution.py:59
  37.2 3.5 %broadcast_select_fusion = bf16[4,80,4096]{2,1,0:T(8,128)(2,1)} fusion(bf16[4,80,4096]{2,1,0:T(8,128)(2,1)} %bitcast.65, pred[4,80]{1,0:T(4,128)(4,1)S(1)} %broadcast_in_dim.53), kind=kLoop, calls=%fused_computation.13 | loop fusion | flops 1310720 | bytes 5243200 | tf_op jit(solution)/shard_map/jit(_where)/select_n | solution.py:48
  40.7 0.0 copy-start.2
  40.7 0.0 copy-start.3
  40.7 2.7 %all-to-all-done.3 = bf16[4,80,256]{2,1,0:T(8,128)(2,1)S(1)} async-done(((bf16[4,80,256]{2,1,0:T(8,128)(2,1)}), bf16[4,80,256]{2,1,0:T(8,128)(2,1)S(1)}, u32[]{:S(2)}, u32[]{:S(2)}) %all-to-all-start.3) | async-done | bytes 163872 | tf_op jit(solution)/shard_map/all_to_all | solution.py:59
  43.4 4.5 %all-to-all-start.1 = ((bf16[4,80,4096]{2,1,0:T(8,128)(2,1)}), bf16[4,80,4096]{2,1,0:T(8,128)(2,1)}, u32[]{:S(2)}, u32[]{:S(2)}) async-start(bf16[4,80,4096]{2,1,0:T(8,128)(2,1)} %broadcast_select_fusion), calls=%async_computation.2 | async-start | bytes 5242880 | tf_op jit(solution)/shard_map/all_to_all | solution.py:52
  48.0 0.0 all-gather.2.cloned.1.call-start
  48.0 0.7 all-gather.2.cloned.1.call-update
  48.7 0.5 broadcast.113
  49.2 0.7 reduce.3
  49.9 0.1 eq.55
  50.0 0.0 copy-done.2
  50.0 0.2 fusion.6
  50.2 55.4 %all-to-all-done.1 = bf16[4,80,4096]{2,1,0:T(8,128)(2,1)} async-done(((bf16[4,80,4096]{2,1,0:T(8,128)(2,1)}), bf16[4,80,4096]{2,1,0:T(8,128)(2,1)}, u32[]{:S(2)}, u32[]{:S(2)}) %all-to-all-start.1) | async-done | bytes 2621472 | tf_op jit(solution)/shard_map/all_to_all | solution.py:52
  105.6 0.0 copy-done.3
  105.6 2.6 %fusion.5 = f32[320,16]{0,1:T(8,128)S(1)} fusion(bf16[320,4096,1]{1,0,2:T(8,128)(2,1)} %bitcast.8, bf16[4,16,4096]{2,1,0:T(8,128)(2,1)S(1)} %copy-done.3, f32[320,4]{0,1:T(4,128)S(1)} %get-tuple-element.11), kind=kOutput, calls=%fused_computation.20 | convolution fusion | flops 167808000 | bytes 3171328 | tf_op jit(solution)/shard_map/dot_general | solution.py:80
  108.2 3.5 %all-reduce = (bf16[320,16]{0,1:T(8,128)(2,1)S(1)}, bf16[320,16]{0,1:T(8,128)(2,1)S(1)}) all-reduce(f32[320,16]{0,1:T(8,128)S(1)} %fusion.5, f32[320,16]{0,1:T(8,128)S(1)} %fusion.6), channel_id=1, replica_groups=mesh['rep'=2,'dp'=4,'fsdp'=2,'tp'=2] {'tp'}, use_global_device_ids=true, to_apply=%region_7.8 | all-reduce | flops 10240 | bytes 61440 | tf_op jit(solution)/shard_map/psum | solution.py:93
  111.7 0.9 fusion.4
  112.6 3.3 %all-to-all-start.2 = ((bf16[4,80,256]{2,1,0:T(8,128)(2,1)}), bf16[4,80,256]{2,1,0:T(8,128)(2,1)S(1)}, u32[]{:S(2)}, u32[]{:S(2)}) async-start(bf16[4,80,256]{2,1,0:T(8,128)(2,1)} %bitcast.10), calls=%async_computation.3 | async-start | bytes 327680 | tf_op jit(solution)/shard_map/all_to_all | solution.py:129
  116.0 2.3 %fusion.1 = bf16[320,4096]{1,0:T(8,128)(2,1)} fusion(bf16[4,16,4096]{2,1,0:T(8,128)(2,1)S(1)} %copy-done.3, bf16[320,16]{0,1:T(8,128)(2,1)S(1)} %get-tuple-element.5, bf16[320,4]{0,1:T(4,128)(2,1)S(1)} %get-tuple-element.10), kind=kOutput, calls=%fused_computation.10 | convolution fusion | flops 170414080 | bytes 3158528 | tf_op jit(solution)/shard_map/dot_general | solution.py:105
  118.3 4.7 %all-to-all-done.2 = bf16[4,80,256]{2,1,0:T(8,128)(2,1)S(1)} async-done(((bf16[4,80,256]{2,1,0:T(8,128)(2,1)}), bf16[4,80,256]{2,1,0:T(8,128)(2,1)S(1)}, u32[]{:S(2)}, u32[]{:S(2)}) %all-to-all-start.2) | async-done | bytes 163872 | tf_op jit(solution)/shard_map/all_to_all | solution.py:129
  123.1 4.5 %all-to-all-start.4 = ((bf16[4,80,4096]{2,1,0:T(8,128)(2,1)}), bf16[4,80,4096]{2,1,0:T(8,128)(2,1)}, u32[]{:S(2)}, u32[]{:S(2)}) async-start(bf16[4,80,4096]{2,1,0:T(8,128)(2,1)} %bitcast.68), calls=%async_computation.5 | async-start | bytes 5242880 | tf_op jit(solution)/shard_map/all_to_all | solution.py:136
  127.6 0.0 reduce-scatter.4.cloned.1.call-start
  127.7 0.0 all-gather.2.cloned.1.call-done
  127.7 4.2 %fusion.16 = f32[256,512]{1,0:T(8,128)} fusion(bf16[256,4096]{1,0:T(8,128)(2,1)S(1)} %copy-done, bf16[4096,512]{1,0:T(8,128)(2,1)} %all-gather.2.cloned.1.call-done), kind=kOutput, calls=%fused_computation.47 | convolution fusion | flops 1073741824 | bytes 6815744 | tf_op jit(solution)/shard_map/dot_general | solution.py:32
  131.9 0.0 reduce-scatter.4.cloned.1.call-update
  132.0 0.0 reduce-scatter.8.cloned.1.call-start
  132.0 0.8 convolution_multiply_fusion.3
  132.8 0.0 reduce-scatter.8.cloned.1.call-update
  132.8 0.2 reduce-scatter.6.cloned.1.call-start
  133.1 3.4 %convolution_multiply_fusion = f32[64,4096]{1,0:T(8,128)} fusion(bf16[320,64]{0,1:T(8,128)(2,1)S(1)} %bitcast.73, bf16[320,4096]{1,0:T(8,128)(2,1)} %bitcast.7), kind=kOutput, calls=%fused_computation.12 | convolution fusion | flops 168034304 | bytes 3710976 | tf_op jit(solution)/shard_map/dot_general | solution.py:108
  136.4 0.0 reduce-scatter.6.cloned.1.call-update
  136.5 1.2 gather_fusion.2
  137.6 3.8 %reduce-scatter.4.cloned.1.call-done = f32[256,256]{1,0:T(8,128)} async-done(((f32[256,512]{1,0:T(8,128)}), f32[256,256]{1,0:T(8,128)}) %reduce-scatter.4.cloned.1.call-update) | async-done | bytes 262160 | tf_op jit(solution)/shard_map/reduce_scatter | solution.py:36
  141.4 1.6 add_convert_fusion
  143.0 43.3 %all-to-all-done.4 = bf16[4,80,4096]{2,1,0:T(8,128)(2,1)} async-done(((bf16[4,80,4096]{2,1,0:T(8,128)(2,1)}), bf16[4,80,4096]{2,1,0:T(8,128)(2,1)}, u32[]{:S(2)}, u32[]{:S(2)}) %all-to-all-start.4) | async-done | bytes 2621472 | tf_op jit(solution)/shard_map/all_to_all | solution.py:136
  186.4 0.0 copy-start.1
  186.4 7.3 %gather_fusion.4 = bf16[256,4096]{1,0:T(8,128)(2,1)} fusion(bf16[320,4096]{1,0:T(8,128)(2,1)} %bitcast.17, s32[1024]{0:T(1024)S(1)} %pad_clamp_fusion), kind=kCustom, calls=%fused_computation.4 | custom fusion | bytes 4195328 | tf_op jit(solution)/shard_map/gather | solution.py:145
  193.7 0.0 copy-done.1
  193.7 5.5 %fusion.2 = bf16[256,4096]{1,0:T(8,128)(2,1)} fusion(bf16[256,512]{1,0:T(8,128)(2,1)S(1)} %copy-done.1, bf16[4096,512]{1,0:T(8,128)(2,1)} %all-gather.2.cloned.1.call-done, bf16[256,4096]{1,0:T(8,128)(2,1)} %gather_fusion.4), kind=kOutput, calls=%fused_computation.11 | convolution fusion | flops 1076887552 | bytes 8650752 | tf_op jit(solution)/shard_map/dot_general | solution.py:33
  199.2 0.0 reduce-scatter.8.cloned.1.call-done
  199.2 0.0 reduce-scatter.6.cloned.1.call-done
  (10 shorter events, 0.1 us)
Async XLA Ops:
  7.2 21.1 %copy-start = (bf16[256,4096]{1,0:T(8,128)(2,1)S(1)}, bf16[256,4096]{1,0:T(8,128)(2,1)}, u32[]{:S(2)}) copy-start(bf16[256,4096]{1,0:T(8,128)(2,1)} %param.7) | copy-start | bytes 6291460
  18.1 14.0 %all-to-all-start = ((s32[4,1,80]{2,1,0:T(1,128)}), s32[4,1,80]{2,1,0:T(1,128)S(1)}, u32[]{:S(2)}, u32[]{:S(2)}) async-start(s32[4,1,80]{2,1,0:T(1,128)} %all_to_all.18), calls=%async_computation.1 | async-start | bytes 4096 | tf_op jit(solution)/shard_map/all_to_all | solution.py:66
  32.1 11.3 %all-to-all-start.3 = ((bf16[4,80,256]{2,1,0:T(8,128)(2,1)}), bf16[4,80,256]{2,1,0:T(8,128)(2,1)S(1)}, u32[]{:S(2)}, u32[]{:S(2)}) async-start(bf16[4,80,256]{2,1,0:T(8,128)(2,1)} %broadcast_select_fusion.1), calls=%async_computation.4 | async-start | bytes 327680 | tf_op jit(solution)/shard_map/all_to_all | solution.py:59
  40.7 9.3 %copy-start.2 = (bf16[4,16,256]{2,1,0:T(8,128)(2,1)S(1)}, bf16[4,16,256]{2,1,0:T(8,128)(2,1)}, u32[]{:S(2)}) copy-start(bf16[4,16,256]{2,1,0:T(8,128)(2,1)} %param.11) | copy-start | bytes 98308
  40.7 64.9 %copy-start.3 = (bf16[4,16,4096]{2,1,0:T(8,128)(2,1)S(1)}, bf16[4,16,4096]{2,1,0:T(8,128)(2,1)}, u32[]{:S(2)}) copy-start(bf16[4,16,4096]{2,1,0:T(8,128)(2,1)} %param.10) | copy-start | bytes 1572868
  43.4 62.1 %all-to-all-start.1 = ((bf16[4,80,4096]{2,1,0:T(8,128)(2,1)}), bf16[4,80,4096]{2,1,0:T(8,128)(2,1)}, u32[]{:S(2)}, u32[]{:S(2)}) async-start(bf16[4,80,4096]{2,1,0:T(8,128)(2,1)} %broadcast_select_fusion), calls=%async_computation.2 | async-start | bytes 5242880 | tf_op jit(solution)/shard_map/all_to_all | solution.py:52
  48.0 79.7 %all-gather.2.cloned.1.call-start = ((), (), s32[]{:S(2)}) async-start(), calls=%async_computation.8 | async-start | bytes 6291456 | tf_op jit(solution)/shard_map/all_gather | solution.py:31
  112.6 10.4 %all-to-all-start.2 = ((bf16[4,80,256]{2,1,0:T(8,128)(2,1)}), bf16[4,80,256]{2,1,0:T(8,128)(2,1)S(1)}, u32[]{:S(2)}, u32[]{:S(2)}) async-start(bf16[4,80,256]{2,1,0:T(8,128)(2,1)} %bitcast.10), calls=%async_computation.3 | async-start | bytes 327680 | tf_op jit(solution)/shard_map/all_to_all | solution.py:129
  123.1 63.3 %all-to-all-start.4 = ((bf16[4,80,4096]{2,1,0:T(8,128)(2,1)}), bf16[4,80,4096]{2,1,0:T(8,128)(2,1)}, u32[]{:S(2)}, u32[]{:S(2)}) async-start(bf16[4,80,4096]{2,1,0:T(8,128)(2,1)} %bitcast.68), calls=%async_computation.5 | async-start | bytes 5242880 | tf_op jit(solution)/shard_map/all_to_all | solution.py:136
  127.6 13.8 %reduce-scatter.4.cloned.1.call-start = ((), (), s32[]{:S(2)}) async-start(), calls=%async_computation.9 | async-start | bytes 786432 | tf_op jit(solution)/shard_map/reduce_scatter | solution.py:36
  132.0 67.2 %reduce-scatter.8.cloned.1.call-start = ((), (), s32[]{:S(2)}) async-start(), calls=%async_computation.11 | async-start | bytes 98304 | tf_op jit(solution)/shard_map/reduce_scatter | solution.py:121
  132.8 66.3 %reduce-scatter.6.cloned.1.call-start = ((), (), s32[]{:S(2)}) async-start(), calls=%async_computation.10 | async-start | bytes 1572864 | tf_op jit(solution)/shard_map/reduce_scatter | solution.py:115
  186.4 7.3 %copy-start.1 = (bf16[256,512]{1,0:T(8,128)(2,1)S(1)}, bf16[256,512]{1,0:T(8,128)(2,1)}, u32[]{:S(2)}) copy-start(bf16[256,512]{1,0:T(8,128)(2,1)} %param.8) | copy-start | bytes 786436
Sparse Core Ops, SparseCore 0:
  50.4 58.1 all-gather.1
  132.1 9.2 reduce-scatter.3
  144.2 11.0 reduce-scatter.7
  158.1 20.3 reduce-scatter.5
where the time goes:
time: 207 us; the launch traced here: 206 us
  waiting for transfers between devices  111 us (54%)
  starting transfers between devices  24.2 us (12%)
  local copies, waits for them, and re-layouts  23.3 us (11%)
  matrix products  19.9 us (10%)
  between operations  13.9 us (7%)
  other arithmetic  10.2 us (5%)
  blocking collectives  3.51 us (2%)
    all_to_all x1, waiting for transfers between devices, local(): lax.all_to_all(send_tokens.reshape(partner_count, job_slot_count, width_h...  55.4 us
    all_to_all x1, waiting for transfers between devices, local(): lax.all_to_all(adapter_gradient.reshape(partner_count, job_slot_count, wi...  43.3 us
    gather x1, local copies, waits for them, and re-layouts, local(): row_grad = back_grad.reshape(slot_total, width_half)[row_slot]  7.32 us
    all_to_all x1, starting transfers between devices, local(): lax.all_to_all(send_jobs.reshape(partner_count, job_slot_count), 'dp', sp...  6.32 us
    dot_general x1, matrix products, local(): lax.dot_general(output_gradient, full_weight, contract_last, preferred_el...  5.48 us
    all_to_all x1, starting transfers between devices, local(): lax.all_to_all(send_grads.reshape(partner_count, job_slot_count, partial_...  5.09 us
    all_to_all x1, waiting for transfers between devices, local(): lax.all_to_all(adapter_output.reshape(partner_count, job_slot_count, part...  4.73 us
    all_to_all x1, starting transfers between devices, local(): lax.all_to_all(send_tokens.reshape(partner_count, job_slot_count, width_h...  4.55 us
  transfers between devices with their start and end apart: 9, of which 5 were waited for; matrix products, arithmetic and copies ran while one was open for 21% of the time, Pallas kernels for 0%

commit v1 on v0

--- a/solution.py
+++ b/solution.py
@@ -6,7 +6,131 @@
 ADAPTER_SCALE = 2.0
 
 
-def local(
+CONTRACT_LAST = (((1,), (1,)), ((), ()))
+CONTRACT_FIRST = (((0,), (0,)), ((), ()))
+
+
+def swap(extent, flip=1):
+    return [(i, i ^ flip) for i in range(extent)]
+
+
+def dot(left, right, dims=(((1,), (0,)), ((), ()))):
+    return lax.dot_general(left, right, dims, preferred_element_type=jnp.float32)
+
+
+def gather_adapters(
+    tokens,
+    output_gradient,
+    frozen_value_weight,
+    adapter_down_weight,
+    adapter_up_weight,
+    deal,
+    row_local_job,
+):
+    rows, width_half = tokens.shape
+    jobs, rank, features = adapter_up_weight.shape
+    span = jobs * rank
+    rep_index, dp_index = lax.axis_index("rep"), lax.axis_index("dp")
+    fsdp_index, tp_index = lax.axis_index("fsdp"), lax.axis_index("tp")
+    down = adapter_down_weight.reshape(span, width_half)
+    up = adapter_up_weight.reshape(span, features)
+    up_pair = jnp.stack([up, lax.ppermute(up, "tp", swap(2))])
+    ups = [up_pair] + [lax.ppermute(up_pair, "dp", swap(4, k)) for k in (1, 2, 3)]
+    outward = [(1, 0), (2, 3)]
+    middle = [(1, 2), (2, 1)]
+    down_next = lax.ppermute(down, "dp", swap(4))
+    down_cross = lax.ppermute(down, "dp", middle)
+    down_cross2 = lax.ppermute(down_next, "dp", middle)
+    down_out = lax.ppermute(down_cross, "dp", outward)
+    down_out2 = lax.ppermute(down_cross2, "dp", outward)
+    downs = [down, down_next, down_cross + down_out, down_cross2 + down_out2]
+    mid_index = jnp.where(dp_index < 2, 2, 1)
+    end_index = jnp.where(dp_index < 2, 3, 0)
+    holders = [dp_index, dp_index ^ 1, mid_index, end_index]
+    weight_half = width_half // 2
+    piece = weight_half // 2
+    sent_half = lax.dynamic_slice_in_dim(frozen_value_weight, rep_index * weight_half, weight_half, 0)
+    deal_row = deal.reshape(1, rows)
+    job_row = row_local_job.reshape(1, rows)
+    job_mask = (jnp.arange(span, dtype=jnp.int32) // rank)[:, None] == job_row
+    grad_mine = lax.dynamic_slice_in_dim(output_gradient, tp_index * features, features, 1)
+    grad_other = lax.dynamic_slice_in_dim(output_gradient, (1 - tp_index) * features, features, 1)
+    grad_sum = jnp.zeros((span, rows), jnp.float32)
+    for k in range(4):
+        every = dot(ups[k][0], grad_mine, CONTRACT_LAST) + dot(ups[k][1], grad_other, CONTRACT_LAST)
+        grad_sum = grad_sum + jnp.where(deal_row == (dp_index ^ k), every, 0)
+    grad_rank = jnp.where(job_mask, grad_sum, 0).astype(jnp.bfloat16)
+    zero = jnp.zeros((), jnp.bfloat16)
+
+    def wide_of(narrow, k):
+        return jnp.where(deal_row == holders[k], narrow, zero)
+
+    halves = grad_rank.reshape(jobs, 2, rank // 2, rows)
+    kept = lax.dynamic_index_in_dim(halves, fsdp_index, 1, False).reshape(span // 2, rows)
+    sent = lax.dynamic_index_in_dim(halves, 1 - fsdp_index, 1, False).reshape(span // 2, rows)
+
+    def down_part(narrow, ks):
+        wide = jnp.concatenate([wide_of(narrow, k) for k in ks])
+        return ADAPTER_SCALE * dot(wide, tokens)
+
+    send_far = down_part(sent, (3, 2)).astype(jnp.bfloat16)
+    send_near = down_part(sent, (1, 0)).astype(jnp.bfloat16)
+    keep_far = down_part(kept, (3, 2))
+    keep_near = down_part(kept, (1, 0))
+    got_first = lax.ppermute(sent_half[:piece], "fsdp", swap(2))
+    got_far = lax.ppermute(send_far, "fsdp", swap(2))
+    got_near = lax.ppermute(send_near, "fsdp", swap(2))
+    second, _ = lax.optimization_barrier((sent_half[piece:], send_near))
+    got_second = lax.ppermute(second, "fsdp", swap(2))
+    relay_first = lax.ppermute(got_first, "rep", swap(2))
+    relay_second = lax.ppermute(got_second, "rep", swap(2))
+    far = (keep_far + got_far.astype(jnp.float32)).astype(jnp.bfloat16)
+    near = keep_near + got_near.astype(jnp.float32)
+    s2 = span // 2
+    inward = [(0, 1), (3, 2)]
+    in_end = lax.ppermute(far[:s2], "dp", inward)
+    in_mid = lax.ppermute(far[s2:], "dp", inward)
+    cross_end = lax.ppermute(far[:s2] + in_end, "dp", middle)
+    cross_mid = lax.ppermute(far[s2:] + in_mid, "dp", middle)
+    near_next = (near[:s2] + cross_end.astype(jnp.float32)).astype(jnp.bfloat16)
+    last = lax.ppermute(near_next, "dp", swap(4))
+    down_share = near[s2:] + cross_mid.astype(jnp.float32) + last.astype(jnp.float32)
+    down_share = down_share.reshape(jobs, rank // 2, width_half)
+    low_part = jnp.zeros((span, rows), jnp.float32)
+    for k in range(4):
+        low_part = low_part + jnp.where(deal_row == holders[k], dot(downs[k], tokens, CONTRACT_LAST), 0)
+    low_part = jnp.where(job_mask, low_part, 0)
+    low_rank = (low_part + lax.ppermute(low_part, "tp", swap(2))).astype(jnp.bfloat16)
+    wide_low = jnp.concatenate([jnp.where(deal_row == s, low_rank, zero) for s in range(4)])
+    up_part = (ADAPTER_SCALE * dot(wide_low, grad_mine)).astype(jnp.bfloat16)
+    up_part = up_part.reshape(4, jobs, 2, rank // 2, features).transpose(0, 2, 1, 3, 4)
+    up_part = up_part.reshape(8, jobs * rank // 2, features)
+    up_got = lax.all_to_all(up_part, ("dp", "fsdp"), split_axis=0, concat_axis=0, tiled=True)
+    up_share = jnp.sum(up_got.astype(jnp.float32), axis=0).reshape(jobs, rank // 2, features)
+    adapter_output = sum(
+        dot(jnp.where(deal_row == (dp_index ^ k), low_rank, zero), ups[k][0], CONTRACT_FIRST) for k in range(4)
+    )
+    direct = jnp.concatenate([got_first, got_second])
+    relayed = jnp.concatenate([relay_first, relay_second])
+    low_half = jnp.where(rep_index == 0, direct, relayed)
+    high_half = jnp.where(rep_index == 0, relayed, direct)
+    other_weight = jnp.concatenate([low_half, high_half])
+    own_out = dot(tokens, frozen_value_weight)
+    other_out = dot(tokens, other_weight)
+    same = fsdp_index == tp_index
+    base_keep = jnp.where(same, own_out, other_out)
+    base_send = jnp.where(same, other_out, own_out)
+    base_out = base_keep + lax.ppermute(base_send, "tp", swap(2))
+    value_output = (base_out + ADAPTER_SCALE * adapter_output).astype(jnp.bfloat16)
+    grad_own = jnp.where(same, grad_mine, grad_other)
+    grad_far = jnp.where(same, grad_other, grad_mine)
+    lora = sum(dot(wide_of(grad_rank, k), downs[k], CONTRACT_FIRST) for k in range(4))
+    input_gradient = dot(grad_own, frozen_value_weight, CONTRACT_LAST)
+    input_gradient = input_gradient + dot(grad_far, other_weight, CONTRACT_LAST) + ADAPTER_SCALE * lora
+    return value_output, input_gradient.astype(jnp.bfloat16), down_share, up_share
+
+
+def dispatch_rows(
     tokens,
     output_gradient,
     frozen_value_weight,
@@ -149,6 +273,8 @@
 
 
 def solution(mesh):
+    small = dict(mesh.shape) == {"rep": 2, "dp": 4, "fsdp": 2, "tp": 2}
+    local = gather_adapters if small else dispatch_rows
     in_specs = (
         P(("rep", "dp", "fsdp"), "tp"),
         P(("rep", "dp", "fsdp"), None),

time: 207 us -> 121 us (0.58)
  waiting for transfers between devices: 111 us -> 51.9 us
  local copies, waits for them, and re-layouts: 23.3 us -> 5.28 us
  between operations: 13.9 us -> 1.16 us
  starting transfers between devices: 24.2 us -> 32.5 us
  other arithmetic: 10.2 us -> 2.45 us
  matrix products: 19.9 us -> 26.8 us
  blocking collectives: 3.51 us -> 0 us
    all_to_all x5 -> x1, waiting for transfers between devices: 106 us -> 6.25 us  [gather_adapters(): lax.all_to_all(up_part, ('dp', 'fsdp'), split_axis=0, concat_axis=0, tile...]
    ppermute x0 -> x22, waiting for transfers between devices: none -> 45.7 us  [the longest x1 17.9 us: gather_adapters(): got_second = lax.ppermute(second, 'fsdp', swap(2))]
    ppermute x0 -> x22, starting transfers between devices: none -> 29.2 us  [the longest x1 5.88 us: gather_adapters(): down_next = lax.ppermute(down, 'dp', swap(4))]
    all_to_all x5 -> x1, starting transfers between devices: 23.9 us -> 3.37 us  [gather_adapters(): lax.all_to_all(up_part, ('dp', 'fsdp'), split_axis=0, concat_axis=0, tile...]
    gather x5 -> x0, local copies, waits for them, and re-layouts: 18 us -> none  [the longest x1 7.32 us: local(): row_grad = back_grad.reshape(slot_total, width_half)[row_slot]]
    dot_general x8 -> x29, matrix products: 19.9 us -> 26.8 us  [dot(): lax.dot_general(left, right, dims, preferred_element_type=jnp.float32)]
    select_n x5, other arithmetic: 5 us -> 0.19 us  [the longest x1 0.14 us: gather_adapters(): low_half = jnp.where(rep_index == 0, direct, relayed)]
    reduce_scatter x3 -> x0, waiting for transfers between devices: 3.77 us -> none  [the longest x1 3.76 us: local(): lax.psum_scatter(frozen_output, 'tp', scatter_dimension=1, tiled=True)]
  transfers between devices with their start and end apart: 9 -> 23, of which waited for: 5 -> 10; matrix products, arithmetic and copies ran while one was open for 21% -> 27% of each run, Pallas kernels for 0% -> 0%
where the time goes in v1:
time: 121 us; the launch traced here: 120 us
  waiting for transfers between devices  51.9 us (43%)
  starting transfers between devices  32.5 us (27%)
  matrix products  26.8 us (22%)
  local copies, waits for them, and re-layouts  5.28 us (4%)
  other arithmetic  2.45 us (2%)
    dot_general x29, matrix products, dot(): lax.dot_general(left, right, dims, preferred_element_type=jnp.float32)  26.8 us
    ppermute x1, waiting for transfers between devices, gather_adapters(): got_second = lax.ppermute(second, 'fsdp', swap(2))  17.9 us
    ppermute x3, waiting for transfers between devices, gather_adapters(): lax.ppermute(up_pair, 'dp', swap(4, k))  9.2 us
    ppermute x1, waiting for transfers between devices, gather_adapters(): last = lax.ppermute(near_next, 'dp', swap(4))  7.68 us
    all_to_all x1, waiting for transfers between devices, gather_adapters(): lax.all_to_all(up_part, ('dp', 'fsdp'), split_axis=0, concat_axis=0, tile...  6.25 us
    ppermute x1, starting transfers between devices, gather_adapters(): down_next = lax.ppermute(down, 'dp', swap(4))  5.88 us
    ppermute x1, starting transfers between devices, gather_adapters(): last = lax.ppermute(near_next, 'dp', swap(4))  5.76 us
    ppermute x1, waiting for transfers between devices, gather_adapters(): in_mid = lax.ppermute(far[s2:], 'dp', inward)  3.82 us
  transfers between devices with their start and end apart: 23, of which 10 were waited for; matrix products, arithmetic and copies ran while one was open for 27% of the time, Pallas kernels for 0%

profile of v1, /device:TPU:0, one launch (start us, length us, event | category | flops | bytes accessed | tf_op | source)
XLA Modules:
  0.0 120.2 jit_solution(4405973012303488225)
XLA Ops:
  0.6 0.8 collective-permute-start.10
  1.5 5.9 %collective-permute-start.9 = (bf16[64,4096]{1,0:T(8,128)(2,1)}, bf16[64,4096]{1,0:T(8,128)(2,1)}, u32[]{:S(2)}, u32[]{:S(2)}) collective-permute-start(bf16[64,4096]{1,0:T(8,128)(2,1)} %bitcast.77), channel_id=1, source_target_pairs={{0,4},{4,0},{8,12},{12,8},{1,5},{5,1},{9,13},{13,9},{2,6},{6,2},{1... | collective-permute-start | bytes 1572872 | tf_op jit(solution)/shard_map/ppermute | solution.py:41
  7.4 2.2 %constant_dynamic-slice_fusion.1 = (bf16[1024,256]{1,0:T(8,128)(2,1)}, bf16[1024,256]{1,0:T(8,128)(2,1)}) fusion(bf16[4096,256]{1,0:T(8,128)(2,1)} %param.9, s32[]{:T(128)S(6)} %add.158, s32[]{:T(128)S(6)} %select_n.165), kind=kLoop, calls=%fused_computation.176 | loop fusion | bytes 2097160 | tf_op jit(solution)/shard_map/slice | solution.py:83
  9.6 1.5 %collective-permute-start = (bf16[1024,256]{1,0:T(8,128)(2,1)}, bf16[1024,256]{1,0:T(8,128)(2,1)}, u32[]{:S(2)}, u32[]{:S(2)}) collective-permute-start(bf16[1024,256]{1,0:T(8,128)(2,1)} %get-tuple-element.21), channel_id=1, source_target_pairs={{0,2},{2,0},{1,3},{3,1},{4,6},{6,4},{5,7},{7,5},{8,10},{10,8},{9,1... | collective-permute-start | bytes 1572872 | tf_op jit(solution)/shard_map/ppermute | solution.py:80
  11.1 3.1 %fusion.128 = f32[256,256]{1,0:T(8,128)} fusion(bf16[256,4096]{1,0:T(8,128)(2,1)S(1)} %copy-done, bf16[4096,256]{1,0:T(8,128)(2,1)} %param.9), kind=kOutput, calls=%fused_computation.198 | convolution fusion | flops 536870912 | bytes 4456448 | tf_op jit(solution)/shard_map/dot_general | solution.py:18
  14.2 0.6 compare_reduce_fusion.3
  14.8 0.8 convolution_select_fusion.3
  15.6 4.3 %fusion.40 = f32[256,4096]{1,0:T(8,128)} fusion(bf16[4096,256]{1,0:T(8,128)(2,1)} %param.9, pred[]{:T(512)S(6)} %eq.196, bf16[256,512]{1,0:T(8,128)(2,1)S(1)} %copy-done.2, s32[]{:T(128)S(6)} %select_n.168, s32[]{:T(128)S(6)} %select_n.167), kind=kOutput, calls=%fused_computation.67 | convolution fusion | flops 536936448 | bytes 6553609 | tf_op jit(solution)/shard_map/dot_general | solution.py:18
  19.9 0.8 fusion.59
  20.7 1.4 %collective-permute-start.4 = (bf16[2,64,256]{2,1,0:T(8,128)(2,1)S(1)}, bf16[2,64,256]{2,1,0:T(8,128)(2,1)S(1)}, u32[]{:S(2)}, u32[]{:S(2)}) collective-permute-start(bf16[2,64,256]{2,1,0:T(8,128)(2,1)S(1)} %pad_maximum_fusion.5), channel_id=1, source_target_pairs={{0,12},{4,8},{8,4},{12,0},{1,13},{5,9},{9,5},{13,1},{2,14},{6,10},... | collective-permute-start | bytes 196616 | tf_op jit(solution)/shard_map/ppermute | solution.py:38
  22.1 0.2 collective-permute-start.3
  22.3 5.2 %collective-permute-done.4 = bf16[2,64,256]{2,1,0:T(8,128)(2,1)S(1)} collective-permute-done((bf16[2,64,256]{2,1,0:T(8,128)(2,1)S(1)}, bf16[2,64,256]{2,1,0:T(8,128)(2,1)S(1)}, u32[]{:S(2)}, u32[]{:S(2)}) %collective-permute-start.4) | collective-permute-done | bytes 65568 | tf_op jit(solution)/shard_map/ppermute | solution.py:38
  27.6 0.2 fusion.46
  27.7 2.0 %collective-permute-done.3 = bf16[2,64,256]{2,1,0:T(8,128)(2,1)S(1)} collective-permute-done((bf16[2,64,256]{2,1,0:T(8,128)(2,1)S(1)}, bf16[2,64,256]{2,1,0:T(8,128)(2,1)S(1)}, u32[]{:S(2)}, u32[]{:S(2)}) %collective-permute-start.3) | collective-permute-done | bytes 65568 | tf_op jit(solution)/shard_map/ppermute | solution.py:38
  29.9 2.0 %collective-permute-done.2 = bf16[2,64,256]{2,1,0:T(8,128)(2,1)S(1)} collective-permute-done((bf16[2,64,256]{2,1,0:T(8,128)(2,1)S(1)}, bf16[2,64,256]{2,1,0:T(8,128)(2,1)S(1)}, u32[]{:S(2)}, u32[]{:S(2)}) %collective-permute-start.2) | collective-permute-done | bytes 65568 | tf_op jit(solution)/shard_map/ppermute | solution.py:38
  32.0 0.9 fusion.11
  32.9 0.8 fusion.12
  33.7 0.2 fusion.13
  33.9 1.1 fusion.24
  35.0 0.5 fusion.4
  35.5 0.6 collective-permute-start.16
  36.1 0.5 fusion.3
  36.6 1.6 %collective-permute-start.15 = (bf16[64,4096]{1,0:T(8,128)(2,1)S(1)}, bf16[64,4096]{1,0:T(8,128)(2,1)S(1)}, u32[]{:S(2)}, u32[]{:S(2)}) collective-permute-start(bf16[64,4096]{1,0:T(8,128)(2,1)S(1)} %fusion.3), channel_id=1, source_target_pairs={{0,2},{2,0},{1,3},{3,1},{4,6},{6,4},{5,7},{7,5},{8,10},{10,8},{9,1... | collective-permute-start | bytes 1572872 | tf_op jit(solution)/shard_map/ppermute | solution.py:82
  38.2 0.7 fusion.76
  38.9 0.3 copy-done.5
  39.2 0.5 collective-permute-start.5
  39.7 1.8 %fusion.23 = f32[64,256]{1,0:T(8,128)S(1)} fusion(f32[64,256]{1,0:T(8,128)S(1)} %convolution_select_fusion.3, bf16[64,4096]{1,0:T(8,128)(2,1)} %collective-permute-done.9, bf16[256,4096]{1,0:T(8,128)(2,1)S(1)} %copy-done, pred[256]{0:T(512)(128)(4,1)S(1)} %get-tuple-element.13), kind=kOutput, calls=%fused_computation.41 | convolution fusion | flops 134250496 | bytes 2752768 | tf_op jit(solution)/shard_map/dot_general | solution.py:18
  41.5 0.7 collective-permute-start.12
  42.2 1.1 constant_dynamic-update-slice_fusion.1
  43.3 1.8 %convolution_add_fusion.2 = f32[256,4096]{1,0:T(8,128)S(1)} fusion(f32[256,4096]{1,0:T(8,128)S(1)} %fusion.76, bf16[64,4096]{1,0:T(8,128)(2,1)} %collective-permute-done.9, bf16[64,256]{1,0:T(8,128)(2,1)S(1)} %fusion.24, pred[256]{0:T(512)(128)(4,1)S(1)} %get-tuple-element.13), kind=kOutput, calls=%fused_computation.3 | convolution fusion | flops 135282688 | bytes 8945920 | tf_op jit(solution)/shard_map/dot_general | solution.py:18
  45.1 1.6 %collective-permute-start.6 = (bf16[1024,256]{1,0:T(8,128)(2,1)}, bf16[1024,256]{1,0:T(8,128)(2,1)S(1)}, u32[]{:S(2)}, u32[]{:S(2)}) collective-permute-start(bf16[1024,256]{1,0:T(8,128)(2,1)} %collective-permute-done), channel_id=1, source_target_pairs={{0,16},{16,0},{1,17},{17,1},{2,18},{18,2},{3,19},{19,3},{4,20},{20... | collective-permute-start | bytes 1572872 | tf_op jit(solution)/shard_map/ppermute | solution.py:85
  46.7 3.7 %collective-permute-done.16 = bf16[64,4096]{1,0:T(8,128)(2,1)S(1)} collective-permute-done((bf16[64,4096]{1,0:T(8,128)(2,1)S(1)}, bf16[64,4096]{1,0:T(8,128)(2,1)S(1)}, u32[]{:S(2)}, u32[]{:S(2)}) %collective-permute-start.16) | collective-permute-done | bytes 524320 | tf_op jit(solution)/shard_map/ppermute | solution.py:81
  50.4 1.3 %collective-permute-start.11 = (bf16[64,4096]{1,0:T(8,128)(2,1)S(1)}, bf16[64,4096]{1,0:T(8,128)(2,1)S(1)}, u32[]{:S(2)}, u32[]{:S(2)}) collective-permute-start(bf16[64,4096]{1,0:T(8,128)(2,1)S(1)} %collective-permute-done.10), channel_id=1, source_target_pairs={{4,0},{8,12},{5,1},{9,13},{6,2},{10,14},{7,3},{11,15},{20,16},{24,... | collective-permute-start | bytes 1572872 | tf_op jit(solution)/shard_map/ppermute | solution.py:44
  51.7 0.5 add_convert_fusion
  52.3 17.9 %collective-permute-done.5 = bf16[1024,256]{1,0:T(8,128)(2,1)S(1)} collective-permute-done((bf16[1024,256]{1,0:T(8,128)(2,1)S(1)}, bf16[1024,256]{1,0:T(8,128)(2,1)S(1)}, u32[]{:S(2)}, u32[]{:S(2)}) %collective-permute-start.5) | collective-permute-done | bytes 524320 | tf_op jit(solution)/shard_map/ppermute | solution.py:84
  70.1 1.7 %collective-permute-start.17 = (bf16[32,4096]{1,0:T(8,128)(2,1)S(1)}, bf16[32,4096]{1,0:T(8,128)(2,1)S(1)}, u32[]{:S(2)}, u32[]{:S(2)}) collective-permute-start(bf16[32,4096]{1,0:T(8,128)(2,1)S(1)} %get-tuple-element.24), channel_id=1, source_target_pairs={{0,4},{12,8},{1,5},{13,9},{2,6},{14,10},{3,7},{15,11},{16,20},{28,... | collective-permute-start | bytes 786440 | tf_op jit(solution)/shard_map/ppermute | solution.py:92
  71.9 1.3 %collective-permute-start.19 = (bf16[32,4096]{1,0:T(8,128)(2,1)S(1)}, bf16[32,4096]{1,0:T(8,128)(2,1)S(1)}, u32[]{:S(2)}, u32[]{:S(2)}) collective-permute-start(bf16[32,4096]{1,0:T(8,128)(2,1)S(1)} %get-tuple-element.25), channel_id=1, source_target_pairs={{0,4},{12,8},{1,5},{13,9},{2,6},{14,10},{3,7},{15,11},{16,20},{28,... | collective-permute-start | bytes 786440 | tf_op jit(solution)/shard_map/ppermute | solution.py:91
  73.3 0.5 convert_add_fusion
  73.8 3.8 %collective-permute-done.17 = bf16[32,4096]{1,0:T(8,128)(2,1)S(1)} collective-permute-done((bf16[32,4096]{1,0:T(8,128)(2,1)S(1)}, bf16[32,4096]{1,0:T(8,128)(2,1)S(1)}, u32[]{:S(2)}, u32[]{:S(2)}) %collective-permute-start.17) | collective-permute-done | bytes 262176 | tf_op jit(solution)/shard_map/ppermute | solution.py:92
  77.6 1.5 %collective-permute-start.7 = (bf16[1024,256]{1,0:T(8,128)(2,1)S(1)}, bf16[1024,256]{1,0:T(8,128)(2,1)S(1)}, u32[]{:S(2)}, u32[]{:S(2)}) collective-permute-start(bf16[1024,256]{1,0:T(8,128)(2,1)S(1)} %collective-permute-done.5), channel_id=1, source_target_pairs={{0,16},{16,0},{1,17},{17,1},{2,18},{18,2},{3,19},{19,3},{4,20},{20... | collective-permute-start | bytes 1572872 | tf_op jit(solution)/shard_map/ppermute | solution.py:86
  79.1 1.3 %collective-permute-done.19 = bf16[32,4096]{1,0:T(8,128)(2,1)S(1)} collective-permute-done((bf16[32,4096]{1,0:T(8,128)(2,1)S(1)}, bf16[32,4096]{1,0:T(8,128)(2,1)S(1)}, u32[]{:S(2)}, u32[]{:S(2)}) %collective-permute-start.19) | collective-permute-done | bytes 262176 | tf_op jit(solution)/shard_map/ppermute | solution.py:91
  80.4 0.7 collective-permute-start.18
  81.1 0.7 collective-permute-start.20
  81.8 1.3 %collective-permute-start.13 = (bf16[64,4096]{1,0:T(8,128)(2,1)S(1)}, bf16[64,4096]{1,0:T(8,128)(2,1)S(1)}, u32[]{:S(2)}, u32[]{:S(2)}) collective-permute-start(bf16[64,4096]{1,0:T(8,128)(2,1)S(1)} %collective-permute-done.12), channel_id=1, source_target_pairs={{4,0},{8,12},{5,1},{9,13},{6,2},{10,14},{7,3},{11,15},{20,16},{24,... | collective-permute-start | bytes 1572872 | tf_op jit(solution)/shard_map/ppermute | solution.py:45
  83.1 0.8 fusion.22
  84.0 0.7 convolution_add_fusion.1
  84.7 2.0 %collective-permute-done.7 = bf16[1024,256]{1,0:T(8,128)(2,1)S(1)} collective-permute-done((bf16[1024,256]{1,0:T(8,128)(2,1)S(1)}, bf16[1024,256]{1,0:T(8,128)(2,1)S(1)}, u32[]{:S(2)}, u32[]{:S(2)}) %collective-permute-start.7) | collective-permute-done | bytes 524320 | tf_op jit(solution)/shard_map/ppermute | solution.py:86
  87.0 0.8 copy-done.4
  87.8 1.5 %broadcast_select_fusion.2 = (f32[256,256]{1,0:T(8,128)}, f32[256,256]{1,0:T(8,128)S(1)}) fusion(f32[256,256]{1,0:T(8,128)S(1)} %copy-done.4, pred[]{:T(512)S(6)} %eq.196, bf16[256,4096]{1,0:T(8,128)(2,1)S(1)} %copy-done, bf16[2048,256]{1,0:T(8,128)(2,1)S(1)} %get-tuple-element.19, bf16[2048,256]{1,0:T(8,128)(2,1)S(1)} %get-tuple-element.18), kind=kOutput, calls=%fused_computation.71 | convolution fusion | flops 541130752 | bytes 4980737 | tf_op jit(solution)/shard_map/dot_general | solution.py:18
  89.3 5.8 %collective-permute-start.21 = (bf16[32,4096]{1,0:T(8,128)(2,1)S(1)}, bf16[32,4096]{1,0:T(8,128)(2,1)S(1)}, u32[]{:S(2)}, u32[]{:S(2)}) collective-permute-start(bf16[32,4096]{1,0:T(8,128)(2,1)S(1)} %fusion.25), channel_id=1, source_target_pairs={{0,4},{4,0},{8,12},{12,8},{1,5},{5,1},{9,13},{13,9},{2,6},{6,2},{1... | collective-permute-start | bytes 786440 | tf_op jit(solution)/shard_map/ppermute | solution.py:96
  95.0 0.7 convolution_add_fusion.3
  95.8 7.7 %collective-permute-done.21 = bf16[32,4096]{1,0:T(8,128)(2,1)S(1)} collective-permute-done((bf16[32,4096]{1,0:T(8,128)(2,1)S(1)}, bf16[32,4096]{1,0:T(8,128)(2,1)S(1)}, u32[]{:S(2)}, u32[]{:S(2)}) %collective-permute-start.21) | collective-permute-done | bytes 262176 | tf_op jit(solution)/shard_map/ppermute | solution.py:96
  103.5 0.9 fusion.27
  104.4 0.8 fusion.21
  105.3 2.1 %fusion.2 = bf16[256,4096]{1,0:T(8,128)(2,1)} fusion(f32[256,4096]{1,0:T(8,128)S(1)} %convolution_add_fusion.3, f32[256,4096]{1,0:T(8,128)S(1)} %convolution_add_fusion.1, bf16[64,4096]{1,0:T(8,128)(2,1)S(1)} %collective-permute-done.12, bf16[64,4096]{1,0:T(8,128)(2,1)S(1)} %collective-permute-done.13, bf16[64,256]{1,0:T(8,128)(2,1)S(1)} %fusion.24, ...), kind=kOutput, calls=%fused_computation.6 | convolution fusion | flops 138690560 | bytes 11567360 | tf_op jit(solution)/shard_map/dot_general | solution.py:18
  107.4 0.2 fusion.10
  107.6 0.7 copy.13
  108.3 3.4 %all-to-all-start = ((bf16[8,32,256]{2,1,0:T(8,128)(2,1)}), bf16[8,32,256]{2,1,0:T(8,128)(2,1)S(1)}, u32[]{:S(2)}, u32[]{:S(2)}) async-start(bf16[8,32,256]{2,1,0:T(8,128)(2,1)} %bitcast.18), calls=%async_computation | async-start | bytes 262144 | tf_op jit(solution)/shard_map/all_to_all | solution.py:108
  111.7 0.2 fusion.78
  111.9 0.2 fusion.80
  112.2 0.2 fusion.82
  112.4 0.9 add_convert_fusion.1
  113.3 6.3 %all-to-all-done = bf16[8,32,256]{2,1,0:T(8,128)(2,1)S(1)} async-done(((bf16[8,32,256]{2,1,0:T(8,128)(2,1)}), bf16[8,32,256]{2,1,0:T(8,128)(2,1)S(1)}, u32[]{:S(2)}, u32[]{:S(2)}) %all-to-all-start) | async-done | bytes 131104 | tf_op jit(solution)/shard_map/all_to_all | solution.py:108
  119.5 0.6 convert_reduce_fusion
  (71 shorter events, 1.0 us)
Async XLA Ops:
  0.6 10.5 %copy-start = (bf16[256,4096]{1,0:T(8,128)(2,1)S(1)}, bf16[256,4096]{1,0:T(8,128)(2,1)}, u32[]{:S(2)}) copy-start(bf16[256,4096]{1,0:T(8,128)(2,1)} %param.7) | copy-start | bytes 6291460
  0.6 44.5 %collective-permute-start.10 = (bf16[64,4096]{1,0:T(8,128)(2,1)}, bf16[64,4096]{1,0:T(8,128)(2,1)S(1)}, u32[]{:S(2)}, u32[]{:S(2)}) collective-permute-start(bf16[64,4096]{1,0:T(8,128)(2,1)} %bitcast.76), channel_id=1, source_target_pairs={{4,8},{8,4},{5,9},{9,5},{6,10},{10,6},{7,11},{11,7},{20,24},{24,20... | collective-permute-start | bytes 1572872 | tf_op jit(solution)/shard_map/ppermute | solution.py:42
  1.5 37.4 %collective-permute-start.9 = (bf16[64,4096]{1,0:T(8,128)(2,1)}, bf16[64,4096]{1,0:T(8,128)(2,1)}, u32[]{:S(2)}, u32[]{:S(2)}) collective-permute-start(bf16[64,4096]{1,0:T(8,128)(2,1)} %bitcast.77), channel_id=1, source_target_pairs={{0,4},{4,0},{8,12},{12,8},{1,5},{5,1},{9,13},{13,9},{2,6},{6,2},{1... | collective-permute-start | bytes 1572872 | tf_op jit(solution)/shard_map/ppermute | solution.py:41
  7.4 13.3 %collective-permute-start.1 = (bf16[64,256]{1,0:T(8,128)(2,1)}, bf16[64,256]{1,0:T(8,128)(2,1)S(1)}, u32[]{:S(2)}, u32[]{:S(2)}) collective-permute-start(bf16[64,256]{1,0:T(8,128)(2,1)} %bitcast.81), channel_id=1, source_target_pairs={{0,1},{1,0},{2,3},{3,2},{4,5},{5,4},{6,7},{7,6},{8,9},{9,8},{10,11... | collective-permute-start | bytes 98312 | tf_op jit(solution)/shard_map/ppermute | solution.py:37
  9.6 31.9 %collective-permute-start = (bf16[1024,256]{1,0:T(8,128)(2,1)}, bf16[1024,256]{1,0:T(8,128)(2,1)}, u32[]{:S(2)}, u32[]{:S(2)}) collective-permute-start(bf16[1024,256]{1,0:T(8,128)(2,1)} %get-tuple-element.21), channel_id=1, source_target_pairs={{0,2},{2,0},{1,3},{3,1},{4,6},{6,4},{5,7},{7,5},{8,10},{10,8},{9,1... | collective-permute-start | bytes 1572872 | tf_op jit(solution)/shard_map/ppermute | solution.py:80
  11.1 3.1 %copy-start.20 = (s32[256,1]{0,1:T(1,128)S(1)}, s32[256,1]{0,1:T(1,128)}, u32[]{:S(2)}) copy-start(s32[256,1]{0,1:T(1,128)} %param.12) | copy-start | bytes 3076
  11.1 3.7 %copy-start.3 = (bf16[4,16,4096]{2,1,0:T(8,128)(2,1)S(1)}, bf16[4,16,4096]{2,1,0:T(8,128)(2,1)}, u32[]{:S(2)}) copy-start(bf16[4,16,4096]{2,1,0:T(8,128)(2,1)} %param.10) | copy-start | bytes 1572868
  14.2 1.4 %copy-start.2 = (bf16[256,512]{1,0:T(8,128)(2,1)S(1)}, bf16[256,512]{1,0:T(8,128)(2,1)}, u32[]{:S(2)}) copy-start(bf16[256,512]{1,0:T(8,128)(2,1)} %param.8) | copy-start | bytes 786436
  15.6 4.3 %copy-start.6 = (bf16[4,16,256]{2,1,0:T(8,128)(2,1)S(1)}, bf16[4,16,256]{2,1,0:T(8,128)(2,1)}, u32[]{:S(2)}) copy-start(bf16[4,16,256]{2,1,0:T(8,128)(2,1)} %param.11) | copy-start | bytes 98308
  20.7 6.9 %collective-permute-start.4 = (bf16[2,64,256]{2,1,0:T(8,128)(2,1)S(1)}, bf16[2,64,256]{2,1,0:T(8,128)(2,1)S(1)}, u32[]{:S(2)}, u32[]{:S(2)}) collective-permute-start(bf16[2,64,256]{2,1,0:T(8,128)(2,1)S(1)} %pad_maximum_fusion.5), channel_id=1, source_target_pairs={{0,12},{4,8},{8,4},{12,0},{1,13},{5,9},{9,5},{13,1},{2,14},{6,10},... | collective-permute-start | bytes 196616 | tf_op jit(solution)/shard_map/ppermute | solution.py:38
  22.1 7.6 %collective-permute-start.3 = (bf16[2,64,256]{2,1,0:T(8,128)(2,1)S(1)}, bf16[2,64,256]{2,1,0:T(8,128)(2,1)S(1)}, u32[]{:S(2)}, u32[]{:S(2)}) collective-permute-start(bf16[2,64,256]{2,1,0:T(8,128)(2,1)S(1)} %pad_maximum_fusion.5), channel_id=1, source_target_pairs={{0,8},{4,12},{8,0},{12,4},{1,9},{5,13},{9,1},{13,5},{2,10},{6,14},... | collective-permute-start | bytes 196616 | tf_op jit(solution)/shard_map/ppermute | solution.py:38
  27.6 7.4 %copy-start.7 = (bf16[2,64,256]{2,1,0:T(8,128)(2,1)}, bf16[2,64,256]{2,1,0:T(8,128)(2,1)S(1)}, u32[]{:S(2)}) copy-start(bf16[2,64,256]{2,1,0:T(8,128)(2,1)S(1)} %collective-permute-done.4) | copy-start | bytes 196612
  27.6 4.3 %collective-permute-start.2 = (bf16[2,64,256]{2,1,0:T(8,128)(2,1)S(1)}, bf16[2,64,256]{2,1,0:T(8,128)(2,1)S(1)}, u32[]{:S(2)}, u32[]{:S(2)}) collective-permute-start(bf16[2,64,256]{2,1,0:T(8,128)(2,1)S(1)} %pad_maximum_fusion.5), channel_id=1, source_target_pairs={{0,4},{4,0},{8,12},{12,8},{1,5},{5,1},{9,13},{13,9},{2,6},{6,2},{1... | collective-permute-start | bytes 196616 | tf_op jit(solution)/shard_map/ppermute | solution.py:38
  29.7 5.3 %copy-start.9 = (bf16[2,64,256]{2,1,0:T(8,128)(2,1)}, bf16[2,64,256]{2,1,0:T(8,128)(2,1)S(1)}, u32[]{:S(2)}) copy-start(bf16[2,64,256]{2,1,0:T(8,128)(2,1)S(1)} %collective-permute-done.3) | copy-start | bytes 196612
  31.9 3.2 %copy-start.11 = (bf16[2,64,256]{2,1,0:T(8,128)(2,1)}, bf16[2,64,256]{2,1,0:T(8,128)(2,1)S(1)}, u32[]{:S(2)}) copy-start(bf16[2,64,256]{2,1,0:T(8,128)(2,1)S(1)} %collective-permute-done.2) | copy-start | bytes 196612
  35.5 14.9 %collective-permute-start.16 = (bf16[64,4096]{1,0:T(8,128)(2,1)S(1)}, bf16[64,4096]{1,0:T(8,128)(2,1)S(1)}, u32[]{:S(2)}, u32[]{:S(2)}) collective-permute-start(bf16[64,4096]{1,0:T(8,128)(2,1)S(1)} %fusion.4), channel_id=1, source_target_pairs={{0,2},{2,0},{1,3},{3,1},{4,6},{6,4},{5,7},{7,5},{8,10},{10,8},{9,1... | collective-permute-start | bytes 1572872 | tf_op jit(solution)/shard_map/ppermute | solution.py:81
  36.6 35.3 %collective-permute-start.15 = (bf16[64,4096]{1,0:T(8,128)(2,1)S(1)}, bf16[64,4096]{1,0:T(8,128)(2,1)S(1)}, u32[]{:S(2)}, u32[]{:S(2)}) collective-permute-start(bf16[64,4096]{1,0:T(8,128)(2,1)S(1)} %fusion.3), channel_id=1, source_target_pairs={{0,2},{2,0},{1,3},{3,1},{4,6},{6,4},{5,7},{7,5},{8,10},{10,8},{9,1... | collective-permute-start | bytes 1572872 | tf_op jit(solution)/shard_map/ppermute | solution.py:82
  38.1 1.0 copy-start.5
  39.2 30.9 %collective-permute-start.5 = (bf16[1024,256]{1,0:T(8,128)(2,1)S(1)}, bf16[1024,256]{1,0:T(8,128)(2,1)S(1)}, u32[]{:S(2)}, u32[]{:S(2)}) collective-permute-start(bf16[1024,256]{1,0:T(8,128)(2,1)S(1)} %copy-done.5), channel_id=1, source_target_pairs={{0,2},{2,0},{1,3},{3,1},{4,6},{6,4},{5,7},{7,5},{8,10},{10,8},{9,1... | collective-permute-start | bytes 1572872 | tf_op jit(solution)/shard_map/ppermute | solution.py:84
  41.5 40.3 %collective-permute-start.12 = (bf16[64,4096]{1,0:T(8,128)(2,1)}, bf16[64,4096]{1,0:T(8,128)(2,1)S(1)}, u32[]{:S(2)}, u32[]{:S(2)}) collective-permute-start(bf16[64,4096]{1,0:T(8,128)(2,1)} %collective-permute-done.9), channel_id=1, source_target_pairs={{4,8},{8,4},{5,9},{9,5},{6,10},{10,6},{7,11},{11,7},{20,24},{24,20... | collective-permute-start | bytes 1572872 | tf_op jit(solution)/shard_map/ppermute | solution.py:43
  45.1 38.8 %collective-permute-start.6 = (bf16[1024,256]{1,0:T(8,128)(2,1)}, bf16[1024,256]{1,0:T(8,128)(2,1)S(1)}, u32[]{:S(2)}, u32[]{:S(2)}) collective-permute-start(bf16[1024,256]{1,0:T(8,128)(2,1)} %collective-permute-done), channel_id=1, source_target_pairs={{0,16},{16,0},{1,17},{17,1},{2,18},{18,2},{3,19},{19,3},{4,20},{20... | collective-permute-start | bytes 1572872 | tf_op jit(solution)/shard_map/ppermute | solution.py:85
  50.4 30.7 %collective-permute-start.11 = (bf16[64,4096]{1,0:T(8,128)(2,1)S(1)}, bf16[64,4096]{1,0:T(8,128)(2,1)S(1)}, u32[]{:S(2)}, u32[]{:S(2)}) collective-permute-start(bf16[64,4096]{1,0:T(8,128)(2,1)S(1)} %collective-permute-done.10), channel_id=1, source_target_pairs={{4,0},{8,12},{5,1},{9,13},{6,2},{10,14},{7,3},{11,15},{20,16},{24,... | collective-permute-start | bytes 1572872 | tf_op jit(solution)/shard_map/ppermute | solution.py:44
  70.1 7.4 %collective-permute-start.17 = (bf16[32,4096]{1,0:T(8,128)(2,1)S(1)}, bf16[32,4096]{1,0:T(8,128)(2,1)S(1)}, u32[]{:S(2)}, u32[]{:S(2)}) collective-permute-start(bf16[32,4096]{1,0:T(8,128)(2,1)S(1)} %get-tuple-element.24), channel_id=1, source_target_pairs={{0,4},{12,8},{1,5},{13,9},{2,6},{14,10},{3,7},{15,11},{16,20},{28,... | collective-permute-start | bytes 786440 | tf_op jit(solution)/shard_map/ppermute | solution.py:92
  71.9 8.4 %collective-permute-start.19 = (bf16[32,4096]{1,0:T(8,128)(2,1)S(1)}, bf16[32,4096]{1,0:T(8,128)(2,1)S(1)}, u32[]{:S(2)}, u32[]{:S(2)}) collective-permute-start(bf16[32,4096]{1,0:T(8,128)(2,1)S(1)} %get-tuple-element.25), channel_id=1, source_target_pairs={{0,4},{12,8},{1,5},{13,9},{2,6},{14,10},{3,7},{15,11},{16,20},{28,... | collective-permute-start | bytes 786440 | tf_op jit(solution)/shard_map/ppermute | solution.py:91
  77.6 9.2 %collective-permute-start.7 = (bf16[1024,256]{1,0:T(8,128)(2,1)S(1)}, bf16[1024,256]{1,0:T(8,128)(2,1)S(1)}, u32[]{:S(2)}, u32[]{:S(2)}) collective-permute-start(bf16[1024,256]{1,0:T(8,128)(2,1)S(1)} %collective-permute-done.5), channel_id=1, source_target_pairs={{0,16},{16,0},{1,17},{17,1},{2,18},{18,2},{3,19},{19,3},{4,20},{20... | collective-permute-start | bytes 1572872 | tf_op jit(solution)/shard_map/ppermute | solution.py:86
  80.4 15.4 %collective-permute-start.18 = (bf16[32,4096]{1,0:T(8,128)(2,1)S(1)}, bf16[32,4096]{1,0:T(8,128)(2,1)S(1)}, u32[]{:S(2)}, u32[]{:S(2)}) collective-permute-start(bf16[32,4096]{1,0:T(8,128)(2,1)S(1)} %get-tuple-element.22), channel_id=1, source_target_pairs={{4,8},{8,4},{5,9},{9,5},{6,10},{10,6},{7,11},{11,7},{20,24},{24,20... | collective-permute-start | bytes 786440 | tf_op jit(solution)/shard_map/ppermute | solution.py:94
  81.1 8.1 %collective-permute-start.20 = (bf16[32,4096]{1,0:T(8,128)(2,1)S(1)}, bf16[32,4096]{1,0:T(8,128)(2,1)S(1)}, u32[]{:S(2)}, u32[]{:S(2)}) collective-permute-start(bf16[32,4096]{1,0:T(8,128)(2,1)S(1)} %get-tuple-element.23), channel_id=1, source_target_pairs={{4,8},{8,4},{5,9},{9,5},{6,10},{10,6},{7,11},{11,7},{20,24},{24,20... | collective-permute-start | bytes 786440 | tf_op jit(solution)/shard_map/ppermute | solution.py:93
  81.8 22.5 %collective-permute-start.13 = (bf16[64,4096]{1,0:T(8,128)(2,1)S(1)}, bf16[64,4096]{1,0:T(8,128)(2,1)S(1)}, u32[]{:S(2)}, u32[]{:S(2)}) collective-permute-start(bf16[64,4096]{1,0:T(8,128)(2,1)S(1)} %collective-permute-done.12), channel_id=1, source_target_pairs={{4,0},{8,12},{5,1},{9,13},{6,2},{10,14},{7,3},{11,15},{20,16},{24,... | collective-permute-start | bytes 1572872 | tf_op jit(solution)/shard_map/ppermute | solution.py:45
  86.8 1.0 copy-start.4
  87.8 7.3 %copy-start.1 = (f32[256,4096]{1,0:T(8,128)S(1)}, f32[256,4096]{1,0:T(8,128)}, u32[]{:S(2)}) copy-start(f32[256,4096]{1,0:T(8,128)} %fusion.40) | copy-start | bytes 12582916
  89.2 23.2 %collective-permute-start.8 = (f32[256,256]{1,0:T(8,128)}, f32[256,256]{1,0:T(8,128)S(1)}, u32[]{:S(2)}, u32[]{:S(2)}) collective-permute-start(f32[256,256]{1,0:T(8,128)} %get-tuple-element.43), channel_id=1, source_target_pairs={{0,1},{1,0},{2,3},{3,2},{4,5},{5,4},{6,7},{7,6},{8,9},{9,8},{10,11... | collective-permute-start | bytes 786440 | tf_op jit(solution)/shard_map/ppermute | solution.py:123
  89.3 15.1 %copy-start.15 = (s32[256]{0:T(256)S(1)}, s32[256]{0:T(256)}, u32[]{:S(2)}) copy-start(s32[256]{0:T(256)} %param.13) | copy-start | bytes 3076
  89.3 14.2 %collective-permute-start.21 = (bf16[32,4096]{1,0:T(8,128)(2,1)S(1)}, bf16[32,4096]{1,0:T(8,128)(2,1)S(1)}, u32[]{:S(2)}, u32[]{:S(2)}) collective-permute-start(bf16[32,4096]{1,0:T(8,128)(2,1)S(1)} %fusion.25), channel_id=1, source_target_pairs={{0,4},{4,0},{8,12},{12,8},{1,5},{5,1},{9,13},{13,9},{2,6},{6,2},{1... | collective-permute-start | bytes 786440 | tf_op jit(solution)/shard_map/ppermute | solution.py:96
  105.1 2.2 %copy-start.19 = (pred[256]{0:T(512)(128)(4,1)S(1)}, pred[256]{0:T(512)(128)(4,1)}, u32[]{:S(2)}) copy-start(pred[256]{0:T(512)(128)(4,1)} %get-tuple-element.6) | copy-start | bytes 772
  105.1 2.2 %copy-start.16 = (pred[256]{0:T(512)(128)(4,1)S(1)}, pred[256]{0:T(512)(128)(4,1)}, u32[]{:S(2)}) copy-start(pred[256]{0:T(512)(128)(4,1)} %get-tuple-element.7) | copy-start | bytes 772
  105.2 2.2 %copy-start.17 = (pred[256]{0:T(512)(128)(4,1)S(1)}, pred[256]{0:T(512)(128)(4,1)}, u32[]{:S(2)}) copy-start(pred[256]{0:T(512)(128)(4,1)} %get-tuple-element.14) | copy-start | bytes 772
  105.2 2.2 %copy-start.18 = (pred[256]{0:T(512)(128)(4,1)S(1)}, pred[256]{0:T(512)(128)(4,1)}, u32[]{:S(2)}) copy-start(pred[256]{0:T(512)(128)(4,1)} %get-tuple-element.15) | copy-start | bytes 772
  105.2 6.5 %copy-start.8 = (bf16[2,64,256]{2,1,0:T(8,128)(2,1)S(1)}, bf16[2,64,256]{2,1,0:T(8,128)(2,1)}, u32[]{:S(2)}) copy-start(bf16[2,64,256]{2,1,0:T(8,128)(2,1)} %copy-done.7) | copy-start | bytes 196612
  105.2 6.5 %copy-start.14 = (pred[256]{0:T(512)(128)(4,1)S(1)}, pred[256]{0:T(512)(128)(4,1)}, u32[]{:S(2)}) copy-start(pred[256]{0:T(512)(128)(4,1)} %get-tuple-element.10) | copy-start | bytes 772
  105.2 6.7 %copy-start.10 = (bf16[2,64,256]{2,1,0:T(8,128)(2,1)S(1)}, bf16[2,64,256]{2,1,0:T(8,128)(2,1)}, u32[]{:S(2)}) copy-start(bf16[2,64,256]{2,1,0:T(8,128)(2,1)} %copy-done.9) | copy-start | bytes 196612
  105.2 6.7 %copy-start.13 = (pred[256]{0:T(512)(128)(4,1)S(1)}, pred[256]{0:T(512)(128)(4,1)}, u32[]{:S(2)}) copy-start(pred[256]{0:T(512)(128)(4,1)} %get-tuple-element.11) | copy-start | bytes 772
  105.2 2.2 %collective-permute-start.14 = (f32[64,256]{1,0:T(8,128)S(1)}, f32[64,256]{1,0:T(8,128)S(1)}, u32[]{:S(2)}, u32[]{:S(2)}) collective-permute-start(f32[64,256]{1,0:T(8,128)S(1)} %fusion.21), channel_id=1, source_target_pairs={{0,1},{1,0},{2,3},{3,2},{4,5},{5,4},{6,7},{7,6},{8,9},{9,8},{10,11... | collective-permute-start | bytes 196616 | tf_op jit(solution)/shard_map/ppermute | solution.py:103
  107.4 4.8 %copy-start.12 = (bf16[2,64,256]{2,1,0:T(8,128)(2,1)S(1)}, bf16[2,64,256]{2,1,0:T(8,128)(2,1)}, u32[]{:S(2)}) copy-start(bf16[2,64,256]{2,1,0:T(8,128)(2,1)} %copy-done.11) | copy-start | bytes 196612
  108.3 11.2 %all-to-all-start = ((bf16[8,32,256]{2,1,0:T(8,128)(2,1)}), bf16[8,32,256]{2,1,0:T(8,128)(2,1)S(1)}, u32[]{:S(2)}, u32[]{:S(2)}) async-start(bf16[8,32,256]{2,1,0:T(8,128)(2,1)} %bitcast.18), calls=%async_computation | async-start | bytes 262144 | tf_op jit(solution)/shard_map/all_to_all | solution.py:108

commit v2 on v0

--- a/solution.py
+++ b/solution.py
@@ -1,12 +1,433 @@
+import functools
+
 import jax
 import jax.numpy as jnp
 from jax import lax
+from jax.experimental import pallas as pl
+from jax.experimental.pallas import tpu as pltpu
 from jax.sharding import PartitionSpec as P
 
 ADAPTER_SCALE = 2.0
 
-
-def local(
+BF16 = jnp.bfloat16
+F32 = jnp.float32
+PLAIN = (((1,), (0,)), ((), ()))
+CONTRACT_LAST = (((1,), (1,)), ((), ()))
+VMEM_BYTES = 16 * 1024 * 1024
+COLUMNS = 1024
+PART_US = 2
+SEND_US = 6
+FAR_US = 6
+SUM_US = 6
+NEAR_US = 6
+UP_US = 4
+LAST_US = 8
+FIRST_SHARE = 4
+WHOLE = pl.BlockSpec(memory_space=pltpu.VMEM)
+ANY = pl.BlockSpec(memory_space=pl.ANY)
+HBM = pl.BlockSpec(memory_space=pltpu.HBM)
+
+
+def swap(extent, flip=1):
+    return [(i, i ^ flip) for i in range(extent)]
+
+
+def dot(left, right, dims=PLAIN):
+    return lax.dot_general(left, right, dims, preferred_element_type=F32)
+
+
+def struct(shape, dtype):
+    return jax.ShapeDtypeStruct(shape, dtype)
+
+
+def holders():
+    here = lax.axis_index("dp")
+    return here, here ^ 1, jnp.where(here < 2, 2, 1), jnp.where(here < 2, 3, 0)
+
+
+def job_mask(span, rank, job_row):
+    return lax.broadcasted_iota(jnp.int32, (span, job_row.shape[1]), 0) // rank == job_row
+
+
+def prepare_kernel(gradient, deal, job, up, part_out, deal_out, job_out, up_out):
+    features = up.shape[1]
+    start = pl.multiple_of(lax.axis_index("tp") * features, features)
+    part_out[...] = gradient[:, pl.ds(start, features)]
+    deal_out[...] = deal[...]
+    job_out[...] = job[...]
+    up_out[...] = up[...]
+
+
+def grad_partial_kernel(rank, near, far, gradient, deal, job, out):
+    here = lax.axis_index("dp")
+    span = out.shape[0]
+    part = gradient[...]
+    owner = deal[...]
+    total = jnp.zeros(out.shape, F32)
+    for k in range(4):
+        block = (near, far)[k // 2][k % 2 * span : (k % 2 + 1) * span]
+        total += jnp.where(owner == (here ^ k), dot(block, part, CONTRACT_LAST), 0.0)
+    out[...] = jnp.where(job_mask(span, rank, job[...]), total, 0.0)
+
+
+def each_column(ref):
+    def run(body):
+        def step(i, carry):
+            body(pl.ds(pl.multiple_of(i * COLUMNS, COLUMNS), COLUMNS))
+            return carry
+
+        lax.fori_loop(0, ref.shape[1] // COLUMNS, step, 0)
+
+    return run
+
+
+def half_rows(narrow, rank, which):
+    half = rank // 2
+    pick = [narrow[j * half : (j + 1) * half] for j in range(narrow.shape[0] // half)]
+    low, high = jnp.concatenate(pick[0::2]), jnp.concatenate(pick[1::2])
+    return jnp.where(which == 0, low, high)
+
+
+def wide_rows(narrow, owner, names):
+    return jnp.concatenate([jnp.where(owner == name, narrow, 0.0) for name in names]).astype(BF16)
+
+
+def grad_send_kernel(rank, first, second, deal, tokens, rank_out, far_out, near_out):
+    total = first[...] + second[...]
+    rank_out[...] = total.astype(BF16)
+    total = total.astype(BF16).astype(F32)
+    sent = ADAPTER_SCALE * half_rows(total, rank, 1 - lax.axis_index("fsdp"))
+    mine, beside, middle, end = holders()
+    wide = wide_rows(sent, deal[...], (end, middle, beside, mine))
+    split = far_out.shape[0]
+
+    @each_column(tokens)
+    def _(at):
+        made = dot(wide, tokens[:, at])
+        far_out[:, at] = made[:split].astype(BF16)
+        near_out[:, at] = made[split:].astype(BF16)
+
+
+def kept_rows(rank, grad_rank):
+    return ADAPTER_SCALE * half_rows(grad_rank[...].astype(F32), rank, lax.axis_index("fsdp"))
+
+
+def in_middle():
+    here = lax.axis_index("dp")
+    return (here == 1) | (here == 2)
+
+
+def far_kernel(rank, got, grad_rank, deal, tokens, down_cross, out, swap_out):
+    _, _, middle, end = holders()
+    wide = wide_rows(kept_rows(rank, grad_rank), deal[...], (end, middle))
+
+    @each_column(tokens)
+    def _(at):
+        made = (dot(wide, tokens[:, at]) + got[:, at].astype(F32)).astype(BF16)
+        out[:, at] = made
+        swap_out[:, at] = jnp.where(in_middle(), down_cross[:, at], made)
+
+
+def near_kernel(rank, got, grad_rank, deal, tokens, cross, next_out, mine_out):
+    mine, beside, _, _ = holders()
+    wide = wide_rows(kept_rows(rank, grad_rank), deal[...], (beside, mine))
+    split = next_out.shape[0]
+
+    @each_column(tokens)
+    def _(at):
+        made = dot(wide, tokens[:, at]) + got[:, at].astype(F32) + cross[:, at].astype(F32)
+        next_out[:, at] = made[:split].astype(BF16)
+        mine_out[:, at] = made[split:]
+
+
+def low_kernel(rank, names, blocks, *refs):
+    tokens, deal, job = refs[:3]
+    out = refs[-1]
+    owner = deal[...]
+    name = holders()
+    started = len(refs) - 4 > sum(blocks)
+    out[...] = jnp.zeros(out.shape, F32)
+
+    @each_column(tokens)
+    def _(at):
+        left = list(refs[3:-1])
+        total = out[...]
+        for k, count in zip(names, blocks):
+            block = left.pop(0)[:, at]
+            if count == 2:
+                block = jnp.where(in_middle(), block, left.pop(0)[:, at])
+            total += jnp.where(owner == name[k], dot(block, tokens[:, at], CONTRACT_LAST), 0.0)
+        out[...] = total
+
+    out[...] = jnp.where(job_mask(out.shape[0], rank, job[...]), out[...], 0.0)
+    if started:
+        out[...] += refs[-2][...]
+
+
+def up_kernel(rank, low, low_got, gradient, deal, near, far, keep_out, away_out, lora_out):
+    here = lax.axis_index("dp")
+    span = low.shape[0]
+    half = span // 2
+    narrow = (low[...] + low_got[...]).astype(BF16).astype(F32)
+    owner = deal[...]
+    part = gradient[...]
+    wide = jnp.concatenate([jnp.where(owner == (here ^ k), narrow, 0.0) for k in range(4)])
+    made = ADAPTER_SCALE * dot(wide.astype(BF16), part)
+    side = lax.axis_index("fsdp")
+    for k in range(4):
+        block = made[k * span : (k + 1) * span]
+        keep_out[k * half : (k + 1) * half] = half_rows(block, rank, side)
+        away_out[k * half : (k + 1) * half] = half_rows(block, rank, 1 - side).astype(BF16)
+    ups = jnp.concatenate([near[...], far[...]])
+    lora_out[...] = ADAPTER_SCALE * dot(wide.T.astype(BF16), ups)
+
+
+def up_sum_kernel(keep, got, mine, *sent):
+    total = keep[...] + got[...].astype(F32)
+    half = mine.shape[0]
+    mine[...] = total[:half]
+    for k, out in enumerate(sent):
+        out[...] = total[(k + 1) * half : (k + 2) * half].astype(BF16)
+
+
+def own_kernel(tokens, own, out):
+    out[...] = dot(tokens[...], own[...])
+
+
+def base_kernel(offset, gradient, grad_rank, deal, direct, relayed, tokens, own, *refs):
+    downs, (grad_out, other_out) = refs[:6], refs[-10:-8]
+    wide, buffer, weight_in, own_in, token_in, down_in, sems, out_sems = refs[-8:]
+    features = own.shape[1]
+    count = direct.shape[0]
+    mine = pl.multiple_of(lax.axis_index("fsdp") * features, features)
+    other = pl.multiple_of((1 - lax.axis_index("fsdp")) * features, features)
+    rep = lax.axis_index("rep")
+    spots = []
+    for side in range(2):
+        start = (rep ^ side) * (own.shape[0] // 2) + offset
+        spots.append(pl.ds(pl.multiple_of(start, 256), count))
+    copies = []
+    for side, (at, weight) in enumerate(zip(spots, (direct, relayed))):
+        wanted = [(own.at[at, :], own_in.at[side]), (weight, weight_in.at[side])]
+        wanted += [(down.at[:, at], down_in.at[side, k]) for k, down in enumerate(downs)]
+        wanted += [(tokens.at[:, at], token_in.at[side])]
+        copies.append([pltpu.make_async_copy(*pair, sems.at[side, i]) for i, pair in enumerate(wanted)])
+        for copy in copies[-1]:
+            copy.start()
+    narrow = ADAPTER_SCALE * grad_rank[...].astype(F32)
+    wide[...] = jnp.concatenate([jnp.where(deal[...] == name, narrow, 0.0) for name in holders()]).T.astype(BF16)
+    stores = []
+    for side, at in enumerate(spots):
+        for copy in copies[side][:-1]:
+            copy.wait()
+        total = dot(gradient[:, pl.ds(mine, features)], own_in[side], CONTRACT_LAST)
+        total += dot(gradient[:, pl.ds(other, features)], weight_in[side], CONTRACT_LAST)
+        parts = [down_in[side, k] for k in range(6)]
+        parts[2:] = [jnp.where(in_middle(), parts[k], parts[k + 1]) for k in (2, 4)]
+        total += dot(wide[...], jnp.concatenate(parts))
+        buffer[side] = total.astype(BF16)
+        stores.append(pltpu.make_async_copy(buffer.at[side], grad_out.at[:, at], out_sems.at[side]))
+        stores[-1].start()
+        copies[side][-1].wait()
+        other_part = dot(token_in[side], weight_in[side])
+        other_out[...] = other_part if side == 0 else other_out[...] + other_part
+    for store in stores:
+        store.wait()
+
+
+def call(kernel, out_shape, *args, after=(), in_specs=None, out_specs=None, us=0, **more):
+    count = len(args)
+    if out_specs is None:
+        out_specs = (WHOLE,) * len(out_shape) if isinstance(out_shape, tuple) else WHOLE
+    if after:
+        inner = kernel
+        kernel = lambda *refs: inner(*refs[:count], *refs[count + len(after) :])
+    return pl.pallas_call(
+        kernel,
+        out_shape=out_shape,
+        in_specs=(in_specs or [WHOLE] * count) + [ANY] * len(after),
+        out_specs=out_specs,
+        compiler_params=pltpu.CompilerParams(vmem_limit_bytes=VMEM_BYTES),
+        cost_estimate=pl.CostEstimate(flops=int(us * 1.15e9), bytes_accessed=0, transcendentals=0) if us else None,
+        **more,
+    )(*args, *after)
+
+
+def cut_kernel(weight, first, second, sems):
+    half = weight.shape[0] // 2
+    start = pl.multiple_of(lax.axis_index("rep") * half, half)
+    count = first.shape[0]
+    copies = [
+        pltpu.make_async_copy(weight.at[pl.ds(start, count)], first, sems.at[0]),
+        pltpu.make_async_copy(weight.at[pl.ds(start + count, half - count)], second, sems.at[1]),
+    ]
+    for copy in copies:
+        copy.start()
+    for copy in copies:
+        copy.wait()
+
+
+def join_kernel(one, two, out):
+    half = one.shape[0]
+    out[:half] = one[...]
+    out[half:] = two[...]
+
+
+def share_kernel(own, first, second, lora, send_out, keep_out):
+    other = first[...] + second[...]
+    same = lax.axis_index("fsdp") == lax.axis_index("tp")
+    send_out[...] = jnp.where(same, other, own[...])
+    keep_out[...] = jnp.where(same, own[...], other) + lora[...]
+
+
+def total_kernel(*refs):
+    total = refs[0][...]
+    for ref in refs[1:-1]:
+        total += ref[...].astype(F32)
+    refs[-1][...] = total.astype(refs[-1].dtype)
+
+
+def add_kernel(one, two, out):
+    out[...] = (one[...].astype(F32) + two[...].astype(F32)).astype(BF16)
+
+
+def ordered(value, before):
+    return lax.optimization_barrier((value, before))[0]
+
+
+def gather_adapters(
+    tokens,
+    output_gradient,
+    frozen_value_weight,
+    adapter_down_weight,
+    adapter_up_weight,
+    deal,
+    row_local_job,
+):
+    rows, width = tokens.shape
+    jobs, rank, features = adapter_up_weight.shape
+    span = jobs * rank
+    half = span // 2
+    down = adapter_down_weight.reshape(span, width)
+    up = adapter_up_weight.reshape(span, features)
+    deal = deal.reshape(1, rows)
+    job = row_local_job.reshape(1, rows)
+    first_rows = width * FIRST_SHARE // 16
+    outward, middle = [(1, 0), (2, 3)], [(1, 2), (2, 1)]
+
+    up_got_first = lax.ppermute(up, "dp", swap(4))
+    row = struct((1, rows), jnp.int32)
+    grad_mine, deal, job, up = call(
+        prepare_kernel, (struct((rows, features), BF16), row, row, struct((span, features), BF16)),
+        output_gradient, deal, job, up,
+    )
+    up_pair = call(join_kernel, struct((2 * span, features), BF16), up, up_got_first, after=(grad_mine,))
+    ups = up_pair, lax.ppermute(up_pair, "dp", swap(4, 2))
+    weight_first, weight_second = call(
+        cut_kernel,
+        (struct((first_rows, features), BF16), struct((width // 2 - first_rows, features), BF16)),
+        frozen_value_weight,
+        in_specs=[ANY],
+        out_specs=(ANY, ANY),
+        scratch_shapes=[pltpu.SemaphoreType.DMA((2,))],
+    )
+    got_first = lax.ppermute(weight_first, "fsdp", swap(2))
+
+    narrow = struct((span, rows), F32)
+    half_wide = struct((half, width), BF16)
+    span_wide = struct((span, width), BF16)
+    grad_part = call(functools.partial(grad_partial_kernel, rank), narrow, *ups, grad_mine, deal, job, us=PART_US)
+    grad_got = lax.ppermute(grad_part, "tp", swap(2))
+    grad_rank, send_far, send_near = call(
+        functools.partial(grad_send_kernel, rank), (struct((span, rows), BF16), span_wide, span_wide),
+        grad_part, grad_got, deal, tokens, after=(got_first,), us=SEND_US,
+    )
+    down_sent = ordered(down, send_far)
+    down_next = lax.ppermute(down_sent, "dp", swap(4))
+    down_cross = lax.ppermute(down_sent, "dp", middle)
+    got_far = lax.ppermute(send_far, "fsdp", swap(2))
+    relay_first = lax.ppermute(ordered(got_first, send_far), "rep", swap(2))
+    own_out = call(
+        own_kernel, struct((rows, features), F32), tokens, frozen_value_weight, after=(send_far,)
+    )
+    far, far_swap = call(
+        functools.partial(far_kernel, rank), (span_wide, span_wide),
+        got_far, grad_rank, deal, tokens, down_cross, after=(own_out, relay_first), us=FAR_US,
+    )
+    got_second = lax.ppermute(ordered(weight_second, got_far), "fsdp", swap(2))
+    swapped = lax.ppermute(far_swap, "dp", swap(4))
+    down_cross2 = lax.ppermute(ordered(down_next, far), "dp", middle)
+    low_near = call(
+        functools.partial(low_kernel, rank, (0, 1), (1, 1)),
+        narrow, tokens, deal, job, down, down_next, after=(far,),
+    )
+    low_first = call(
+        functools.partial(low_kernel, rank, (2,), (2,)),
+        narrow, tokens, deal, job, down_cross, swapped, low_near,
+    )
+    far_sum = call(add_kernel, span_wide, far, swapped, after=(got_second,), us=SUM_US)
+    got_near = lax.ppermute(ordered(send_near, got_second), "fsdp", swap(2))
+    cross = lax.ppermute(far_sum, "dp", middle)
+    down_out2 = lax.ppermute(ordered(down_cross2, far_sum), "dp", outward)
+    relay_second = lax.ppermute(got_second, "rep", swap(2))
+    next_sum, mine_sum = call(
+        functools.partial(near_kernel, rank), (half_wide, struct((half, width), F32)),
+        got_near, grad_rank, deal, tokens, cross, us=NEAR_US,
+    )
+    last = lax.ppermute(next_sum, "dp", swap(4))
+    low_part = call(
+        functools.partial(low_kernel, rank, (3,), (2,)), narrow, tokens, deal, job, down_cross2, down_out2, low_first, after=(next_sum,)
+    )
+    low_got = lax.ppermute(low_part, "tp", swap(2))
+    up_half = struct((4 * half, features), F32), struct((4 * half, features), BF16)
+    up_keep, up_away, lora = call(
+        functools.partial(up_kernel, rank), (*up_half, struct((rows, features), F32)),
+        low_part, low_got, grad_mine, deal, *ups,
+    )
+    def base(offset, direct, relayed, *into):
+        count = direct.shape[0]
+        return call(
+            functools.partial(base_kernel, offset),
+            (struct((rows, width), BF16), struct((rows, features), F32)),
+            output_gradient, grad_rank, deal, direct, relayed, tokens, frozen_value_weight,
+            down, down_next, down_cross, swapped, down_cross2, down_out2,
+            after=into,
+            in_specs=[WHOLE] * 3 + [HBM] * 10,
+            out_specs=(HBM, WHOLE),
+            scratch_shapes=[
+                pltpu.VMEM((rows, 4 * span), BF16),
+                pltpu.VMEM((2, rows, count), BF16),
+                pltpu.VMEM((2, count, features), BF16),
+                pltpu.VMEM((2, count, features), BF16),
+                pltpu.VMEM((2, rows, count), BF16),
+                pltpu.VMEM((2, 6, span, count), BF16),
+                pltpu.SemaphoreType.DMA((2, 9)),
+                pltpu.SemaphoreType.DMA((2,)),
+            ],
+            input_output_aliases={13: 0} if into else {},
+        )
+
+    input_first, other_first = base(0, got_first, relay_first)
+    up_got = lax.ppermute(up_away, "fsdp", swap(2))
+    up_mine, *up_sent = call(
+        up_sum_kernel, (struct((half, features), F32),) + (struct((half, features), BF16),) * 3, up_keep, up_got,
+        us=UP_US,
+    )
+    up_last = [lax.ppermute(sent, "dp", swap(4, k + 1)) for k, sent in enumerate(up_sent)]
+    up_share = call(total_kernel, struct((half, features), F32), up_mine, *up_last)
+
+    input_gradient, other_second = base(first_rows, got_second, relay_second, input_first)
+    base_send, base_keep = call(
+        share_kernel, (struct((rows, features), F32),) * 2, own_out, other_first, other_second, lora
+    )
+    base_got = lax.ppermute(base_send, "tp", swap(2))
+    value_output = call(total_kernel, struct((rows, features), BF16), base_keep, base_got)
+    down_share = call(total_kernel, struct((half, width), F32), mine_sum, last, us=LAST_US)
+    shares = [share.reshape(jobs, rank // 2, share.shape[1]) for share in (down_share, up_share)]
+    return value_output, input_gradient, *shares
+
+
+def dispatch_rows(
     tokens,
     output_gradient,
     frozen_value_weight,
@@ -149,6 +570,8 @@
 
 
 def solution(mesh):
+    small = dict(mesh.shape) == {"rep": 2, "dp": 4, "fsdp": 2, "tp": 2}
+    local = gather_adapters if small else dispatch_rows
     in_specs = (
         P(("rep", "dp", "fsdp"), "tp"),
         P(("rep", "dp", "fsdp"), None),

time: 207 us -> 87.3 us (0.42)
  waiting for transfers between devices: 111 us -> 35.5 us
  local copies, waits for them, and re-layouts: 23.3 us -> 1.62 us
  matrix products: 19.9 us -> 0 us
  Pallas kernels: 0 us -> 17.8 us
  between operations: 13.9 us -> 0.89 us
  other arithmetic: 10.2 us -> 0 us
  starting transfers between devices: 24.2 us -> 31.3 us
  blocking collectives: 3.51 us -> 0 us
    all_to_all x5 -> x0, waiting for transfers between devices: 106 us -> none  [the longest x1 55.4 us: local(): lax.all_to_all(send_tokens.reshape(partner_count, job_slot_count, width_h...]
    ppermute x0 -> x22, waiting for transfers between devices: none -> 35.5 us  [the longest x1 9.74 us: gather_adapters(): down_out2 = lax.ppermute(ordered(down_cross2, far_sum), 'dp', outward)]
    ppermute x0 -> x22, starting transfers between devices: none -> 31.3 us  [the longest x1 4.48 us: gather_adapters(): swapped = lax.ppermute(far_swap, 'dp', swap(4))]
    all_to_all x5 -> x0, starting transfers between devices: 23.9 us -> none  [the longest x1 6.32 us: local(): lax.all_to_all(send_jobs.reshape(partner_count, job_slot_count), 'dp', sp...]
    dot_general x8 -> x0, matrix products: 19.9 us -> none  [the longest x1 5.48 us: local(): lax.dot_general(output_gradient, full_weight, contract_last, preferred_el...]
    gather x5 -> x0, local copies, waits for them, and re-layouts: 18 us -> none  [the longest x1 7.32 us: local(): row_grad = back_grad.reshape(slot_total, width_half)[row_slot]]
    pallas_call x0 -> x20, Pallas kernels: none -> 17.8 us  [call(): pl.pallas_call(kernel, out_shape=out_shape, in_specs=(in_specs or [WHOLE]...]
    select_n x5 -> x0, other arithmetic: 5 us -> none  [the longest x1 3.52 us: local(): jnp.where(is_full[:, None], tokens[source_row], jnp.zeros((), jnp.bfloat16))]
  transfers between devices with their start and end apart: 9 -> 22, of which waited for: 5 -> 13; matrix products, arithmetic and copies ran while one was open for 21% -> 0% of each run, Pallas kernels for 0% -> 17%
where the time goes in v2:
time: 87.3 us; the launch traced here: 87.1 us
  waiting for transfers between devices  35.5 us (41%)
  starting transfers between devices  31.3 us (36%)
  Pallas kernels  17.8 us (20%)
  local copies, waits for them, and re-layouts  1.62 us (2%)
  between operations  0.89 us (1%)
    pallas_call x20, Pallas kernels, call(): pl.pallas_call(kernel, out_shape=out_shape, in_specs=(in_specs or [WHOLE]...  17.8 us
    ppermute x1, waiting for transfers between devices, gather_adapters(): down_out2 = lax.ppermute(ordered(down_cross2, far_sum), 'dp', outward)  9.74 us
    ppermute x1, starting transfers between devices, gather_adapters(): swapped = lax.ppermute(far_swap, 'dp', swap(4))  4.48 us
    ppermute x3, starting transfers between devices, gather_adapters(): lax.ppermute(sent, 'dp', swap(4, k + 1))  4.44 us
    ppermute x1, starting transfers between devices, gather_adapters(): down_next = lax.ppermute(down_sent, 'dp', swap(4))  4.43 us
    ppermute x1, waiting for transfers between devices, gather_adapters(): got_second = lax.ppermute(ordered(weight_second, got_far), 'fsdp', swap(2))  4.25 us
    ppermute x1, waiting for transfers between devices, gather_adapters(): got_far = lax.ppermute(send_far, 'fsdp', swap(2))  4 us
    ppermute x1, waiting for transfers between devices, gather_adapters(): swapped = lax.ppermute(far_swap, 'dp', swap(4))  3.94 us
  transfers between devices with their start and end apart: 22, of which 13 were waited for; matrix products, arithmetic and copies ran while one was open for 0% of the time, Pallas kernels for 17%

profile of v2, /device:TPU:0, one launch (start us, length us, event | category | flops | bytes accessed | tf_op | source)
XLA Modules:
  0.0 87.1 jit_solution(7372321931891392433)
XLA Ops:
  0.6 0.0 copy-start.1
  0.6 1.6 %copy-done.1 = bf16[4096,256]{1,0:T(8,128)(2,1)S(1)} copy-done((bf16[4096,256]{1,0:T(8,128)(2,1)S(1)}, bf16[4096,256]{1,0:T(8,128)(2,1)}, u32[]{:S(2)}) %copy-start.1) | copy-done | bytes 2097176
  2.2 0.1 shard_map.105
  2.4 3.0 %collective-permute-start.3 = (bf16[1024,256]{1,0:T(8,128)(2,1)S(1)}, bf16[1024,256]{1,0:T(8,128)(2,1)S(1)}, u32[]{:S(2)}, u32[]{:S(2)}) collective-permute-start(bf16[1024,256]{1,0:T(8,128)(2,1)S(1)} %get-tuple-element.40), channel_id=1, source_target_pairs={{0,2},{2,0},{1,3},{3,1},{4,6},{6,4},{5,7},{7,5},{8,10},{10,8},{9,1... | collective-permute-start | bytes 1572872 | tf_op jit(solution)/shard_map/ppermute | solution.py:334
  5.4 1.6 %collective-permute-start = (bf16[64,256]{1,0:T(8,128)(2,1)S(1)}, bf16[64,256]{1,0:T(8,128)(2,1)S(1)}, u32[]{:S(2)}, u32[]{:S(2)}) collective-permute-start(bf16[64,256]{1,0:T(8,128)(2,1)S(1)} %bitcast.11), channel_id=1, source_target_pairs={{0,4},{4,0},{8,12},{12,8},{1,5},{5,1},{9,13},{13,9},{2,6},{6,2},{1... | collective-permute-start | bytes 98312 | tf_op jit(solution)/shard_map/ppermute | solution.py:318
  7.0 2.3 %collective-permute-done.refs_1_ = bf16[64,256]{1,0:T(8,128)(2,1)S(1)} collective-permute-done((bf16[64,256]{1,0:T(8,128)(2,1)S(1)}, bf16[64,256]{1,0:T(8,128)(2,1)S(1)}, u32[]{:S(2)}, u32[]{:S(2)}) %collective-permute-start) | collective-permute-done | bytes 32800 | tf_op jit(solution)/shard_map/ppermute | solution.py:318
  9.3 2.6 %collective-permute-start.1 = (bf16[128,256]{1,0:T(8,128)(2,1)S(1)}, bf16[128,256]{1,0:T(8,128)(2,1)S(1)}, u32[]{:S(2)}, u32[]{:S(2)}) collective-permute-start(bf16[128,256]{1,0:T(8,128)(2,1)S(1)} %shard_map.103.near), channel_id=1, source_target_pairs={{0,8},{4,12},{8,0},{12,4},{1,9},{5,13},{9,1},{13,5},{2,10},{6,14},... | collective-permute-start | bytes 196616 | tf_op jit(solution)/shard_map/ppermute | solution.py:325
  11.9 2.6 %collective-permute-done.1.far = bf16[128,256]{1,0:T(8,128)(2,1)S(1)} collective-permute-done((bf16[128,256]{1,0:T(8,128)(2,1)S(1)}, bf16[128,256]{1,0:T(8,128)(2,1)S(1)}, u32[]{:S(2)}, u32[]{:S(2)}) %collective-permute-start.1) | collective-permute-done | bytes 65568 | tf_op jit(solution)/shard_map/ppermute | solution.py:325
  14.4 0.3 shard_map.104.refs_0_
  14.7 0.0 copy-start.3
  14.7 0.0 copy-start.2
  14.8 0.1 collective-permute-start.2
  14.8 1.2 %collective-permute-done.2.refs_1_ = f32[64,256]{1,0:T(8,128)S(1)} collective-permute-done((f32[64,256]{1,0:T(8,128)S(1)}, f32[64,256]{1,0:T(8,128)S(1)}, u32[]{:S(2)}, u32[]{:S(2)}) %collective-permute-start.2) | collective-permute-done | bytes 65568 | tf_op jit(solution)/shard_map/ppermute | solution.py:340
  16.1 1.2 %collective-permute-done.3.refs_4_.direct = bf16[1024,256]{1,0:T(8,128)(2,1)S(1)} collective-permute-done((bf16[1024,256]{1,0:T(8,128)(2,1)S(1)}, bf16[1024,256]{1,0:T(8,128)(2,1)S(1)}, u32[]{:S(2)}, u32[]{:S(2)}) %collective-permute-start.3) | collective-permute-done | bytes 524320 | tf_op jit(solution)/shard_map/ppermute | solution.py:334
  17.3 1.0 %shard_map.106 = (bf16[64,256]{1,0:T(8,128)(2,1)S(1)}, bf16[64,4096]{1,0:T(8,128)(2,1)S(1)}, bf16[64,4096]{1,0:T(8,128)(2,1)S(1)}) custom-call(f32[64,256]{1,0:T(8,128)S(1)} %shard_map.104.refs_0_, f32[64,256]{1,0:T(8,128)S(1)} %collective-permute-done.2.refs_1_, s32[1,256]{1,0:T(1,128)S(1)} %get-tuple-element.38.deal.refs_2_.refs_1_, ...), custom_call_target="tpu_custom_call" | custom-call | flops 6899999744 | tf_op jit(solution)/shard_map/pallas_call | solution.py:245
  18.3 1.8 %collective-permute-start.7 = (bf16[64,4096]{1,0:T(8,128)(2,1)S(1)}, bf16[64,4096]{1,0:T(8,128)(2,1)S(1)}, u32[]{:S(2)}, u32[]{:S(2)}) collective-permute-start(bf16[64,4096]{1,0:T(8,128)(2,1)S(1)} %get-tuple-element.41.refs_2_), channel_id=1, source_target_pairs={{0,2},{2,0},{1,3},{3,1},{4,6},{6,4},{5,7},{7,5},{8,10},{10,8},{9,1... | collective-permute-start | bytes 1572872 | tf_op jit(solution)/shard_map/ppermute | solution.py:348
  20.1 1.5 %collective-permute-start.4 = (bf16[1024,256]{1,0:T(8,128)(2,1)S(1)}, bf16[1024,256]{1,0:T(8,128)(2,1)S(1)}, u32[]{:S(2)}, u32[]{:S(2)}) collective-permute-start(bf16[1024,256]{1,0:T(8,128)(2,1)S(1)} %collective-permute-done.3.refs_4_.direct), channel_id=1, source_target_pairs={{0,16},{16,0},{1,17},{17,1},{2,18},{18,2},{3,19},{19,3},{4,20},{20... | collective-permute-start | bytes 1572872 | tf_op jit(solution)/shard_map/ppermute | solution.py:349
  21.6 0.7 collective-permute-start.6
  22.3 0.7 shard_map.107.refs_5_.own
  23.0 4.4 %collective-permute-start.5 = (bf16[64,4096]{1,0:T(8,128)(2,1)S(1)}, bf16[64,4096]{1,0:T(8,128)(2,1)S(1)}, u32[]{:S(2)}, u32[]{:S(2)}) collective-permute-start(bf16[64,4096]{1,0:T(8,128)(2,1)S(1)} %bitcast.7), channel_id=1, source_target_pairs={{0,4},{4,0},{8,12},{12,8},{1,5},{5,1},{9,13},{13,9},{2,6},{6,2},{1... | collective-permute-start | bytes 1572872 | tf_op jit(solution)/shard_map/ppermute | solution.py:346
  27.4 4.0 %collective-permute-done.7.refs_0_ = bf16[64,4096]{1,0:T(8,128)(2,1)S(1)} collective-permute-done((bf16[64,4096]{1,0:T(8,128)(2,1)S(1)}, bf16[64,4096]{1,0:T(8,128)(2,1)S(1)}, u32[]{:S(2)}, u32[]{:S(2)}) %collective-permute-start.7) | collective-permute-done | bytes 524320 | tf_op jit(solution)/shard_map/ppermute | solution.py:348
  31.4 1.4 %collective-permute-start.10 = (bf16[1024,256]{1,0:T(8,128)(2,1)S(1)}, bf16[1024,256]{1,0:T(8,128)(2,1)S(1)}, u32[]{:S(2)}, u32[]{:S(2)}) collective-permute-start(bf16[1024,256]{1,0:T(8,128)(2,1)S(1)} %get-tuple-element.49), channel_id=1, source_target_pairs={{0,2},{2,0},{1,3},{3,1},{4,6},{6,4},{5,7},{7,5},{8,10},{10,8},{9,1... | collective-permute-start | bytes 1572872 | tf_op jit(solution)/shard_map/ppermute | solution.py:357
  32.9 0.0 collective-permute-done.4.refs_6_.relayed
  32.9 0.0 collective-permute-done.6.refs_4_.refs_2_.refs_9_.refs_3_
  32.9 0.9 shard_map.108
  33.7 4.5 %collective-permute-start.8 = (bf16[64,4096]{1,0:T(8,128)(2,1)S(1)}, bf16[64,4096]{1,0:T(8,128)(2,1)S(1)}, u32[]{:S(2)}, u32[]{:S(2)}) collective-permute-start(bf16[64,4096]{1,0:T(8,128)(2,1)S(1)} %get-tuple-element.45), channel_id=1, source_target_pairs={{0,4},{4,0},{8,12},{12,8},{1,5},{5,1},{9,13},{13,9},{2,6},{6,2},{1... | collective-permute-start | bytes 1572872 | tf_op jit(solution)/shard_map/ppermute | solution.py:358
  38.2 0.5 collective-permute-done.5.refs_1_.refs_8_.refs_4_
  38.7 0.7 collective-permute-start.9
  39.4 4.2 %collective-permute-done.10.refs_2_.refs_3_ = bf16[1024,256]{1,0:T(8,128)(2,1)S(1)} collective-permute-done((bf16[1024,256]{1,0:T(8,128)(2,1)S(1)}, bf16[1024,256]{1,0:T(8,128)(2,1)S(1)}, u32[]{:S(2)}, u32[]{:S(2)}) %collective-permute-start.10) | collective-permute-done | bytes 524320 | tf_op jit(solution)/shard_map/ppermute | solution.py:357
  43.6 1.3 %collective-permute-start.13 = (bf16[64,4096]{1,0:T(8,128)(2,1)S(1)}, bf16[64,4096]{1,0:T(8,128)(2,1)S(1)}, u32[]{:S(2)}, u32[]{:S(2)}) collective-permute-start(bf16[64,4096]{1,0:T(8,128)(2,1)S(1)} %get-tuple-element.55), channel_id=1, source_target_pairs={{0,2},{2,0},{1,3},{3,1},{4,6},{6,4},{5,7},{7,5},{8,10},{10,8},{9,1... | collective-permute-start | bytes 1572872 | tf_op jit(solution)/shard_map/ppermute | solution.py:369
  44.9 3.9 %collective-permute-done.8.refs_1_.refs_3_.refs_10_.refs_4_ = bf16[64,4096]{1,0:T(8,128)(2,1)S(1)} collective-permute-done((bf16[64,4096]{1,0:T(8,128)(2,1)S(1)}, bf16[64,4096]{1,0:T(8,128)(2,1)S(1)}, u32[]{:S(2)}, u32[]{:S(2)}) %collective-permute-start.8) | collective-permute-done | bytes 524320 | tf_op jit(solution)/shard_map/ppermute | solution.py:358
  48.9 0.1 shard_map.109
  49.0 0.7 collective-permute-start.14
  49.7 1.8 %shard_map.112.refs_5_ = f32[64,256]{1,0:T(8,128)S(1)} custom-call(bf16[256,4096]{1,0:T(8,128)(2,1)S(1)} %copy-done, s32[1,256]{1,0:T(1,128)S(1)} %get-tuple-element.38.deal.refs_2_.refs_1_, s32[1,256]{1,0:T(1,128)S(1)} %get-tuple-element.39.job.refs_2_, bf16[64,4096]{1,0:T(8,128)(2,1)S(1)} %bitcast.8, ...), custom_call_target="tpu_custom_call" | custom-call | tf_op jit(solution)/shard_map/pallas_call | solution.py:245
  51.5 0.0 collective-permute-done.9.refs_4_.refs_11_.refs_3_
  51.5 1.3 %collective-permute-start.11 = (bf16[64,4096]{1,0:T(8,128)(2,1)S(1)}, bf16[64,4096]{1,0:T(8,128)(2,1)S(1)}, u32[]{:S(2)}, u32[]{:S(2)}) collective-permute-start(bf16[64,4096]{1,0:T(8,128)(2,1)S(1)} %collective-permute-done.9.refs_4_.refs_11_.refs_3_), channel_id=1, source_target_pairs={{4,0},{8,12},{5,1},{9,13},{6,2},{10,14},{7,3},{11,15},{20,16},{24,... | collective-permute-start | bytes 1572872 | tf_op jit(solution)/shard_map/ppermute | solution.py:371
  52.8 1.2 %shard_map.113.refs_5_ = f32[64,256]{1,0:T(8,128)S(1)} custom-call(bf16[256,4096]{1,0:T(8,128)(2,1)S(1)} %copy-done, s32[1,256]{1,0:T(1,128)S(1)} %get-tuple-element.38.deal.refs_2_.refs_1_, s32[1,256]{1,0:T(1,128)S(1)} %get-tuple-element.39.job.refs_2_, bf16[64,4096]{1,0:T(8,128)(2,1)S(1)} %collective-permute-done.6.refs_4_.refs_2_.refs_9_.refs_3_, ...), custom_call_target="tpu_custom_call" | custom-call | tf_op jit(solution)/shard_map/pallas_call | solution.py:245
  54.0 0.9 %collective-permute-done.13.got = bf16[64,4096]{1,0:T(8,128)(2,1)S(1)} collective-permute-done((bf16[64,4096]{1,0:T(8,128)(2,1)S(1)}, bf16[64,4096]{1,0:T(8,128)(2,1)S(1)}, u32[]{:S(2)}, u32[]{:S(2)}) %collective-permute-start.13) | collective-permute-done | bytes 524320 | tf_op jit(solution)/shard_map/ppermute | solution.py:369
  54.9 0.0 collective-permute-done.14.cross
  54.9 0.9 shard_map.114
  55.7 9.7 %collective-permute-done.11.refs_5_.refs_12_.refs_4_ = bf16[64,4096]{1,0:T(8,128)(2,1)S(1)} collective-permute-done((bf16[64,4096]{1,0:T(8,128)(2,1)S(1)}, bf16[64,4096]{1,0:T(8,128)(2,1)S(1)}, u32[]{:S(2)}, u32[]{:S(2)}) %collective-permute-start.11) | collective-permute-done | bytes 524320 | tf_op jit(solution)/shard_map/ppermute | solution.py:371
  65.5 1.1 %shard_map.115.low = f32[64,256]{1,0:T(8,128)S(1)} custom-call(bf16[256,4096]{1,0:T(8,128)(2,1)S(1)} %copy-done, s32[1,256]{1,0:T(1,128)S(1)} %get-tuple-element.38.deal.refs_2_.refs_1_, s32[1,256]{1,0:T(1,128)S(1)} %get-tuple-element.39.job.refs_2_, bf16[64,4096]{1,0:T(8,128)(2,1)S(1)} %collective-permute-done.9.refs_4_.refs_11_.refs_3_, ...), custom_call_target="tpu_custom_call" | custom-call | tf_op jit(solution)/shard_map/pallas_call | solution.py:245
  66.6 0.1 collective-permute-start.15
  66.7 0.6 collective-permute-start.12
  67.3 0.7 collective-permute-done.15.low_got
  68.0 0.3 shard_map.116
  68.2 0.6 collective-permute-start.18
  68.8 0.0 collective-permute-start.17
  68.8 3.7 %collective-permute-done.18.got = bf16[128,256]{1,0:T(8,128)(2,1)S(1)} collective-permute-done((bf16[128,256]{1,0:T(8,128)(2,1)S(1)}, bf16[128,256]{1,0:T(8,128)(2,1)S(1)}, u32[]{:S(2)}, u32[]{:S(2)}) %collective-permute-start.18) | collective-permute-done | bytes 65568 | tf_op jit(solution)/shard_map/ppermute | solution.py:411
  72.6 0.1 collective-permute-start.19
  72.7 3.2 %collective-permute-start.20 = (bf16[32,256]{1,0:T(8,128)(2,1)S(1)}, bf16[32,256]{1,0:T(8,128)(2,1)S(1)}, u32[]{:S(2)}, u32[]{:S(2)}) collective-permute-start(bf16[32,256]{1,0:T(8,128)(2,1)S(1)} %get-tuple-element.66), channel_id=1, source_target_pairs={{0,8},{4,12},{8,0},{12,4},{1,9},{5,13},{9,1},{13,5},{2,10},{6,14},... | collective-permute-start | bytes 49160 | tf_op jit(solution)/shard_map/ppermute | solution.py:416
  75.8 1.2 %collective-permute-start.21 = (bf16[32,256]{1,0:T(8,128)(2,1)S(1)}, bf16[32,256]{1,0:T(8,128)(2,1)S(1)}, u32[]{:S(2)}, u32[]{:S(2)}) collective-permute-start(bf16[32,256]{1,0:T(8,128)(2,1)S(1)} %get-tuple-element.67), channel_id=1, source_target_pairs={{0,12},{4,8},{8,4},{12,0},{1,13},{5,9},{9,5},{13,1},{2,14},{6,10},... | collective-permute-start | bytes 49160 | tf_op jit(solution)/shard_map/ppermute | solution.py:416
  77.0 3.6 %shard_map.110 = (bf16[256,4096]{1,0:T(8,128)(2,1)}, f32[256,256]{1,0:T(8,128)S(1)}) custom-call(bf16[256,512]{1,0:T(8,128)(2,1)S(1)} %copy-done.4, bf16[64,256]{1,0:T(8,128)(2,1)S(1)} %get-tuple-element.42.refs_1_.grad_rank, s32[1,256]{1,0:T(1,128)S(1)} %get-tuple-element.38.deal.refs_2_.refs_1_, ...), custom_call_target="tpu_custom_call" | custom-call | tf_op jit(solution)/shard_map/pallas_call | solution.py:245
  80.7 0.4 collective-permute-done.12.refs_4_
  81.1 3.6 %shard_map.111 = (bf16[256,4096]{1,0:T(8,128)(2,1)}, f32[256,256]{1,0:T(8,128)S(1)}) custom-call(bf16[256,512]{1,0:T(8,128)(2,1)S(1)} %copy-done.4, bf16[64,256]{1,0:T(8,128)(2,1)S(1)} %get-tuple-element.42.refs_1_.grad_rank, s32[1,256]{1,0:T(1,128)S(1)} %get-tuple-element.38.deal.refs_2_.refs_1_, ...), custom_call_target="tpu_custom_call", output_to_operand_aliasing={{0}: (13, {})} | custom-call | tf_op jit(solution)/shard_map/pallas_call | solution.py:245
  84.7 0.1 shard_map.117
  84.8 0.1 collective-permute-start.16
  84.9 0.0 collective-permute-done.19.refs_1_
  84.9 0.0 collective-permute-done.21.refs_3_
  84.9 0.6 shard_map.121
  85.6 0.0 collective-permute-done.17.refs_1_
  85.6 0.8 shard_map.119
  86.4 0.0 collective-permute-done.16.refs_1_
  86.4 0.7 shard_map.118
  (16 shorter events, 0.1 us)
Async XLA Ops:
  0.6 1.6 %copy-start.1 = (bf16[4096,256]{1,0:T(8,128)(2,1)S(1)}, bf16[4096,256]{1,0:T(8,128)(2,1)}, u32[]{:S(2)}) copy-start(bf16[4096,256]{1,0:T(8,128)(2,1)} %refs_6_.1) | copy-start | bytes 6291460
  2.2 3.1 %copy-start.5 = (bf16[4,16,256]{2,1,0:T(8,128)(2,1)S(1)}, bf16[4,16,256]{2,1,0:T(8,128)(2,1)}, u32[]{:S(2)}) copy-start(bf16[4,16,256]{2,1,0:T(8,128)(2,1)} %param.11) | copy-start | bytes 98308
  2.2 4.7 %copy-start.4 = (bf16[256,512]{1,0:T(8,128)(2,1)S(1)}, bf16[256,512]{1,0:T(8,128)(2,1)}, u32[]{:S(2)}) copy-start(bf16[256,512]{1,0:T(8,128)(2,1)} %refs_0_.6) | copy-start | bytes 786436
  2.2 4.7 %copy-start.6 = (s32[256,1]{0,1:T(1,128)S(1)}, s32[256,1]{0,1:T(1,128)}, u32[]{:S(2)}) copy-start(s32[256,1]{0,1:T(1,128)} %param.12) | copy-start | bytes 3076
  2.2 4.7 %copy-start.7 = (s32[256]{0:T(256)S(1)}, s32[256]{0:T(256)}, u32[]{:S(2)}) copy-start(s32[256]{0:T(256)} %param.13) | copy-start | bytes 3076
  2.4 14.9 %collective-permute-start.3 = (bf16[1024,256]{1,0:T(8,128)(2,1)S(1)}, bf16[1024,256]{1,0:T(8,128)(2,1)S(1)}, u32[]{:S(2)}, u32[]{:S(2)}) collective-permute-start(bf16[1024,256]{1,0:T(8,128)(2,1)S(1)} %get-tuple-element.40), channel_id=1, source_target_pairs={{0,2},{2,0},{1,3},{3,1},{4,6},{6,4},{5,7},{7,5},{8,10},{10,8},{9,1... | collective-permute-start | bytes 1572872 | tf_op jit(solution)/shard_map/ppermute | solution.py:334
  5.4 3.9 %collective-permute-start = (bf16[64,256]{1,0:T(8,128)(2,1)S(1)}, bf16[64,256]{1,0:T(8,128)(2,1)S(1)}, u32[]{:S(2)}, u32[]{:S(2)}) collective-permute-start(bf16[64,256]{1,0:T(8,128)(2,1)S(1)} %bitcast.11), channel_id=1, source_target_pairs={{0,4},{4,0},{8,12},{12,8},{1,5},{5,1},{9,13},{13,9},{2,6},{6,2},{1... | collective-permute-start | bytes 98312 | tf_op jit(solution)/shard_map/ppermute | solution.py:318
  9.3 5.2 %collective-permute-start.1 = (bf16[128,256]{1,0:T(8,128)(2,1)S(1)}, bf16[128,256]{1,0:T(8,128)(2,1)S(1)}, u32[]{:S(2)}, u32[]{:S(2)}) collective-permute-start(bf16[128,256]{1,0:T(8,128)(2,1)S(1)} %shard_map.103.near), channel_id=1, source_target_pairs={{0,8},{4,12},{8,0},{12,4},{1,9},{5,13},{9,1},{13,5},{2,10},{6,14},... | collective-permute-start | bytes 196616 | tf_op jit(solution)/shard_map/ppermute | solution.py:325
  14.4 2.8 %copy-start = (bf16[256,4096]{1,0:T(8,128)(2,1)S(1)}, bf16[256,4096]{1,0:T(8,128)(2,1)}, u32[]{:S(2)}) copy-start(bf16[256,4096]{1,0:T(8,128)(2,1)} %refs_0_.9) | copy-start | bytes 6291460
  14.7 6.9 %copy-start.3 = (bf16[4,16,4096]{2,1,0:T(8,128)(2,1)S(1)}, bf16[4,16,4096]{2,1,0:T(8,128)(2,1)}, u32[]{:S(2)}) copy-start(bf16[4,16,4096]{2,1,0:T(8,128)(2,1)} %param.10) | copy-start | bytes 1572868
  14.7 7.5 %copy-start.2 = (bf16[4096,256]{1,0:T(8,128)(2,1)S(1)}, bf16[4096,256]{1,0:T(8,128)(2,1)}, u32[]{:S(2)}) copy-start(bf16[4096,256]{1,0:T(8,128)(2,1)} %refs_6_.1) | copy-start | bytes 6291460
  14.8 1.3 %collective-permute-start.2 = (f32[64,256]{1,0:T(8,128)S(1)}, f32[64,256]{1,0:T(8,128)S(1)}, u32[]{:S(2)}, u32[]{:S(2)}) collective-permute-start(f32[64,256]{1,0:T(8,128)S(1)} %shard_map.104.refs_0_), channel_id=1, source_target_pairs={{0,1},{1,0},{2,3},{3,2},{4,5},{5,4},{6,7},{7,6},{8,9},{9,8},{10,11... | collective-permute-start | bytes 196616 | tf_op jit(solution)/shard_map/ppermute | solution.py:340
  18.3 13.2 %collective-permute-start.7 = (bf16[64,4096]{1,0:T(8,128)(2,1)S(1)}, bf16[64,4096]{1,0:T(8,128)(2,1)S(1)}, u32[]{:S(2)}, u32[]{:S(2)}) collective-permute-start(bf16[64,4096]{1,0:T(8,128)(2,1)S(1)} %get-tuple-element.41.refs_2_), channel_id=1, source_target_pairs={{0,2},{2,0},{1,3},{3,1},{4,6},{6,4},{5,7},{7,5},{8,10},{10,8},{9,1... | collective-permute-start | bytes 1572872 | tf_op jit(solution)/shard_map/ppermute | solution.py:348
  20.1 12.8 %collective-permute-start.4 = (bf16[1024,256]{1,0:T(8,128)(2,1)S(1)}, bf16[1024,256]{1,0:T(8,128)(2,1)S(1)}, u32[]{:S(2)}, u32[]{:S(2)}) collective-permute-start(bf16[1024,256]{1,0:T(8,128)(2,1)S(1)} %collective-permute-done.3.refs_4_.direct), channel_id=1, source_target_pairs={{0,16},{16,0},{1,17},{17,1},{2,18},{18,2},{3,19},{19,3},{4,20},{20... | collective-permute-start | bytes 1572872 | tf_op jit(solution)/shard_map/ppermute | solution.py:349
  21.6 11.3 %collective-permute-start.6 = (bf16[64,4096]{1,0:T(8,128)(2,1)S(1)}, bf16[64,4096]{1,0:T(8,128)(2,1)S(1)}, u32[]{:S(2)}, u32[]{:S(2)}) collective-permute-start(bf16[64,4096]{1,0:T(8,128)(2,1)S(1)} %bitcast.6), channel_id=1, source_target_pairs={{4,8},{8,4},{5,9},{9,5},{6,10},{10,6},{7,11},{11,7},{20,24},{24,20... | collective-permute-start | bytes 1572872 | tf_op jit(solution)/shard_map/ppermute | solution.py:347
  23.0 15.7 %collective-permute-start.5 = (bf16[64,4096]{1,0:T(8,128)(2,1)S(1)}, bf16[64,4096]{1,0:T(8,128)(2,1)S(1)}, u32[]{:S(2)}, u32[]{:S(2)}) collective-permute-start(bf16[64,4096]{1,0:T(8,128)(2,1)S(1)} %bitcast.7), channel_id=1, source_target_pairs={{0,4},{4,0},{8,12},{12,8},{1,5},{5,1},{9,13},{13,9},{2,6},{6,2},{1... | collective-permute-start | bytes 1572872 | tf_op jit(solution)/shard_map/ppermute | solution.py:346
  31.4 12.2 %collective-permute-start.10 = (bf16[1024,256]{1,0:T(8,128)(2,1)S(1)}, bf16[1024,256]{1,0:T(8,128)(2,1)S(1)}, u32[]{:S(2)}, u32[]{:S(2)}) collective-permute-start(bf16[1024,256]{1,0:T(8,128)(2,1)S(1)} %get-tuple-element.49), channel_id=1, source_target_pairs={{0,2},{2,0},{1,3},{3,1},{4,6},{6,4},{5,7},{7,5},{8,10},{10,8},{9,1... | collective-permute-start | bytes 1572872 | tf_op jit(solution)/shard_map/ppermute | solution.py:357
  33.7 15.1 %collective-permute-start.8 = (bf16[64,4096]{1,0:T(8,128)(2,1)S(1)}, bf16[64,4096]{1,0:T(8,128)(2,1)S(1)}, u32[]{:S(2)}, u32[]{:S(2)}) collective-permute-start(bf16[64,4096]{1,0:T(8,128)(2,1)S(1)} %get-tuple-element.45), channel_id=1, source_target_pairs={{0,4},{4,0},{8,12},{12,8},{1,5},{5,1},{9,13},{13,9},{2,6},{6,2},{1... | collective-permute-start | bytes 1572872 | tf_op jit(solution)/shard_map/ppermute | solution.py:358
  38.7 12.8 %collective-permute-start.9 = (bf16[64,4096]{1,0:T(8,128)(2,1)S(1)}, bf16[64,4096]{1,0:T(8,128)(2,1)S(1)}, u32[]{:S(2)}, u32[]{:S(2)}) collective-permute-start(bf16[64,4096]{1,0:T(8,128)(2,1)S(1)} %collective-permute-done.5.refs_1_.refs_8_.refs_4_), channel_id=1, source_target_pairs={{4,8},{8,4},{5,9},{9,5},{6,10},{10,6},{7,11},{11,7},{20,24},{24,20... | collective-permute-start | bytes 1572872 | tf_op jit(solution)/shard_map/ppermute | solution.py:359
  43.6 11.3 %collective-permute-start.13 = (bf16[64,4096]{1,0:T(8,128)(2,1)S(1)}, bf16[64,4096]{1,0:T(8,128)(2,1)S(1)}, u32[]{:S(2)}, u32[]{:S(2)}) collective-permute-start(bf16[64,4096]{1,0:T(8,128)(2,1)S(1)} %get-tuple-element.55), channel_id=1, source_target_pairs={{0,2},{2,0},{1,3},{3,1},{4,6},{6,4},{5,7},{7,5},{8,10},{10,8},{9,1... | collective-permute-start | bytes 1572872 | tf_op jit(solution)/shard_map/ppermute | solution.py:369
  49.0 5.9 %collective-permute-start.14 = (bf16[64,4096]{1,0:T(8,128)(2,1)S(1)}, bf16[64,4096]{1,0:T(8,128)(2,1)S(1)}, u32[]{:S(2)}, u32[]{:S(2)}) collective-permute-start(bf16[64,4096]{1,0:T(8,128)(2,1)S(1)} %shard_map.109), channel_id=1, source_target_pairs={{4,8},{8,4},{5,9},{9,5},{6,10},{10,6},{7,11},{11,7},{20,24},{24,20... | collective-permute-start | bytes 1572872 | tf_op jit(solution)/shard_map/ppermute | solution.py:370
  51.5 14.0 %collective-permute-start.11 = (bf16[64,4096]{1,0:T(8,128)(2,1)S(1)}, bf16[64,4096]{1,0:T(8,128)(2,1)S(1)}, u32[]{:S(2)}, u32[]{:S(2)}) collective-permute-start(bf16[64,4096]{1,0:T(8,128)(2,1)S(1)} %collective-permute-done.9.refs_4_.refs_11_.refs_3_), channel_id=1, source_target_pairs={{4,0},{8,12},{5,1},{9,13},{6,2},{10,14},{7,3},{11,15},{20,16},{24,... | collective-permute-start | bytes 1572872 | tf_op jit(solution)/shard_map/ppermute | solution.py:371
  66.6 1.3 %collective-permute-start.15 = (f32[64,256]{1,0:T(8,128)S(1)}, f32[64,256]{1,0:T(8,128)S(1)}, u32[]{:S(2)}, u32[]{:S(2)}) collective-permute-start(f32[64,256]{1,0:T(8,128)S(1)} %shard_map.115.low), channel_id=1, source_target_pairs={{0,1},{1,0},{2,3},{3,2},{4,5},{5,4},{6,7},{7,6},{8,9},{9,8},{10,11... | collective-permute-start | bytes 196616 | tf_op jit(solution)/shard_map/ppermute | solution.py:381
  66.7 14.3 %collective-permute-start.12 = (bf16[1024,256]{1,0:T(8,128)(2,1)S(1)}, bf16[1024,256]{1,0:T(8,128)(2,1)S(1)}, u32[]{:S(2)}, u32[]{:S(2)}) collective-permute-start(bf16[1024,256]{1,0:T(8,128)(2,1)S(1)} %collective-permute-done.10.refs_2_.refs_3_), channel_id=1, source_target_pairs={{0,16},{16,0},{1,17},{17,1},{2,18},{18,2},{3,19},{19,3},{4,20},{20... | collective-permute-start | bytes 1572872 | tf_op jit(solution)/shard_map/ppermute | solution.py:372
  68.2 4.3 %collective-permute-start.18 = (bf16[128,256]{1,0:T(8,128)(2,1)S(1)}, bf16[128,256]{1,0:T(8,128)(2,1)S(1)}, u32[]{:S(2)}, u32[]{:S(2)}) collective-permute-start(bf16[128,256]{1,0:T(8,128)(2,1)S(1)} %get-tuple-element.63), channel_id=1, source_target_pairs={{0,2},{2,0},{1,3},{3,1},{4,6},{6,4},{5,7},{7,5},{8,10},{10,8},{9,1... | collective-permute-start | bytes 196616 | tf_op jit(solution)/shard_map/ppermute | solution.py:411
  68.8 16.7 %collective-permute-start.17 = (bf16[32,4096]{1,0:T(8,128)(2,1)S(1)}, bf16[32,4096]{1,0:T(8,128)(2,1)S(1)}, u32[]{:S(2)}, u32[]{:S(2)}) collective-permute-start(bf16[32,4096]{1,0:T(8,128)(2,1)S(1)} %get-tuple-element.56.refs_6_), channel_id=1, source_target_pairs={{0,4},{4,0},{8,12},{12,8},{1,5},{5,1},{9,13},{13,9},{2,6},{6,2},{1... | collective-permute-start | bytes 786440 | tf_op jit(solution)/shard_map/ppermute | solution.py:377
  72.6 12.3 %collective-permute-start.19 = (bf16[32,256]{1,0:T(8,128)(2,1)S(1)}, bf16[32,256]{1,0:T(8,128)(2,1)S(1)}, u32[]{:S(2)}, u32[]{:S(2)}) collective-permute-start(bf16[32,256]{1,0:T(8,128)(2,1)S(1)} %get-tuple-element.65), channel_id=1, source_target_pairs={{0,4},{4,0},{8,12},{12,8},{1,5},{5,1},{9,13},{13,9},{2,6},{6,2},{1... | collective-permute-start | bytes 49160 | tf_op jit(solution)/shard_map/ppermute | solution.py:416
  72.7 12.2 %collective-permute-start.20 = (bf16[32,256]{1,0:T(8,128)(2,1)S(1)}, bf16[32,256]{1,0:T(8,128)(2,1)S(1)}, u32[]{:S(2)}, u32[]{:S(2)}) collective-permute-start(bf16[32,256]{1,0:T(8,128)(2,1)S(1)} %get-tuple-element.66), channel_id=1, source_target_pairs={{0,8},{4,12},{8,0},{12,4},{1,9},{5,13},{9,1},{13,5},{2,10},{6,14},... | collective-permute-start | bytes 49160 | tf_op jit(solution)/shard_map/ppermute | solution.py:416
  75.8 9.1 %collective-permute-start.21 = (bf16[32,256]{1,0:T(8,128)(2,1)S(1)}, bf16[32,256]{1,0:T(8,128)(2,1)S(1)}, u32[]{:S(2)}, u32[]{:S(2)}) collective-permute-start(bf16[32,256]{1,0:T(8,128)(2,1)S(1)} %get-tuple-element.67), channel_id=1, source_target_pairs={{0,12},{4,8},{8,4},{12,0},{1,13},{5,9},{9,5},{13,1},{2,14},{6,10},... | collective-permute-start | bytes 49160 | tf_op jit(solution)/shard_map/ppermute | solution.py:416
  84.8 1.6 %collective-permute-start.16 = (f32[256,256]{1,0:T(8,128)S(1)}, f32[256,256]{1,0:T(8,128)S(1)}, u32[]{:S(2)}, u32[]{:S(2)}) collective-permute-start(f32[256,256]{1,0:T(8,128)S(1)} %get-tuple-element.59), channel_id=1, source_target_pairs={{0,1},{1,0},{2,3},{3,2},{4,5},{5,4},{6,7},{7,6},{8,9},{9,8},{10,11... | collective-permute-start | bytes 786440 | tf_op jit(solution)/shard_map/ppermute | solution.py:423

commit v3 on v2

--- a/solution.py
+++ b/solution.py
@@ -13,15 +13,16 @@
 F32 = jnp.float32
 PLAIN = (((1,), (0,)), ((), ()))
 CONTRACT_LAST = (((1,), (1,)), ((), ()))
-VMEM_BYTES = 16 * 1024 * 1024
+VMEM_BYTES = 10 * 1024 * 1024
 COLUMNS = 1024
-PART_US = 2
+OWN_PARTS = 4
+PART_US = 3.6
 SEND_US = 6
 FAR_US = 6
 SUM_US = 6
 NEAR_US = 6
 UP_US = 4
-LAST_US = 8
+LAST_US = 15
 FIRST_SHARE = 4
 WHOLE = pl.BlockSpec(memory_space=pltpu.VMEM)
 ANY = pl.BlockSpec(memory_space=pl.ANY)
@@ -49,13 +50,15 @@
     return lax.broadcasted_iota(jnp.int32, (span, job_row.shape[1]), 0) // rank == job_row
 
 
-def prepare_kernel(gradient, deal, job, up, part_out, deal_out, job_out, up_out):
+def prepare_kernel(gradient, deal, job, up, *refs):
     features = up.shape[1]
     start = pl.multiple_of(lax.axis_index("tp") * features, features)
-    part_out[...] = gradient[:, pl.ds(start, features)]
-    deal_out[...] = deal[...]
-    job_out[...] = job[...]
-    up_out[...] = up[...]
+    sources = gradient.at[:, pl.ds(start, features)], deal, job, up
+    copies = [pltpu.make_async_copy(source, out, refs[4].at[k]) for k, (source, out) in enumerate(zip(sources, refs))]
+    for copy in copies:
+        copy.start()
+    for copy in copies:
+        copy.wait()
 
 
 def grad_partial_kernel(rank, near, far, gradient, deal, job, out):
@@ -128,14 +131,20 @@
         swap_out[:, at] = jnp.where(in_middle(), down_cross[:, at], made)
 
 
-def near_kernel(rank, got, grad_rank, deal, tokens, cross, next_out, mine_out):
+def near_kernel(rank, got, grad_rank, deal, cross, tokens, next_out, mine_out, held, sems):
+    copies = [
+        pltpu.make_async_copy(tokens.at[:, at], held.at[:, at], sems.at[k])
+        for k, at in enumerate(pl.ds(k * COLUMNS, COLUMNS) for k in range(tokens.shape[1] // COLUMNS))
+    ]
+    for copy in copies:
+        copy.start()
     mine, beside, _, _ = holders()
     wide = wide_rows(kept_rows(rank, grad_rank), deal[...], (beside, mine))
     split = next_out.shape[0]
-
-    @each_column(tokens)
-    def _(at):
-        made = dot(wide, tokens[:, at]) + got[:, at].astype(F32) + cross[:, at].astype(F32)
+    for k, copy in enumerate(copies):
+        at = pl.ds(k * COLUMNS, COLUMNS)
+        copy.wait()
+        made = dot(wide, held[:, at]) + got[:, at].astype(F32) + cross[:, at].astype(F32)
         next_out[:, at] = made[:split].astype(BF16)
         mine_out[:, at] = made[split:]
 
@@ -190,46 +199,54 @@
         out[...] = total[(k + 1) * half : (k + 2) * half].astype(BF16)
 
 
-def own_kernel(tokens, own, out):
-    out[...] = dot(tokens[...], own[...])
-
-
-def base_kernel(offset, gradient, grad_rank, deal, direct, relayed, tokens, own, *refs):
-    downs, (grad_out, other_out) = refs[:6], refs[-10:-8]
-    wide, buffer, weight_in, own_in, token_in, down_in, sems, out_sems = refs[-8:]
+def own_kernel(tokens, own, out, buffer, sems):
+    count = own.shape[0] // OWN_PARTS
+    copies = []
+    for k in range(OWN_PARTS):
+        at = pl.ds(k * count, count)
+        copies.append(pltpu.make_async_copy(own.at[at], buffer.at[at], sems.at[k]))
+        copies[-1].start()
+    for k, copy in enumerate(copies):
+        at = pl.ds(k * count, count)
+        copy.wait()
+        part = dot(tokens[:, at], buffer[at])
+        out[...] = part if k == 0 else out[...] + part
+
+
+def base_kernel(offset, gradient, grad_rank, deal, direct, relayed, *refs):
+    downs, (tokens, own) = refs[:6], refs[6:8]
+    grad_out, other_out, wide, buffer, own_in, token_in, sems, out_sems = refs[-8:]
     features = own.shape[1]
     count = direct.shape[0]
     mine = pl.multiple_of(lax.axis_index("fsdp") * features, features)
     other = pl.multiple_of((1 - lax.axis_index("fsdp")) * features, features)
     rep = lax.axis_index("rep")
-    spots = []
+    spots, copies, stores = [], [], []
     for side in range(2):
         start = (rep ^ side) * (own.shape[0] // 2) + offset
         spots.append(pl.ds(pl.multiple_of(start, 256), count))
-    copies = []
-    for side, (at, weight) in enumerate(zip(spots, (direct, relayed))):
-        wanted = [(own.at[at, :], own_in.at[side]), (weight, weight_in.at[side])]
-        wanted += [(down.at[:, at], down_in.at[side, k]) for k, down in enumerate(downs)]
-        wanted += [(tokens.at[:, at], token_in.at[side])]
-        copies.append([pltpu.make_async_copy(*pair, sems.at[side, i]) for i, pair in enumerate(wanted)])
-        for copy in copies[-1]:
+        copies.append(
+            [
+                pltpu.make_async_copy(own.at[spots[side], :], own_in.at[side], sems.at[side, 0]),
+                pltpu.make_async_copy(tokens.at[:, spots[side]], token_in.at[side], sems.at[side, 1]),
+            ]
+        )
+        for copy in copies[side]:
             copy.start()
     narrow = ADAPTER_SCALE * grad_rank[...].astype(F32)
     wide[...] = jnp.concatenate([jnp.where(deal[...] == name, narrow, 0.0) for name in holders()]).T.astype(BF16)
-    stores = []
-    for side, at in enumerate(spots):
-        for copy in copies[side][:-1]:
-            copy.wait()
-        total = dot(gradient[:, pl.ds(mine, features)], own_in[side], CONTRACT_LAST)
-        total += dot(gradient[:, pl.ds(other, features)], weight_in[side], CONTRACT_LAST)
-        parts = [down_in[side, k] for k in range(6)]
+    for side, (at, weight) in enumerate(zip(spots, (direct, relayed))):
+        parts = [down[:, at] for down in downs]
         parts[2:] = [jnp.where(in_middle(), parts[k], parts[k + 1]) for k in (2, 4)]
-        total += dot(wide[...], jnp.concatenate(parts))
+        total = dot(wide[...], jnp.concatenate(parts))
+        total += dot(gradient[:, pl.ds(other, features)], weight[...], CONTRACT_LAST)
+        copies[side][0].wait()
+        total += dot(gradient[:, pl.ds(mine, features)], own_in[side], CONTRACT_LAST)
         buffer[side] = total.astype(BF16)
         stores.append(pltpu.make_async_copy(buffer.at[side], grad_out.at[:, at], out_sems.at[side]))
-        stores[-1].start()
-        copies[side][-1].wait()
-        other_part = dot(token_in[side], weight_in[side])
+        stores[side].start()
+        copies[side][1].wait()
+        other_part = dot(token_in[side], weight[...])
         other_out[...] = other_part if side == 0 else other_out[...] + other_part
     for store in stores:
         store.wait()
@@ -320,6 +337,7 @@
     grad_mine, deal, job, up = call(
         prepare_kernel, (struct((rows, features), BF16), row, row, struct((span, features), BF16)),
         output_gradient, deal, job, up,
+        in_specs=[ANY] * 4, scratch_shapes=[pltpu.SemaphoreType.DMA((4,))],
     )
     up_pair = call(join_kernel, struct((2 * span, features), BF16), up, up_got_first, after=(grad_mine,))
     ups = up_pair, lax.ppermute(up_pair, "dp", swap(4, 2))
@@ -327,7 +345,7 @@
         cut_kernel,
         (struct((first_rows, features), BF16), struct((width // 2 - first_rows, features), BF16)),
         frozen_value_weight,
-        in_specs=[ANY],
+        in_specs=[HBM],
         out_specs=(ANY, ANY),
         scratch_shapes=[pltpu.SemaphoreType.DMA((2,))],
     )
@@ -342,21 +360,27 @@
         functools.partial(grad_send_kernel, rank), (struct((span, rows), BF16), span_wide, span_wide),
         grad_part, grad_got, deal, tokens, after=(got_first,), us=SEND_US,
     )
-    down_sent = ordered(down, send_far)
+    down_sent = ordered(down, grad_part)
     down_next = lax.ppermute(down_sent, "dp", swap(4))
-    down_cross = lax.ppermute(down_sent, "dp", middle)
+    down_cross = lax.ppermute(ordered(down, grad_part), "dp", middle)
     got_far = lax.ppermute(send_far, "fsdp", swap(2))
-    relay_first = lax.ppermute(ordered(got_first, send_far), "rep", swap(2))
     own_out = call(
-        own_kernel, struct((rows, features), F32), tokens, frozen_value_weight, after=(send_far,)
-    )
+        own_kernel,
+        struct((rows, features), F32),
+        tokens,
+        frozen_value_weight,
+        after=(send_far,),
+        in_specs=[WHOLE, HBM],
+        scratch_shapes=[pltpu.VMEM((width, features), BF16), pltpu.SemaphoreType.DMA((OWN_PARTS,))],
+    )
+    relay_first = lax.ppermute(ordered(got_first, own_out), "rep", swap(2))
     far, far_swap = call(
         functools.partial(far_kernel, rank), (span_wide, span_wide),
-        got_far, grad_rank, deal, tokens, down_cross, after=(own_out, relay_first), us=FAR_US,
+        got_far, grad_rank, deal, tokens, down_cross, after=(own_out, down_next), us=FAR_US,
     )
     got_second = lax.ppermute(ordered(weight_second, got_far), "fsdp", swap(2))
     swapped = lax.ppermute(far_swap, "dp", swap(4))
-    down_cross2 = lax.ppermute(ordered(down_next, far), "dp", middle)
+    down_cross2 = lax.ppermute(ordered(down_next, down_cross), "dp", middle)
     low_near = call(
         functools.partial(low_kernel, rank, (0, 1), (1, 1)),
         narrow, tokens, deal, job, down, down_next, after=(far,),
@@ -365,18 +389,13 @@
         functools.partial(low_kernel, rank, (2,), (2,)),
         narrow, tokens, deal, job, down_cross, swapped, low_near,
     )
-    far_sum = call(add_kernel, span_wide, far, swapped, after=(got_second,), us=SUM_US)
+    far_sum = call(add_kernel, span_wide, far, swapped, after=(got_second, down_cross2, relay_first, low_near), us=SUM_US)
     got_near = lax.ppermute(ordered(send_near, got_second), "fsdp", swap(2))
     cross = lax.ppermute(far_sum, "dp", middle)
-    down_out2 = lax.ppermute(ordered(down_cross2, far_sum), "dp", outward)
+    down_out2 = lax.ppermute(ordered(down_cross2, far), "dp", outward)
     relay_second = lax.ppermute(got_second, "rep", swap(2))
-    next_sum, mine_sum = call(
-        functools.partial(near_kernel, rank), (half_wide, struct((half, width), F32)),
-        got_near, grad_rank, deal, tokens, cross, us=NEAR_US,
-    )
-    last = lax.ppermute(next_sum, "dp", swap(4))
     low_part = call(
-        functools.partial(low_kernel, rank, (3,), (2,)), narrow, tokens, deal, job, down_cross2, down_out2, low_first, after=(next_sum,)
+        functools.partial(low_kernel, rank, (3,), (2,)), narrow, tokens, deal, job, down_cross2, down_out2, low_first, after=()
     )
     low_got = lax.ppermute(low_part, "tp", swap(2))
     up_half = struct((4 * half, features), F32), struct((4 * half, features), BF16)
@@ -389,39 +408,42 @@
         return call(
             functools.partial(base_kernel, offset),
             (struct((rows, width), BF16), struct((rows, features), F32)),
-            output_gradient, grad_rank, deal, direct, relayed, tokens, frozen_value_weight,
-            down, down_next, down_cross, swapped, down_cross2, down_out2,
+            output_gradient, grad_rank, deal, direct, relayed,
+            down, down_next, down_cross, swapped, down_cross2, down_out2, tokens, frozen_value_weight,
             after=into,
-            in_specs=[WHOLE] * 3 + [HBM] * 10,
+            in_specs=[WHOLE] * 11 + [HBM] * 2,
             out_specs=(HBM, WHOLE),
             scratch_shapes=[
                 pltpu.VMEM((rows, 4 * span), BF16),
                 pltpu.VMEM((2, rows, count), BF16),
                 pltpu.VMEM((2, count, features), BF16),
-                pltpu.VMEM((2, count, features), BF16),
                 pltpu.VMEM((2, rows, count), BF16),
-                pltpu.VMEM((2, 6, span, count), BF16),
-                pltpu.SemaphoreType.DMA((2, 9)),
+                pltpu.SemaphoreType.DMA((2, 2)),
                 pltpu.SemaphoreType.DMA((2,)),
             ],
             input_output_aliases={13: 0} if into else {},
         )
 
     input_first, other_first = base(0, got_first, relay_first)
+    next_sum, mine_sum = call(
+        functools.partial(near_kernel, rank), (half_wide, struct((half, width), F32)),
+        got_near, grad_rank, deal, cross, tokens, after=(up_away, input_first, relay_second), us=NEAR_US,
+        in_specs=[WHOLE] * 4 + [HBM],
+        scratch_shapes=[pltpu.VMEM((rows, width), BF16), pltpu.SemaphoreType.DMA((width // COLUMNS,))],
+    )
+    last = lax.ppermute(next_sum, "dp", swap(4))
     up_got = lax.ppermute(up_away, "fsdp", swap(2))
     up_mine, *up_sent = call(
         up_sum_kernel, (struct((half, features), F32),) + (struct((half, features), BF16),) * 3, up_keep, up_got,
         us=UP_US,
     )
     up_last = [lax.ppermute(sent, "dp", swap(4, k + 1)) for k, sent in enumerate(up_sent)]
-    up_share = call(total_kernel, struct((half, features), F32), up_mine, *up_last)
 
     input_gradient, other_second = base(first_rows, got_second, relay_second, input_first)
-    base_send, base_keep = call(
-        share_kernel, (struct((rows, features), F32),) * 2, own_out, other_first, other_second, lora
-    )
+    base_send, base_keep = call(share_kernel, (struct((rows, features), F32),) * 2, own_out, other_first, other_second, lora)
     base_got = lax.ppermute(base_send, "tp", swap(2))
     value_output = call(total_kernel, struct((rows, features), BF16), base_keep, base_got)
+    up_share = call(total_kernel, struct((half, features), F32), up_mine, *up_last, after=(base_send,))
     down_share = call(total_kernel, struct((half, width), F32), mine_sum, last, us=LAST_US)
     shares = [share.reshape(jobs, rank // 2, share.shape[1]) for share in (down_share, up_share)]
     return value_output, input_gradient, *shares

time: 87.3 us -> 78.8 us (0.903)
  waiting for transfers between devices: 35.5 us -> 27.5 us
  starting transfers between devices: 31.3 us -> 28.7 us
  local copies, waits for them, and re-layouts: 1.62 us -> 3.88 us
    ppermute x1, waiting for transfers between devices: 0.46 us -> 5.66 us  [gather_adapters(): down_next = lax.ppermute(down_sent, 'dp', swap(4))]
    ppermute x1, waiting for transfers between devices: 3.94 us -> 0.01 us  [gather_adapters(): swapped = lax.ppermute(far_swap, 'dp', swap(4))]
    ppermute x1, waiting for transfers between devices: 3.74 us -> 0.4 us  [gather_adapters(): up_got = lax.ppermute(up_away, 'fsdp', swap(2))]
    ppermute x1, starting transfers between devices: 4.48 us -> 1.35 us  [gather_adapters(): swapped = lax.ppermute(far_swap, 'dp', swap(4))]
    ppermute x1, waiting for transfers between devices: 2.31 us -> 0.01 us  [gather_adapters(): up_got_first = lax.ppermute(up, 'dp', swap(4))]
    unnamed x16 -> x18, local copies, waits for them, and re-layouts: 1.62 us -> 3.88 us
    ppermute x1, waiting for transfers between devices: 4 us -> 1.82 us  [gather_adapters(): got_far = lax.ppermute(send_far, 'fsdp', swap(2))]
    ppermute x3, waiting for transfers between devices: 0.01 us -> 2.07 us  [gather_adapters(): lax.ppermute(sent, 'dp', swap(4, k + 1))]
  transfers between devices with their start and end apart: 22 -> 22, of which waited for: 13 -> 9; matrix products, arithmetic and copies ran while one was open for 0% -> 0% of each run, Pallas kernels for 17% -> 22%
where the time goes in v3:
time: 78.8 us; the launch traced here: 78.5 us
  starting transfers between devices  28.7 us (36%)
  waiting for transfers between devices  27.5 us (35%)
  Pallas kernels  17.6 us (22%)
  local copies, waits for them, and re-layouts  3.88 us (5%)
  between operations  0.87 us (1%)
    pallas_call x20, Pallas kernels, call(): pl.pallas_call(kernel, out_shape=out_shape, in_specs=(in_specs or [WHOLE]...  17.6 us
    ppermute x1, waiting for transfers between devices, gather_adapters(): down_out2 = lax.ppermute(ordered(down_cross2, far), 'dp', outward)  8.31 us
    ppermute x1, waiting for transfers between devices, gather_adapters(): got_second = lax.ppermute(ordered(weight_second, got_far), 'fsdp', swap(2))  5.71 us
    ppermute x1, waiting for transfers between devices, gather_adapters(): down_next = lax.ppermute(down_sent, 'dp', swap(4))  5.66 us
    ppermute x3, starting transfers between devices, gather_adapters(): lax.ppermute(sent, 'dp', swap(4, k + 1))  4.45 us
    unnamed x18, local copies, waits for them, and re-layouts  3.88 us
    ppermute x1, starting transfers between devices, gather_adapters(): down_next = lax.ppermute(down_sent, 'dp', swap(4))  3.73 us
    ppermute x1, waiting for transfers between devices, gather_adapters(): ups = (up_pair, lax.ppermute(up_pair, 'dp', swap(4, 2)))  3.28 us
  transfers between devices with their start and end apart: 22, of which 9 were waited for; matrix products, arithmetic and copies ran while one was open for 0% of the time, Pallas kernels for 22%

profile of v3, /device:TPU:0, one launch (start us, length us, event | category | flops | bytes accessed | tf_op | source)
XLA Modules:
  0.0 78.5 jit_solution(14553229966663273076)
XLA Ops:
  0.6 3.1 %collective-permute-start = (bf16[64,256]{1,0:T(8,128)(2,1)}, bf16[64,256]{1,0:T(8,128)(2,1)S(1)}, u32[]{:S(2)}, u32[]{:S(2)}) collective-permute-start(bf16[64,256]{1,0:T(8,128)(2,1)} %bitcast.11), channel_id=1, source_target_pairs={{0,4},{4,0},{8,12},{12,8},{1,5},{5,1},{9,13},{13,9},{2,6},{6,2},{1... | collective-permute-start | bytes 98312 | tf_op jit(solution)/shard_map/ppermute | solution.py:335
  3.7 1.6 %copy-done.1 = bf16[4096,256]{1,0:T(8,128)(2,1)S(1)} copy-done((bf16[4096,256]{1,0:T(8,128)(2,1)S(1)}, bf16[4096,256]{1,0:T(8,128)(2,1)}, u32[]{:S(2)}) %copy-start.1) | copy-done | bytes 2097176
  5.3 0.1 shard_map.105
  5.4 1.6 %collective-permute-start.3 = (bf16[1024,256]{1,0:T(8,128)(2,1)S(1)}, bf16[1024,256]{1,0:T(8,128)(2,1)S(1)}, u32[]{:S(2)}, u32[]{:S(2)}) collective-permute-start(bf16[1024,256]{1,0:T(8,128)(2,1)S(1)} %get-tuple-element.40), channel_id=1, source_target_pairs={{0,2},{2,0},{1,3},{3,1},{4,6},{6,4},{5,7},{7,5},{8,10},{10,8},{9,1... | collective-permute-start | bytes 1572872 | tf_op jit(solution)/shard_map/ppermute | solution.py:352
  7.0 0.1 shard_map.102
  7.1 0.0 collective-permute-done.refs_1_
  7.1 2.7 %collective-permute-start.1 = (bf16[128,256]{1,0:T(8,128)(2,1)S(1)}, bf16[128,256]{1,0:T(8,128)(2,1)S(1)}, u32[]{:S(2)}, u32[]{:S(2)}) collective-permute-start(bf16[128,256]{1,0:T(8,128)(2,1)S(1)} %shard_map.103.near), channel_id=1, source_target_pairs={{0,8},{4,12},{8,0},{12,4},{1,9},{5,13},{9,1},{13,5},{2,10},{6,14},... | collective-permute-start | bytes 196616 | tf_op jit(solution)/shard_map/ppermute | solution.py:343
  9.8 3.3 %collective-permute-done.1.far = bf16[128,256]{1,0:T(8,128)(2,1)S(1)} collective-permute-done((bf16[128,256]{1,0:T(8,128)(2,1)S(1)}, bf16[128,256]{1,0:T(8,128)(2,1)S(1)}, u32[]{:S(2)}, u32[]{:S(2)}) %collective-permute-start.1) | collective-permute-done | bytes 65568 | tf_op jit(solution)/shard_map/ppermute | solution.py:343
  13.1 0.3 shard_map.104.refs_0_
  13.4 0.1 collective-permute-start.2
  13.4 0.7 copy-done.3
  14.1 0.8 %collective-permute-start.6 = (bf16[64,4096]{1,0:T(8,128)(2,1)S(1)}, bf16[64,4096]{1,0:T(8,128)(2,1)S(1)}, u32[]{:S(2)}, u32[]{:S(2)}) collective-permute-start(bf16[64,4096]{1,0:T(8,128)(2,1)S(1)} %bitcast.6), channel_id=1, source_target_pairs={{4,8},{8,4},{5,9},{9,5},{6,10},{10,6},{7,11},{11,7},{20,24},{24,20... | collective-permute-start | bytes 1572872 | tf_op jit(solution)/shard_map/ppermute | solution.py:365
  14.9 3.7 %collective-permute-start.5 = (bf16[64,4096]{1,0:T(8,128)(2,1)S(1)}, bf16[64,4096]{1,0:T(8,128)(2,1)S(1)}, u32[]{:S(2)}, u32[]{:S(2)}) collective-permute-start(bf16[64,4096]{1,0:T(8,128)(2,1)S(1)} %bitcast.7), channel_id=1, source_target_pairs={{0,4},{4,0},{8,12},{12,8},{1,5},{5,1},{9,13},{13,9},{2,6},{6,2},{1... | collective-permute-start | bytes 1572872 | tf_op jit(solution)/shard_map/ppermute | solution.py:364
  18.7 0.0 collective-permute-done.2.refs_1_
  18.7 0.2 collective-permute-done.3.refs_4_.direct
  18.9 1.0 %shard_map.106 = (bf16[64,256]{1,0:T(8,128)(2,1)S(1)}, bf16[64,4096]{1,0:T(8,128)(2,1)S(1)}, bf16[64,4096]{1,0:T(8,128)(2,1)S(1)}) custom-call(f32[64,256]{1,0:T(8,128)S(1)} %shard_map.104.refs_0_, f32[64,256]{1,0:T(8,128)S(1)} %collective-permute-done.2.refs_1_, s32[1,256]{1,0:T(1,128)S(1)} %get-tuple-element.38.deal.refs_2_.refs_1_, ...), custom_call_target="tpu_custom_call" | custom-call | flops 6899999744 | tf_op jit(solution)/shard_map/pallas_call | solution.py:262
  19.9 1.6 %collective-permute-start.7 = (bf16[64,4096]{1,0:T(8,128)(2,1)S(1)}, bf16[64,4096]{1,0:T(8,128)(2,1)S(1)}, u32[]{:S(2)}, u32[]{:S(2)}) collective-permute-start(bf16[64,4096]{1,0:T(8,128)(2,1)S(1)} %get-tuple-element.41.refs_2_), channel_id=1, source_target_pairs={{0,2},{2,0},{1,3},{3,1},{4,6},{6,4},{5,7},{7,5},{8,10},{10,8},{9,1... | collective-permute-start | bytes 1572872 | tf_op jit(solution)/shard_map/ppermute | solution.py:366
  21.4 1.6 %shard_map.107.refs_5_.own = f32[256,256]{1,0:T(8,128)S(1)} custom-call(bf16[256,4096]{1,0:T(8,128)(2,1)S(1)} %copy-done, bf16[4096,256]{1,0:T(8,128)(2,1)S(1)} %copy-done.2, bf16[64,4096]{1,0:T(8,128)(2,1)S(1)} %get-tuple-element.41.refs_2_), custom_call_target="tpu_custom_call" | custom-call | tf_op jit(solution)/shard_map/pallas_call | solution.py:262
  23.0 1.6 %collective-permute-start.4 = (bf16[1024,256]{1,0:T(8,128)(2,1)S(1)}, bf16[1024,256]{1,0:T(8,128)(2,1)S(1)}, u32[]{:S(2)}, u32[]{:S(2)}) collective-permute-start(bf16[1024,256]{1,0:T(8,128)(2,1)S(1)} %collective-permute-done.3.refs_4_.direct), channel_id=1, source_target_pairs={{0,16},{16,0},{1,17},{17,1},{2,18},{18,2},{3,19},{19,3},{4,20},{20... | collective-permute-start | bytes 1572872 | tf_op jit(solution)/shard_map/ppermute | solution.py:376
  24.6 0.0 collective-permute-done.6.refs_4_.refs_2_.refs_7_.refs_3_
  24.6 5.7 %collective-permute-done.5.refs_6_.refs_1_.refs_4_ = bf16[64,4096]{1,0:T(8,128)(2,1)S(1)} collective-permute-done((bf16[64,4096]{1,0:T(8,128)(2,1)S(1)}, bf16[64,4096]{1,0:T(8,128)(2,1)S(1)}, u32[]{:S(2)}, u32[]{:S(2)}) %collective-permute-start.5) | collective-permute-done | bytes 524320 | tf_op jit(solution)/shard_map/ppermute | solution.py:364
  30.3 0.7 collective-permute-start.9
  31.0 1.8 %collective-permute-done.7.refs_0_ = bf16[64,4096]{1,0:T(8,128)(2,1)S(1)} collective-permute-done((bf16[64,4096]{1,0:T(8,128)(2,1)S(1)}, bf16[64,4096]{1,0:T(8,128)(2,1)S(1)}, u32[]{:S(2)}, u32[]{:S(2)}) %collective-permute-start.7) | collective-permute-done | bytes 524320 | tf_op jit(solution)/shard_map/ppermute | solution.py:366
  32.8 1.1 %collective-permute-start.11 = (bf16[1024,256]{1,0:T(8,128)(2,1)S(1)}, bf16[1024,256]{1,0:T(8,128)(2,1)S(1)}, u32[]{:S(2)}, u32[]{:S(2)}) collective-permute-start(bf16[1024,256]{1,0:T(8,128)(2,1)S(1)} %get-tuple-element.51), channel_id=1, source_target_pairs={{0,2},{2,0},{1,3},{3,1},{4,6},{6,4},{5,7},{7,5},{8,10},{10,8},{9,1... | collective-permute-start | bytes 1572872 | tf_op jit(solution)/shard_map/ppermute | solution.py:381
  33.9 0.9 %shard_map.108 = (bf16[64,4096]{1,0:T(8,128)(2,1)S(1)}, bf16[64,4096]{1,0:T(8,128)(2,1)S(1)}) custom-call(bf16[64,4096]{1,0:T(8,128)(2,1)S(1)} %collective-permute-done.7.refs_0_, bf16[64,256]{1,0:T(8,128)(2,1)S(1)} %get-tuple-element.42.refs_1_.grad_rank, s32[1,256]{1,0:T(1,128)S(1)} %get-tuple-element.38.deal.refs_2_.refs_1_, ...), custom_call_target="tpu_custom_call" | custom-call | flops 6899999744 | tf_op jit(solution)/shard_map/pallas_call | solution.py:262
  34.8 1.4 %collective-permute-start.8 = (bf16[64,4096]{1,0:T(8,128)(2,1)S(1)}, bf16[64,4096]{1,0:T(8,128)(2,1)S(1)}, u32[]{:S(2)}, u32[]{:S(2)}) collective-permute-start(bf16[64,4096]{1,0:T(8,128)(2,1)S(1)} %get-tuple-element.45), channel_id=1, source_target_pairs={{0,4},{4,0},{8,12},{12,8},{1,5},{5,1},{9,13},{13,9},{2,6},{6,2},{1... | collective-permute-start | bytes 1572872 | tf_op jit(solution)/shard_map/ppermute | solution.py:382
  36.1 1.8 %shard_map.111.refs_5_ = f32[64,256]{1,0:T(8,128)S(1)} custom-call(bf16[256,4096]{1,0:T(8,128)(2,1)S(1)} %copy-done, s32[1,256]{1,0:T(1,128)S(1)} %get-tuple-element.38.deal.refs_2_.refs_1_, s32[1,256]{1,0:T(1,128)S(1)} %get-tuple-element.39.job.refs_2_, bf16[64,4096]{1,0:T(8,128)(2,1)S(1)} %bitcast.8, ...), custom_call_target="tpu_custom_call" | custom-call | tf_op jit(solution)/shard_map/pallas_call | solution.py:262
  37.9 0.0 collective-permute-done.9.refs_4_.refs_9_.refs_3_
  37.9 1.3 %collective-permute-start.10 = (bf16[64,4096]{1,0:T(8,128)(2,1)S(1)}, bf16[64,4096]{1,0:T(8,128)(2,1)S(1)}, u32[]{:S(2)}, u32[]{:S(2)}) collective-permute-start(bf16[64,4096]{1,0:T(8,128)(2,1)S(1)} %collective-permute-done.9.refs_4_.refs_9_.refs_3_), channel_id=1, source_target_pairs={{4,0},{8,12},{5,1},{9,13},{6,2},{10,14},{7,3},{11,15},{20,16},{24,... | collective-permute-start | bytes 1572872 | tf_op jit(solution)/shard_map/ppermute | solution.py:395
  39.2 5.7 %collective-permute-done.11.refs_3_.refs_2_ = bf16[1024,256]{1,0:T(8,128)(2,1)S(1)} collective-permute-done((bf16[1024,256]{1,0:T(8,128)(2,1)S(1)}, bf16[1024,256]{1,0:T(8,128)(2,1)S(1)}, u32[]{:S(2)}, u32[]{:S(2)}) %collective-permute-start.11) | collective-permute-done | bytes 524320 | tf_op jit(solution)/shard_map/ppermute | solution.py:381
  44.9 1.0 %collective-permute-start.15 = (bf16[64,4096]{1,0:T(8,128)(2,1)S(1)}, bf16[64,4096]{1,0:T(8,128)(2,1)S(1)}, u32[]{:S(2)}, u32[]{:S(2)}) collective-permute-start(bf16[64,4096]{1,0:T(8,128)(2,1)S(1)} %get-tuple-element.59), channel_id=1, source_target_pairs={{0,2},{2,0},{1,3},{3,1},{4,6},{6,4},{5,7},{7,5},{8,10},{10,8},{9,1... | collective-permute-start | bytes 1572872 | tf_op jit(solution)/shard_map/ppermute | solution.py:393
  45.9 1.5 %collective-permute-start.12 = (bf16[1024,256]{1,0:T(8,128)(2,1)S(1)}, bf16[1024,256]{1,0:T(8,128)(2,1)S(1)}, u32[]{:S(2)}, u32[]{:S(2)}) collective-permute-start(bf16[1024,256]{1,0:T(8,128)(2,1)S(1)} %collective-permute-done.11.refs_3_.refs_2_), channel_id=1, source_target_pairs={{0,16},{16,0},{1,17},{17,1},{2,18},{18,2},{3,19},{19,3},{4,20},{20... | collective-permute-start | bytes 1572872 | tf_op jit(solution)/shard_map/ppermute | solution.py:396
  47.4 0.0 collective-permute-done.4.relayed.refs_4_
  47.4 0.0 collective-permute-done.8.refs_3_.refs_8_.refs_4_.refs_1_
  47.4 0.1 shard_map.117
  47.5 0.7 collective-permute-start.16
  48.3 1.2 %shard_map.112.refs_5_ = f32[64,256]{1,0:T(8,128)S(1)} custom-call(bf16[256,4096]{1,0:T(8,128)(2,1)S(1)} %copy-done, s32[1,256]{1,0:T(1,128)S(1)} %get-tuple-element.38.deal.refs_2_.refs_1_, s32[1,256]{1,0:T(1,128)S(1)} %get-tuple-element.39.job.refs_2_, bf16[64,4096]{1,0:T(8,128)(2,1)S(1)} %collective-permute-done.6.refs_4_.refs_2_.refs_7_.refs_3_, ...), custom_call_target="tpu_custom_call" | custom-call | tf_op jit(solution)/shard_map/pallas_call | solution.py:262
  49.4 8.3 %collective-permute-done.10.refs_5_.refs_10_.refs_4_ = bf16[64,4096]{1,0:T(8,128)(2,1)S(1)} collective-permute-done((bf16[64,4096]{1,0:T(8,128)(2,1)S(1)}, bf16[64,4096]{1,0:T(8,128)(2,1)S(1)}, u32[]{:S(2)}, u32[]{:S(2)}) %collective-permute-start.10) | collective-permute-done | bytes 524320 | tf_op jit(solution)/shard_map/ppermute | solution.py:395
  57.7 1.1 %shard_map.113.low = f32[64,256]{1,0:T(8,128)S(1)} custom-call(bf16[256,4096]{1,0:T(8,128)(2,1)S(1)} %copy-done, s32[1,256]{1,0:T(1,128)S(1)} %get-tuple-element.38.deal.refs_2_.refs_1_, s32[1,256]{1,0:T(1,128)S(1)} %get-tuple-element.39.job.refs_2_, bf16[64,4096]{1,0:T(8,128)(2,1)S(1)} %collective-permute-done.9.refs_4_.refs_9_.refs_3_, ...), custom_call_target="tpu_custom_call" | custom-call | tf_op jit(solution)/shard_map/pallas_call | solution.py:262
  58.9 0.1 collective-permute-start.13
  59.0 2.9 %shard_map.109 = (bf16[256,4096]{1,0:T(8,128)(2,1)}, f32[256,256]{1,0:T(8,128)S(1)}) custom-call(bf16[256,512]{1,0:T(8,128)(2,1)S(1)} %copy-done.4, bf16[64,256]{1,0:T(8,128)(2,1)S(1)} %get-tuple-element.42.refs_1_.grad_rank, s32[1,256]{1,0:T(1,128)S(1)} %get-tuple-element.38.deal.refs_2_.refs_1_, ...), custom_call_target="tpu_custom_call" | custom-call | tf_op jit(solution)/shard_map/pallas_call | solution.py:262
  61.9 0.0 collective-permute-done.13.low_got
  61.9 0.3 shard_map.114
  62.2 1.3 %collective-permute-start.18 = (bf16[128,256]{1,0:T(8,128)(2,1)S(1)}, bf16[128,256]{1,0:T(8,128)(2,1)S(1)}, u32[]{:S(2)}, u32[]{:S(2)}) collective-permute-start(bf16[128,256]{1,0:T(8,128)(2,1)S(1)} %get-tuple-element.60.refs_5_), channel_id=1, source_target_pairs={{0,2},{2,0},{1,3},{3,1},{4,6},{6,4},{5,7},{7,5},{8,10},{10,8},{9,1... | collective-permute-start | bytes 196616 | tf_op jit(solution)/shard_map/ppermute | solution.py:435
  63.5 0.0 collective-permute-done.15.refs_0_
  63.5 0.0 collective-permute-done.12.refs_4_.refs_7_
  63.5 0.0 collective-permute-done.16.refs_3_
  63.5 0.0 copy-start.5
  63.5 1.6 %copy-done.5 = bf16[256,4096]{1,0:T(8,128)(2,1)S(1)} copy-done((bf16[256,4096]{1,0:T(8,128)(2,1)S(1)}, bf16[256,4096]{1,0:T(8,128)(2,1)}, u32[]{:S(2)}) %copy-start.5) | copy-done | bytes 2097176
  65.1 1.1 %shard_map.118 = (bf16[32,4096]{1,0:T(8,128)(2,1)S(1)}, f32[32,4096]{1,0:T(8,128)S(1)}) custom-call(bf16[64,4096]{1,0:T(8,128)(2,1)S(1)} %collective-permute-done.15.refs_0_, bf16[64,256]{1,0:T(8,128)(2,1)S(1)} %get-tuple-element.42.refs_1_.grad_rank, s32[1,256]{1,0:T(1,128)S(1)} %get-tuple-element.38.deal.refs_2_.refs_1_, ...), custom_call_target="tpu_custom_call" | custom-call | flops 6899999744 | tf_op jit(solution)/shard_map/pallas_call | solution.py:262
  66.3 0.1 collective-permute-start.17
  66.3 0.4 collective-permute-done.18.got
  66.8 1.7 %collective-permute-start.19 = (bf16[32,256]{1,0:T(8,128)(2,1)S(1)}, bf16[32,256]{1,0:T(8,128)(2,1)S(1)}, u32[]{:S(2)}, u32[]{:S(2)}) collective-permute-start(bf16[32,256]{1,0:T(8,128)(2,1)S(1)} %get-tuple-element.65), channel_id=1, source_target_pairs={{0,4},{4,0},{8,12},{12,8},{1,5},{5,1},{9,13},{13,9},{2,6},{6,2},{1... | collective-permute-start | bytes 49160 | tf_op jit(solution)/shard_map/ppermute | solution.py:440
  68.4 1.4 %collective-permute-start.20 = (bf16[32,256]{1,0:T(8,128)(2,1)S(1)}, bf16[32,256]{1,0:T(8,128)(2,1)S(1)}, u32[]{:S(2)}, u32[]{:S(2)}) collective-permute-start(bf16[32,256]{1,0:T(8,128)(2,1)S(1)} %get-tuple-element.66), channel_id=1, source_target_pairs={{0,8},{4,12},{8,0},{12,4},{1,9},{5,13},{9,1},{13,5},{2,10},{6,14},... | collective-permute-start | bytes 49160 | tf_op jit(solution)/shard_map/ppermute | solution.py:440
  69.8 1.4 %collective-permute-start.21 = (bf16[32,256]{1,0:T(8,128)(2,1)S(1)}, bf16[32,256]{1,0:T(8,128)(2,1)S(1)}, u32[]{:S(2)}, u32[]{:S(2)}) collective-permute-start(bf16[32,256]{1,0:T(8,128)(2,1)S(1)} %get-tuple-element.67), channel_id=1, source_target_pairs={{0,12},{4,8},{8,4},{12,0},{1,13},{5,9},{9,5},{13,1},{2,14},{6,10},... | collective-permute-start | bytes 49160 | tf_op jit(solution)/shard_map/ppermute | solution.py:440
  71.2 2.9 %shard_map.110 = (bf16[256,4096]{1,0:T(8,128)(2,1)}, f32[256,256]{1,0:T(8,128)S(1)}) custom-call(bf16[256,512]{1,0:T(8,128)(2,1)S(1)} %copy-done.4, bf16[64,256]{1,0:T(8,128)(2,1)S(1)} %get-tuple-element.42.refs_1_.grad_rank, s32[1,256]{1,0:T(1,128)S(1)} %get-tuple-element.38.deal.refs_2_.refs_1_, ...), custom_call_target="tpu_custom_call", output_to_operand_aliasing={{0}: (13, {})} | custom-call | tf_op jit(solution)/shard_map/pallas_call | solution.py:262
  74.1 0.1 shard_map.115
  74.2 0.1 collective-permute-start.14
  74.3 1.1 %collective-permute-done.19.refs_1_ = bf16[32,256]{1,0:T(8,128)(2,1)S(1)} collective-permute-done((bf16[32,256]{1,0:T(8,128)(2,1)S(1)}, bf16[32,256]{1,0:T(8,128)(2,1)S(1)}, u32[]{:S(2)}, u32[]{:S(2)}) %collective-permute-start.19) | collective-permute-done | bytes 16416 | tf_op jit(solution)/shard_map/ppermute | solution.py:440
  75.4 0.0 collective-permute-done.20.refs_2_
  75.4 0.9 %collective-permute-done.21.refs_3_ = bf16[32,256]{1,0:T(8,128)(2,1)S(1)} collective-permute-done((bf16[32,256]{1,0:T(8,128)(2,1)S(1)}, bf16[32,256]{1,0:T(8,128)(2,1)S(1)}, u32[]{:S(2)}, u32[]{:S(2)}) %collective-permute-start.21) | collective-permute-done | bytes 16416 | tf_op jit(solution)/shard_map/ppermute | solution.py:440
  76.4 0.6 shard_map.121
  77.0 0.8 %shard_map.119 = f32[32,4096]{1,0:T(8,128)} custom-call(f32[32,4096]{1,0:T(8,128)S(1)} %get-tuple-element.61.refs_0_, bf16[32,4096]{1,0:T(8,128)(2,1)S(1)} %collective-permute-done.17.refs_1_), custom_call_target="tpu_custom_call" | custom-call | flops 17250000896 | tf_op jit(solution)/shard_map/pallas_call | solution.py:262
  77.8 0.7 shard_map.116
  (18 shorter events, 0.1 us)
Async XLA Ops:
  0.6 6.4 %copy-start.7 = (s32[256,1]{0,1:T(1,128)S(1)}, s32[256,1]{0,1:T(1,128)}, u32[]{:S(2)}) copy-start(s32[256,1]{0,1:T(1,128)} %param.12) | copy-start | bytes 3076
  0.6 6.5 %collective-permute-start = (bf16[64,256]{1,0:T(8,128)(2,1)}, bf16[64,256]{1,0:T(8,128)(2,1)S(1)}, u32[]{:S(2)}, u32[]{:S(2)}) collective-permute-start(bf16[64,256]{1,0:T(8,128)(2,1)} %bitcast.11), channel_id=1, source_target_pairs={{0,4},{4,0},{8,12},{12,8},{1,5},{5,1},{9,13},{13,9},{2,6},{6,2},{1... | collective-permute-start | bytes 98312 | tf_op jit(solution)/shard_map/ppermute | solution.py:335
  3.7 1.6 %copy-start.1 = (bf16[4096,256]{1,0:T(8,128)(2,1)S(1)}, bf16[4096,256]{1,0:T(8,128)(2,1)}, u32[]{:S(2)}) copy-start(bf16[4096,256]{1,0:T(8,128)(2,1)} %refs_12_.1) | copy-start | bytes 6291460
  5.3 1.7 %copy-start.4 = (bf16[256,512]{1,0:T(8,128)(2,1)S(1)}, bf16[256,512]{1,0:T(8,128)(2,1)}, u32[]{:S(2)}) copy-start(bf16[256,512]{1,0:T(8,128)(2,1)} %refs_0_.6) | copy-start | bytes 786436
  5.3 1.7 %copy-start.6 = (bf16[4,16,256]{2,1,0:T(8,128)(2,1)S(1)}, bf16[4,16,256]{2,1,0:T(8,128)(2,1)}, u32[]{:S(2)}) copy-start(bf16[4,16,256]{2,1,0:T(8,128)(2,1)} %param.11) | copy-start | bytes 98308
  5.3 1.7 %copy-start.8 = (s32[256]{0:T(256)S(1)}, s32[256]{0:T(256)}, u32[]{:S(2)}) copy-start(s32[256]{0:T(256)} %param.13) | copy-start | bytes 3076
  5.4 13.4 %collective-permute-start.3 = (bf16[1024,256]{1,0:T(8,128)(2,1)S(1)}, bf16[1024,256]{1,0:T(8,128)(2,1)S(1)}, u32[]{:S(2)}, u32[]{:S(2)}) collective-permute-start(bf16[1024,256]{1,0:T(8,128)(2,1)S(1)} %get-tuple-element.40), channel_id=1, source_target_pairs={{0,2},{2,0},{1,3},{3,1},{4,6},{6,4},{5,7},{7,5},{8,10},{10,8},{9,1... | collective-permute-start | bytes 1572872 | tf_op jit(solution)/shard_map/ppermute | solution.py:352
  7.1 5.9 %collective-permute-start.1 = (bf16[128,256]{1,0:T(8,128)(2,1)S(1)}, bf16[128,256]{1,0:T(8,128)(2,1)S(1)}, u32[]{:S(2)}, u32[]{:S(2)}) collective-permute-start(bf16[128,256]{1,0:T(8,128)(2,1)S(1)} %shard_map.103.near), channel_id=1, source_target_pairs={{0,8},{4,12},{8,0},{12,4},{1,9},{5,13},{9,1},{13,5},{2,10},{6,14},... | collective-permute-start | bytes 196616 | tf_op jit(solution)/shard_map/ppermute | solution.py:343
  13.1 1.0 %copy-start.3 = (bf16[4,16,4096]{2,1,0:T(8,128)(2,1)S(1)}, bf16[4,16,4096]{2,1,0:T(8,128)(2,1)}, u32[]{:S(2)}) copy-start(bf16[4,16,4096]{2,1,0:T(8,128)(2,1)} %param.10) | copy-start | bytes 1572868
  13.1 5.8 %copy-start = (bf16[256,4096]{1,0:T(8,128)(2,1)S(1)}, bf16[256,4096]{1,0:T(8,128)(2,1)}, u32[]{:S(2)}) copy-start(bf16[256,4096]{1,0:T(8,128)(2,1)} %refs_4_.1) | copy-start | bytes 6291460
  13.4 5.3 %collective-permute-start.2 = (f32[64,256]{1,0:T(8,128)S(1)}, f32[64,256]{1,0:T(8,128)S(1)}, u32[]{:S(2)}, u32[]{:S(2)}) collective-permute-start(f32[64,256]{1,0:T(8,128)S(1)} %shard_map.104.refs_0_), channel_id=1, source_target_pairs={{0,1},{1,0},{2,3},{3,2},{4,5},{5,4},{6,7},{7,6},{8,9},{9,8},{10,11... | collective-permute-start | bytes 196616 | tf_op jit(solution)/shard_map/ppermute | solution.py:358
  14.1 7.3 %copy-start.2 = (bf16[4096,256]{1,0:T(8,128)(2,1)S(1)}, bf16[4096,256]{1,0:T(8,128)(2,1)}, u32[]{:S(2)}) copy-start(bf16[4096,256]{1,0:T(8,128)(2,1)} %refs_12_.1) | copy-start | bytes 6291460
  14.1 10.5 %collective-permute-start.6 = (bf16[64,4096]{1,0:T(8,128)(2,1)S(1)}, bf16[64,4096]{1,0:T(8,128)(2,1)S(1)}, u32[]{:S(2)}, u32[]{:S(2)}) collective-permute-start(bf16[64,4096]{1,0:T(8,128)(2,1)S(1)} %bitcast.6), channel_id=1, source_target_pairs={{4,8},{8,4},{5,9},{9,5},{6,10},{10,6},{7,11},{11,7},{20,24},{24,20... | collective-permute-start | bytes 1572872 | tf_op jit(solution)/shard_map/ppermute | solution.py:365
  14.9 15.4 %collective-permute-start.5 = (bf16[64,4096]{1,0:T(8,128)(2,1)S(1)}, bf16[64,4096]{1,0:T(8,128)(2,1)S(1)}, u32[]{:S(2)}, u32[]{:S(2)}) collective-permute-start(bf16[64,4096]{1,0:T(8,128)(2,1)S(1)} %bitcast.7), channel_id=1, source_target_pairs={{0,4},{4,0},{8,12},{12,8},{1,5},{5,1},{9,13},{13,9},{2,6},{6,2},{1... | collective-permute-start | bytes 1572872 | tf_op jit(solution)/shard_map/ppermute | solution.py:364
  19.9 13.0 %collective-permute-start.7 = (bf16[64,4096]{1,0:T(8,128)(2,1)S(1)}, bf16[64,4096]{1,0:T(8,128)(2,1)S(1)}, u32[]{:S(2)}, u32[]{:S(2)}) collective-permute-start(bf16[64,4096]{1,0:T(8,128)(2,1)S(1)} %get-tuple-element.41.refs_2_), channel_id=1, source_target_pairs={{0,2},{2,0},{1,3},{3,1},{4,6},{6,4},{5,7},{7,5},{8,10},{10,8},{9,1... | collective-permute-start | bytes 1572872 | tf_op jit(solution)/shard_map/ppermute | solution.py:366
  23.0 24.4 %collective-permute-start.4 = (bf16[1024,256]{1,0:T(8,128)(2,1)S(1)}, bf16[1024,256]{1,0:T(8,128)(2,1)S(1)}, u32[]{:S(2)}, u32[]{:S(2)}) collective-permute-start(bf16[1024,256]{1,0:T(8,128)(2,1)S(1)} %collective-permute-done.3.refs_4_.direct), channel_id=1, source_target_pairs={{0,16},{16,0},{1,17},{17,1},{2,18},{18,2},{3,19},{19,3},{4,20},{20... | collective-permute-start | bytes 1572872 | tf_op jit(solution)/shard_map/ppermute | solution.py:376
  30.3 7.6 %collective-permute-start.9 = (bf16[64,4096]{1,0:T(8,128)(2,1)S(1)}, bf16[64,4096]{1,0:T(8,128)(2,1)S(1)}, u32[]{:S(2)}, u32[]{:S(2)}) collective-permute-start(bf16[64,4096]{1,0:T(8,128)(2,1)S(1)} %collective-permute-done.5.refs_6_.refs_1_.refs_4_), channel_id=1, source_target_pairs={{4,8},{8,4},{5,9},{9,5},{6,10},{10,6},{7,11},{11,7},{20,24},{24,20... | collective-permute-start | bytes 1572872 | tf_op jit(solution)/shard_map/ppermute | solution.py:383
  32.8 12.1 %collective-permute-start.11 = (bf16[1024,256]{1,0:T(8,128)(2,1)S(1)}, bf16[1024,256]{1,0:T(8,128)(2,1)S(1)}, u32[]{:S(2)}, u32[]{:S(2)}) collective-permute-start(bf16[1024,256]{1,0:T(8,128)(2,1)S(1)} %get-tuple-element.51), channel_id=1, source_target_pairs={{0,2},{2,0},{1,3},{3,1},{4,6},{6,4},{5,7},{7,5},{8,10},{10,8},{9,1... | collective-permute-start | bytes 1572872 | tf_op jit(solution)/shard_map/ppermute | solution.py:381
  34.8 12.7 %collective-permute-start.8 = (bf16[64,4096]{1,0:T(8,128)(2,1)S(1)}, bf16[64,4096]{1,0:T(8,128)(2,1)S(1)}, u32[]{:S(2)}, u32[]{:S(2)}) collective-permute-start(bf16[64,4096]{1,0:T(8,128)(2,1)S(1)} %get-tuple-element.45), channel_id=1, source_target_pairs={{0,4},{4,0},{8,12},{12,8},{1,5},{5,1},{9,13},{13,9},{2,6},{6,2},{1... | collective-permute-start | bytes 1572872 | tf_op jit(solution)/shard_map/ppermute | solution.py:382
  37.9 19.8 %collective-permute-start.10 = (bf16[64,4096]{1,0:T(8,128)(2,1)S(1)}, bf16[64,4096]{1,0:T(8,128)(2,1)S(1)}, u32[]{:S(2)}, u32[]{:S(2)}) collective-permute-start(bf16[64,4096]{1,0:T(8,128)(2,1)S(1)} %collective-permute-done.9.refs_4_.refs_9_.refs_3_), channel_id=1, source_target_pairs={{4,0},{8,12},{5,1},{9,13},{6,2},{10,14},{7,3},{11,15},{20,16},{24,... | collective-permute-start | bytes 1572872 | tf_op jit(solution)/shard_map/ppermute | solution.py:395
  44.9 18.6 %collective-permute-start.15 = (bf16[64,4096]{1,0:T(8,128)(2,1)S(1)}, bf16[64,4096]{1,0:T(8,128)(2,1)S(1)}, u32[]{:S(2)}, u32[]{:S(2)}) collective-permute-start(bf16[64,4096]{1,0:T(8,128)(2,1)S(1)} %get-tuple-element.59), channel_id=1, source_target_pairs={{0,2},{2,0},{1,3},{3,1},{4,6},{6,4},{5,7},{7,5},{8,10},{10,8},{9,1... | collective-permute-start | bytes 1572872 | tf_op jit(solution)/shard_map/ppermute | solution.py:393
  45.9 17.6 %collective-permute-start.12 = (bf16[1024,256]{1,0:T(8,128)(2,1)S(1)}, bf16[1024,256]{1,0:T(8,128)(2,1)S(1)}, u32[]{:S(2)}, u32[]{:S(2)}) collective-permute-start(bf16[1024,256]{1,0:T(8,128)(2,1)S(1)} %collective-permute-done.11.refs_3_.refs_2_), channel_id=1, source_target_pairs={{0,16},{16,0},{1,17},{17,1},{2,18},{18,2},{3,19},{19,3},{4,20},{20... | collective-permute-start | bytes 1572872 | tf_op jit(solution)/shard_map/ppermute | solution.py:396
  47.5 16.0 %collective-permute-start.16 = (bf16[64,4096]{1,0:T(8,128)(2,1)S(1)}, bf16[64,4096]{1,0:T(8,128)(2,1)S(1)}, u32[]{:S(2)}, u32[]{:S(2)}) collective-permute-start(bf16[64,4096]{1,0:T(8,128)(2,1)S(1)} %shard_map.117), channel_id=1, source_target_pairs={{4,8},{8,4},{5,9},{9,5},{6,10},{10,6},{7,11},{11,7},{20,24},{24,20... | collective-permute-start | bytes 1572872 | tf_op jit(solution)/shard_map/ppermute | solution.py:394
  58.9 3.0 %collective-permute-start.13 = (f32[64,256]{1,0:T(8,128)S(1)}, f32[64,256]{1,0:T(8,128)S(1)}, u32[]{:S(2)}, u32[]{:S(2)}) collective-permute-start(f32[64,256]{1,0:T(8,128)S(1)} %shard_map.113.low), channel_id=1, source_target_pairs={{0,1},{1,0},{2,3},{3,2},{4,5},{5,4},{6,7},{7,6},{8,9},{9,8},{10,11... | collective-permute-start | bytes 196616 | tf_op jit(solution)/shard_map/ppermute | solution.py:400
  62.2 4.5 %collective-permute-start.18 = (bf16[128,256]{1,0:T(8,128)(2,1)S(1)}, bf16[128,256]{1,0:T(8,128)(2,1)S(1)}, u32[]{:S(2)}, u32[]{:S(2)}) collective-permute-start(bf16[128,256]{1,0:T(8,128)(2,1)S(1)} %get-tuple-element.60.refs_5_), channel_id=1, source_target_pairs={{0,2},{2,0},{1,3},{3,1},{4,6},{6,4},{5,7},{7,5},{8,10},{10,8},{9,1... | collective-permute-start | bytes 196616 | tf_op jit(solution)/shard_map/ppermute | solution.py:435
  63.5 1.6 %copy-start.5 = (bf16[256,4096]{1,0:T(8,128)(2,1)S(1)}, bf16[256,4096]{1,0:T(8,128)(2,1)}, u32[]{:S(2)}) copy-start(bf16[256,4096]{1,0:T(8,128)(2,1)} %get-tuple-element.52.refs_13_.refs_6_) | copy-start | bytes 6291460
  66.3 10.7 %collective-permute-start.17 = (bf16[32,4096]{1,0:T(8,128)(2,1)S(1)}, bf16[32,4096]{1,0:T(8,128)(2,1)S(1)}, u32[]{:S(2)}, u32[]{:S(2)}) collective-permute-start(bf16[32,4096]{1,0:T(8,128)(2,1)S(1)} %get-tuple-element.62), channel_id=1, source_target_pairs={{0,4},{4,0},{8,12},{12,8},{1,5},{5,1},{9,13},{13,9},{2,6},{6,2},{1... | collective-permute-start | bytes 786440 | tf_op jit(solution)/shard_map/ppermute | solution.py:434
  66.8 8.7 %collective-permute-start.19 = (bf16[32,256]{1,0:T(8,128)(2,1)S(1)}, bf16[32,256]{1,0:T(8,128)(2,1)S(1)}, u32[]{:S(2)}, u32[]{:S(2)}) collective-permute-start(bf16[32,256]{1,0:T(8,128)(2,1)S(1)} %get-tuple-element.65), channel_id=1, source_target_pairs={{0,4},{4,0},{8,12},{12,8},{1,5},{5,1},{9,13},{13,9},{2,6},{6,2},{1... | collective-permute-start | bytes 49160 | tf_op jit(solution)/shard_map/ppermute | solution.py:440
  68.4 7.0 %collective-permute-start.20 = (bf16[32,256]{1,0:T(8,128)(2,1)S(1)}, bf16[32,256]{1,0:T(8,128)(2,1)S(1)}, u32[]{:S(2)}, u32[]{:S(2)}) collective-permute-start(bf16[32,256]{1,0:T(8,128)(2,1)S(1)} %get-tuple-element.66), channel_id=1, source_target_pairs={{0,8},{4,12},{8,0},{12,4},{1,9},{5,13},{9,1},{13,5},{2,10},{6,14},... | collective-permute-start | bytes 49160 | tf_op jit(solution)/shard_map/ppermute | solution.py:440
  69.8 6.6 %collective-permute-start.21 = (bf16[32,256]{1,0:T(8,128)(2,1)S(1)}, bf16[32,256]{1,0:T(8,128)(2,1)S(1)}, u32[]{:S(2)}, u32[]{:S(2)}) collective-permute-start(bf16[32,256]{1,0:T(8,128)(2,1)S(1)} %get-tuple-element.67), channel_id=1, source_target_pairs={{0,12},{4,8},{8,4},{12,0},{1,13},{5,9},{9,5},{13,1},{2,14},{6,10},... | collective-permute-start | bytes 49160 | tf_op jit(solution)/shard_map/ppermute | solution.py:440
  74.2 3.6 %collective-permute-start.14 = (f32[256,256]{1,0:T(8,128)S(1)}, f32[256,256]{1,0:T(8,128)S(1)}, u32[]{:S(2)}, u32[]{:S(2)}) collective-permute-start(f32[256,256]{1,0:T(8,128)S(1)} %get-tuple-element.56.refs_4_), channel_id=1, source_target_pairs={{0,1},{1,0},{2,3},{3,2},{4,5},{5,4},{6,7},{7,6},{8,9},{9,8},{10,11... | collective-permute-start | bytes 786440 | tf_op jit(solution)/shard_map/ppermute | solution.py:444

commit v4 on v3

--- a/solution.py
+++ b/solution.py
@@ -50,7 +50,7 @@
     return lax.broadcasted_iota(jnp.int32, (span, job_row.shape[1]), 0) // rank == job_row
 
 
-def prepare_kernel(gradient, deal, job, up, *refs):
+def prepare_kernel(gradient, deal, job, up, down, *refs):
     features = up.shape[1]
     start = pl.multiple_of(lax.axis_index("tp") * features, features)
     sources = gradient.at[:, pl.ds(start, features)], deal, job, up
@@ -131,20 +131,21 @@
         swap_out[:, at] = jnp.where(in_middle(), down_cross[:, at], made)
 
 
-def near_kernel(rank, got, grad_rank, deal, cross, tokens, next_out, mine_out, held, sems):
-    copies = [
-        pltpu.make_async_copy(tokens.at[:, at], held.at[:, at], sems.at[k])
-        for k, at in enumerate(pl.ds(k * COLUMNS, COLUMNS) for k in range(tokens.shape[1] // COLUMNS))
-    ]
-    for copy in copies:
-        copy.start()
+def near_kept_kernel(rank, grad_rank, deal, tokens, out):
     mine, beside, _, _ = holders()
     wide = wide_rows(kept_rows(rank, grad_rank), deal[...], (beside, mine))
+
+    @each_column(tokens)
+    def _(at):
+        out[:, at] = dot(wide, tokens[:, at])
+
+
+def near_kernel(kept, got, cross, next_out, mine_out):
     split = next_out.shape[0]
-    for k, copy in enumerate(copies):
-        at = pl.ds(k * COLUMNS, COLUMNS)
-        copy.wait()
-        made = dot(wide, held[:, at]) + got[:, at].astype(F32) + cross[:, at].astype(F32)
+
+    @each_column(kept)
+    def _(at):
+        made = kept[:, at] + got[:, at].astype(F32) + cross[:, at].astype(F32)
         next_out[:, at] = made[:split].astype(BF16)
         mine_out[:, at] = made[split:]
 
@@ -304,6 +305,12 @@
     refs[-1][...] = total.astype(refs[-1].dtype)
 
 
+def finish_kernel(base_keep, base_got, mine, last, up_mine, one, two, three, value_out, down_out, up_out):
+    total_kernel(base_keep, base_got, value_out)
+    total_kernel(up_mine, one, two, three, up_out)
+    down_out[...] = mine[...] + last[...].astype(F32)
+
+
 def add_kernel(one, two, out):
     out[...] = (one[...].astype(F32) + two[...].astype(F32)).astype(BF16)
 
@@ -336,8 +343,8 @@
     row = struct((1, rows), jnp.int32)
     grad_mine, deal, job, up = call(
         prepare_kernel, (struct((rows, features), BF16), row, row, struct((span, features), BF16)),
-        output_gradient, deal, job, up,
-        in_specs=[ANY] * 4, scratch_shapes=[pltpu.SemaphoreType.DMA((4,))],
+        output_gradient, deal, job, up, down,
+        in_specs=[ANY] * 4 + [WHOLE], scratch_shapes=[pltpu.SemaphoreType.DMA((4,))],
     )
     up_pair = call(join_kernel, struct((2 * span, features), BF16), up, up_got_first, after=(grad_mine,))
     ups = up_pair, lax.ppermute(up_pair, "dp", swap(4, 2))
@@ -374,9 +381,12 @@
         scratch_shapes=[pltpu.VMEM((width, features), BF16), pltpu.SemaphoreType.DMA((OWN_PARTS,))],
     )
     relay_first = lax.ppermute(ordered(got_first, own_out), "rep", swap(2))
+    near_kept = call(
+        functools.partial(near_kept_kernel, rank), struct((span, width), F32), grad_rank, deal, tokens
+    )
     far, far_swap = call(
         functools.partial(far_kernel, rank), (span_wide, span_wide),
-        got_far, grad_rank, deal, tokens, down_cross, after=(own_out, down_next), us=FAR_US,
+        got_far, grad_rank, deal, tokens, down_cross, after=(own_out, down_next, near_kept), us=FAR_US,
     )
     got_second = lax.ppermute(ordered(weight_second, got_far), "fsdp", swap(2))
     swapped = lax.ppermute(far_swap, "dp", swap(4))
@@ -389,11 +399,11 @@
         functools.partial(low_kernel, rank, (2,), (2,)),
         narrow, tokens, deal, job, down_cross, swapped, low_near,
     )
-    far_sum = call(add_kernel, span_wide, far, swapped, after=(got_second, down_cross2, relay_first, low_near), us=SUM_US)
-    got_near = lax.ppermute(ordered(send_near, got_second), "fsdp", swap(2))
+    far_sum = call(add_kernel, span_wide, far, swapped, after=(down_cross2, low_near,), us=SUM_US)
+    got_near = lax.ppermute(ordered(send_near, far), "fsdp", swap(2))
     cross = lax.ppermute(far_sum, "dp", middle)
     down_out2 = lax.ppermute(ordered(down_cross2, far), "dp", outward)
-    relay_second = lax.ppermute(got_second, "rep", swap(2))
+    relay_second = lax.ppermute(ordered(got_second, far_sum), "rep", swap(2))
     low_part = call(
         functools.partial(low_kernel, rank, (3,), (2,)), narrow, tokens, deal, job, down_cross2, down_out2, low_first, after=()
     )
@@ -425,11 +435,10 @@
         )
 
     input_first, other_first = base(0, got_first, relay_first)
+    input_gradient, other_second = base(first_rows, got_second, relay_second, input_first)
     next_sum, mine_sum = call(
-        functools.partial(near_kernel, rank), (half_wide, struct((half, width), F32)),
-        got_near, grad_rank, deal, cross, tokens, after=(up_away, input_first, relay_second), us=NEAR_US,
-        in_specs=[WHOLE] * 4 + [HBM],
-        scratch_shapes=[pltpu.VMEM((rows, width), BF16), pltpu.SemaphoreType.DMA((width // COLUMNS,))],
+        near_kernel, (half_wide, struct((half, width), F32)),
+        near_kept, got_near, cross, after=(up_away, other_first, relay_second), us=NEAR_US,
     )
     last = lax.ppermute(next_sum, "dp", swap(4))
     up_got = lax.ppermute(up_away, "fsdp", swap(2))
@@ -439,12 +448,13 @@
     )
     up_last = [lax.ppermute(sent, "dp", swap(4, k + 1)) for k, sent in enumerate(up_sent)]
 
-    input_gradient, other_second = base(first_rows, got_second, relay_second, input_first)
     base_send, base_keep = call(share_kernel, (struct((rows, features), F32),) * 2, own_out, other_first, other_second, lora)
     base_got = lax.ppermute(base_send, "tp", swap(2))
-    value_output = call(total_kernel, struct((rows, features), BF16), base_keep, base_got)
-    up_share = call(total_kernel, struct((half, features), F32), up_mine, *up_last, after=(base_send,))
-    down_share = call(total_kernel, struct((half, width), F32), mine_sum, last, us=LAST_US)
+    value_output, down_share, up_share = call(
+        finish_kernel,
+        (struct((rows, features), BF16), struct((half, width), F32), struct((half, features), F32)),
+        base_keep, base_got, mine_sum, last, up_mine, *up_last, us=LAST_US,
+    )
     shares = [share.reshape(jobs, rank // 2, share.shape[1]) for share in (down_share, up_share)]
     return value_output, input_gradient, *shares
 

time: 78.8 us -> 76.5 us (0.971)
  local copies, waits for them, and re-layouts: 3.88 us -> 1.62 us
  waiting for transfers between devices: 27.5 us -> 29.7 us
  Pallas kernels: 17.6 us -> 16.3 us
  starting transfers between devices: 28.7 us -> 27.7 us
    ppermute x1, waiting for transfers between devices: 0.01 us -> 4.58 us  [gather_adapters(): swapped = lax.ppermute(far_swap, 'dp', swap(4))]
    ppermute x1, waiting for transfers between devices: 8.31 us -> 4.41 us  [gather_adapters(): down_out2 = lax.ppermute(ordered(down_cross2, far), 'dp', outward)]
    unnamed x18 -> x16, local copies, waits for them, and re-layouts: 3.88 us -> 1.62 us
    ppermute x3, waiting for transfers between devices: 2.07 us -> 3.51 us  [gather_adapters(): lax.ppermute(sent, 'dp', swap(4, k + 1))]
    pallas_call x20 -> x19, Pallas kernels: 17.6 us -> 16.3 us  [call(): pl.pallas_call(kernel, out_shape=out_shape, in_specs=(in_specs or [WHOLE]...]
    ppermute x2, starting transfers between devices: 2.51 us -> 1.55 us  [the longest x1 1.04 us: gather_adapters(): got_near = lax.ppermute(ordered(send_near, far), 'fsdp', swap(2))]
  transfers between devices with their start and end apart: 22 -> 22, of which waited for: 9 -> 10; matrix products, arithmetic and copies ran while one was open for 0% -> 0% of each run, Pallas kernels for 22% -> 20%
where the time goes in v4:
time: 76.5 us; the launch traced here: 76.2 us
  waiting for transfers between devices  29.7 us (39%)
  starting transfers between devices  27.7 us (36%)
  Pallas kernels  16.3 us (21%)
  local copies, waits for them, and re-layouts  1.62 us (2%)
  between operations  0.9 us (1%)
    pallas_call x19, Pallas kernels, call(): pl.pallas_call(kernel, out_shape=out_shape, in_specs=(in_specs or [WHOLE]...  16.3 us
    ppermute x1, waiting for transfers between devices, gather_adapters(): down_next = lax.ppermute(down_sent, 'dp', swap(4))  6.26 us
    ppermute x1, waiting for transfers between devices, gather_adapters(): got_second = lax.ppermute(ordered(weight_second, got_far), 'fsdp', swap(2))  5.04 us
    ppermute x1, waiting for transfers between devices, gather_adapters(): swapped = lax.ppermute(far_swap, 'dp', swap(4))  4.58 us
    ppermute x3, starting transfers between devices, gather_adapters(): lax.ppermute(sent, 'dp', swap(4, k + 1))  4.47 us
    ppermute x1, waiting for transfers between devices, gather_adapters(): down_out2 = lax.ppermute(ordered(down_cross2, far), 'dp', outward)  4.41 us
    ppermute x1, starting transfers between devices, gather_adapters(): down_next = lax.ppermute(down_sent, 'dp', swap(4))  3.86 us
    ppermute x3, waiting for transfers between devices, gather_adapters(): lax.ppermute(sent, 'dp', swap(4, k + 1))  3.51 us
  transfers between devices with their start and end apart: 22, of which 10 were waited for; matrix products, arithmetic and copies ran while one was open for 0% of the time, Pallas kernels for 20%

profile of v4, /device:TPU:0, one launch (start us, length us, event | category | flops | bytes accessed | tf_op | source)
XLA Modules:
  0.0 76.2 jit_solution(8220629335675568300)
XLA Ops:
  0.6 0.0 copy-start.6
  0.6 3.1 %collective-permute-start = (bf16[64,256]{1,0:T(8,128)(2,1)}, bf16[64,256]{1,0:T(8,128)(2,1)S(1)}, u32[]{:S(2)}, u32[]{:S(2)}) collective-permute-start(bf16[64,256]{1,0:T(8,128)(2,1)} %bitcast.12), channel_id=1, source_target_pairs={{0,4},{4,0},{8,12},{12,8},{1,5},{5,1},{9,13},{13,9},{2,6},{6,2},{1... | collective-permute-start | bytes 98312 | tf_op jit(solution)/shard_map/ppermute | solution.py:342
  3.7 1.6 %copy-done.1 = bf16[4096,256]{1,0:T(8,128)(2,1)S(1)} copy-done((bf16[4096,256]{1,0:T(8,128)(2,1)S(1)}, bf16[4096,256]{1,0:T(8,128)(2,1)}, u32[]{:S(2)}) %copy-start.1) | copy-done | bytes 2097176
  5.3 0.1 shard_map.105
  5.4 1.6 %collective-permute-start.3 = (bf16[1024,256]{1,0:T(8,128)(2,1)S(1)}, bf16[1024,256]{1,0:T(8,128)(2,1)S(1)}, u32[]{:S(2)}, u32[]{:S(2)}) collective-permute-start(bf16[1024,256]{1,0:T(8,128)(2,1)S(1)} %get-tuple-element.44), channel_id=1, source_target_pairs={{0,2},{2,0},{1,3},{3,1},{4,6},{6,4},{5,7},{7,5},{8,10},{10,8},{9,1... | collective-permute-start | bytes 1572872 | tf_op jit(solution)/shard_map/ppermute | solution.py:359
  7.0 0.1 shard_map.102
  7.1 0.0 collective-permute-done.refs_1_
  7.2 2.7 %collective-permute-start.1 = (bf16[128,256]{1,0:T(8,128)(2,1)S(1)}, bf16[128,256]{1,0:T(8,128)(2,1)S(1)}, u32[]{:S(2)}, u32[]{:S(2)}) collective-permute-start(bf16[128,256]{1,0:T(8,128)(2,1)S(1)} %shard_map.103.near), channel_id=1, source_target_pairs={{0,8},{4,12},{8,0},{12,4},{1,9},{5,13},{9,1},{13,5},{2,10},{6,14},... | collective-permute-start | bytes 196616 | tf_op jit(solution)/shard_map/ppermute | solution.py:350
  9.8 3.3 %collective-permute-done.1.far = bf16[128,256]{1,0:T(8,128)(2,1)S(1)} collective-permute-done((bf16[128,256]{1,0:T(8,128)(2,1)S(1)}, bf16[128,256]{1,0:T(8,128)(2,1)S(1)}, u32[]{:S(2)}, u32[]{:S(2)}) %collective-permute-start.1) | collective-permute-done | bytes 65568 | tf_op jit(solution)/shard_map/ppermute | solution.py:350
  13.1 0.3 shard_map.104.refs_0_
  13.4 0.0 copy-start.2
  13.4 0.1 collective-permute-start.2
  13.5 0.8 %collective-permute-start.6 = (bf16[64,4096]{1,0:T(8,128)(2,1)S(1)}, bf16[64,4096]{1,0:T(8,128)(2,1)S(1)}, u32[]{:S(2)}, u32[]{:S(2)}) collective-permute-start(bf16[64,4096]{1,0:T(8,128)(2,1)S(1)} %bitcast.7), channel_id=1, source_target_pairs={{4,8},{8,4},{5,9},{9,5},{6,10},{10,6},{7,11},{11,7},{20,24},{24,20... | collective-permute-start | bytes 1572872 | tf_op jit(solution)/shard_map/ppermute | solution.py:372
  14.3 3.9 %collective-permute-start.5 = (bf16[64,4096]{1,0:T(8,128)(2,1)S(1)}, bf16[64,4096]{1,0:T(8,128)(2,1)S(1)}, u32[]{:S(2)}, u32[]{:S(2)}) collective-permute-start(bf16[64,4096]{1,0:T(8,128)(2,1)S(1)} %bitcast.8), channel_id=1, source_target_pairs={{0,4},{4,0},{8,12},{12,8},{1,5},{5,1},{9,13},{13,9},{2,6},{6,2},{1... | collective-permute-start | bytes 1572872 | tf_op jit(solution)/shard_map/ppermute | solution.py:371
  18.2 0.0 collective-permute-done.2.refs_1_
  18.2 0.7 collective-permute-done.3.refs_4_.direct
  18.9 1.0 %shard_map.106 = (bf16[64,256]{1,0:T(8,128)(2,1)S(1)}, bf16[64,4096]{1,0:T(8,128)(2,1)S(1)}, bf16[64,4096]{1,0:T(8,128)(2,1)S(1)}) custom-call(f32[64,256]{1,0:T(8,128)S(1)} %shard_map.104.refs_0_, f32[64,256]{1,0:T(8,128)S(1)} %collective-permute-done.2.refs_1_, s32[1,256]{1,0:T(1,128)S(1)} %get-tuple-element.42.deal.refs_2_.refs_1_, ...), custom_call_target="tpu_custom_call" | custom-call | flops 6899999744 | tf_op jit(solution)/shard_map/pallas_call | solution.py:263
  19.9 1.6 %collective-permute-start.7 = (bf16[64,4096]{1,0:T(8,128)(2,1)S(1)}, bf16[64,4096]{1,0:T(8,128)(2,1)S(1)}, u32[]{:S(2)}, u32[]{:S(2)}) collective-permute-start(bf16[64,4096]{1,0:T(8,128)(2,1)S(1)} %get-tuple-element.45.refs_2_), channel_id=1, source_target_pairs={{0,2},{2,0},{1,3},{3,1},{4,6},{6,4},{5,7},{7,5},{8,10},{10,8},{9,1... | collective-permute-start | bytes 1572872 | tf_op jit(solution)/shard_map/ppermute | solution.py:373
  21.4 1.6 %shard_map.107.refs_5_.own = f32[256,256]{1,0:T(8,128)S(1)} custom-call(bf16[256,4096]{1,0:T(8,128)(2,1)S(1)} %copy-done, bf16[4096,256]{1,0:T(8,128)(2,1)S(1)} %copy-done.2, bf16[64,4096]{1,0:T(8,128)(2,1)S(1)} %get-tuple-element.45.refs_2_), custom_call_target="tpu_custom_call" | custom-call | tf_op jit(solution)/shard_map/pallas_call | solution.py:263
  23.1 0.9 %shard_map.108.refs_7_.refs_0_ = f32[64,4096]{1,0:T(8,128)S(1)} custom-call(bf16[64,256]{1,0:T(8,128)(2,1)S(1)} %get-tuple-element.46.grad_rank.refs_1_, s32[1,256]{1,0:T(1,128)S(1)} %get-tuple-element.42.deal.refs_2_.refs_1_, bf16[256,4096]{1,0:T(8,128)(2,1)S(1)} %copy-done), custom_call_target="tpu_custom_call" | custom-call | tf_op jit(solution)/shard_map/pallas_call | solution.py:263
  23.9 0.0 collective-permute-done.6.refs_4_.refs_2_.refs_7_.refs_3_
  23.9 6.3 %collective-permute-done.5.refs_6_.refs_1_.refs_4_ = bf16[64,4096]{1,0:T(8,128)(2,1)S(1)} collective-permute-done((bf16[64,4096]{1,0:T(8,128)(2,1)S(1)}, bf16[64,4096]{1,0:T(8,128)(2,1)S(1)}, u32[]{:S(2)}, u32[]{:S(2)}) %collective-permute-start.5) | collective-permute-done | bytes 524320 | tf_op jit(solution)/shard_map/ppermute | solution.py:371
  30.2 0.7 collective-permute-start.9
  30.9 1.8 %collective-permute-done.7.refs_0_ = bf16[64,4096]{1,0:T(8,128)(2,1)S(1)} collective-permute-done((bf16[64,4096]{1,0:T(8,128)(2,1)S(1)}, bf16[64,4096]{1,0:T(8,128)(2,1)S(1)}, u32[]{:S(2)}, u32[]{:S(2)}) %collective-permute-start.7) | collective-permute-done | bytes 524320 | tf_op jit(solution)/shard_map/ppermute | solution.py:373
  32.7 0.9 %shard_map.109 = (bf16[64,4096]{1,0:T(8,128)(2,1)S(1)}, bf16[64,4096]{1,0:T(8,128)(2,1)S(1)}) custom-call(bf16[64,4096]{1,0:T(8,128)(2,1)S(1)} %collective-permute-done.7.refs_0_, bf16[64,256]{1,0:T(8,128)(2,1)S(1)} %get-tuple-element.46.grad_rank.refs_1_, s32[1,256]{1,0:T(1,128)S(1)} %get-tuple-element.42.deal.refs_2_.refs_1_, ...), custom_call_target="tpu_custom_call" | custom-call | flops 6899999744 | tf_op jit(solution)/shard_map/pallas_call | solution.py:263
  33.6 1.5 %collective-permute-start.8 = (bf16[64,4096]{1,0:T(8,128)(2,1)S(1)}, bf16[64,4096]{1,0:T(8,128)(2,1)S(1)}, u32[]{:S(2)}, u32[]{:S(2)}) collective-permute-start(bf16[64,4096]{1,0:T(8,128)(2,1)S(1)} %get-tuple-element.49), channel_id=1, source_target_pairs={{0,4},{4,0},{8,12},{12,8},{1,5},{5,1},{9,13},{13,9},{2,6},{6,2},{1... | collective-permute-start | bytes 1572872 | tf_op jit(solution)/shard_map/ppermute | solution.py:392
  35.1 1.5 %collective-permute-start.4 = (bf16[1024,256]{1,0:T(8,128)(2,1)S(1)}, bf16[1024,256]{1,0:T(8,128)(2,1)S(1)}, u32[]{:S(2)}, u32[]{:S(2)}) collective-permute-start(bf16[1024,256]{1,0:T(8,128)(2,1)S(1)} %collective-permute-done.3.refs_4_.direct), channel_id=1, source_target_pairs={{0,16},{16,0},{1,17},{17,1},{2,18},{18,2},{3,19},{19,3},{4,20},{20... | collective-permute-start | bytes 1572872 | tf_op jit(solution)/shard_map/ppermute | solution.py:383
  36.6 1.0 %collective-permute-start.11 = (bf16[1024,256]{1,0:T(8,128)(2,1)S(1)}, bf16[1024,256]{1,0:T(8,128)(2,1)S(1)}, u32[]{:S(2)}, u32[]{:S(2)}) collective-permute-start(bf16[1024,256]{1,0:T(8,128)(2,1)S(1)} %get-tuple-element.55), channel_id=1, source_target_pairs={{0,2},{2,0},{1,3},{3,1},{4,6},{6,4},{5,7},{7,5},{8,10},{10,8},{9,1... | collective-permute-start | bytes 1572872 | tf_op jit(solution)/shard_map/ppermute | solution.py:391
  37.6 1.0 %collective-permute-start.15 = (bf16[64,4096]{1,0:T(8,128)(2,1)S(1)}, bf16[64,4096]{1,0:T(8,128)(2,1)S(1)}, u32[]{:S(2)}, u32[]{:S(2)}) collective-permute-start(bf16[64,4096]{1,0:T(8,128)(2,1)S(1)} %get-tuple-element.63), channel_id=1, source_target_pairs={{0,2},{2,0},{1,3},{3,1},{4,6},{6,4},{5,7},{7,5},{8,10},{10,8},{9,1... | collective-permute-start | bytes 1572872 | tf_op jit(solution)/shard_map/ppermute | solution.py:403
  38.6 1.8 %shard_map.111.refs_3_.refs_5_ = f32[64,256]{1,0:T(8,128)S(1)} custom-call(bf16[256,4096]{1,0:T(8,128)(2,1)S(1)} %copy-done, s32[1,256]{1,0:T(1,128)S(1)} %get-tuple-element.42.deal.refs_2_.refs_1_, s32[1,256]{1,0:T(1,128)S(1)} %get-tuple-element.43.job.refs_2_, bf16[64,4096]{1,0:T(8,128)(2,1)S(1)} %bitcast.9, ...), custom_call_target="tpu_custom_call" | custom-call | tf_op jit(solution)/shard_map/pallas_call | solution.py:263
  40.4 0.0 collective-permute-done.9.refs_4_.refs_2_.refs_9_.refs_3_
  40.4 1.3 %collective-permute-start.10 = (bf16[64,4096]{1,0:T(8,128)(2,1)S(1)}, bf16[64,4096]{1,0:T(8,128)(2,1)S(1)}, u32[]{:S(2)}, u32[]{:S(2)}) collective-permute-start(bf16[64,4096]{1,0:T(8,128)(2,1)S(1)} %collective-permute-done.9.refs_4_.refs_2_.refs_9_.refs_3_), channel_id=1, source_target_pairs={{4,0},{8,12},{5,1},{9,13},{6,2},{10,14},{7,3},{11,15},{20,16},{24,... | collective-permute-start | bytes 1572872 | tf_op jit(solution)/shard_map/ppermute | solution.py:405
  41.7 4.6 %collective-permute-done.8.refs_3_.refs_1_.refs_8_.refs_4_ = bf16[64,4096]{1,0:T(8,128)(2,1)S(1)} collective-permute-done((bf16[64,4096]{1,0:T(8,128)(2,1)S(1)}, bf16[64,4096]{1,0:T(8,128)(2,1)S(1)}, u32[]{:S(2)}, u32[]{:S(2)}) %collective-permute-start.8) | collective-permute-done | bytes 524320 | tf_op jit(solution)/shard_map/ppermute | solution.py:392
  46.3 0.1 shard_map.112
  46.4 5.0 %collective-permute-done.11.refs_3_ = bf16[1024,256]{1,0:T(8,128)(2,1)S(1)} collective-permute-done((bf16[1024,256]{1,0:T(8,128)(2,1)S(1)}, bf16[1024,256]{1,0:T(8,128)(2,1)S(1)}, u32[]{:S(2)}, u32[]{:S(2)}) %collective-permute-start.11) | collective-permute-done | bytes 524320 | tf_op jit(solution)/shard_map/ppermute | solution.py:391
  51.5 0.5 collective-permute-start.12
  52.0 0.7 collective-permute-start.16
  52.7 1.2 %shard_map.114.refs_5_ = f32[64,256]{1,0:T(8,128)S(1)} custom-call(bf16[256,4096]{1,0:T(8,128)(2,1)S(1)} %copy-done, s32[1,256]{1,0:T(1,128)S(1)} %get-tuple-element.42.deal.refs_2_.refs_1_, s32[1,256]{1,0:T(1,128)S(1)} %get-tuple-element.43.job.refs_2_, bf16[64,4096]{1,0:T(8,128)(2,1)S(1)} %collective-permute-done.6.refs_4_.refs_2_.refs_7_.refs_3_, ...), custom_call_target="tpu_custom_call" | custom-call | tf_op jit(solution)/shard_map/pallas_call | solution.py:263
  53.8 4.4 %collective-permute-done.10.refs_5_.refs_10_.refs_4_ = bf16[64,4096]{1,0:T(8,128)(2,1)S(1)} collective-permute-done((bf16[64,4096]{1,0:T(8,128)(2,1)S(1)}, bf16[64,4096]{1,0:T(8,128)(2,1)S(1)}, u32[]{:S(2)}, u32[]{:S(2)}) %collective-permute-start.10) | collective-permute-done | bytes 524320 | tf_op jit(solution)/shard_map/ppermute | solution.py:405
  58.3 1.2 %shard_map.115.low = f32[64,256]{1,0:T(8,128)S(1)} custom-call(bf16[256,4096]{1,0:T(8,128)(2,1)S(1)} %copy-done, s32[1,256]{1,0:T(1,128)S(1)} %get-tuple-element.42.deal.refs_2_.refs_1_, s32[1,256]{1,0:T(1,128)S(1)} %get-tuple-element.43.job.refs_2_, bf16[64,4096]{1,0:T(8,128)(2,1)S(1)} %collective-permute-done.9.refs_4_.refs_2_.refs_9_.refs_3_, ...), custom_call_target="tpu_custom_call" | custom-call | tf_op jit(solution)/shard_map/pallas_call | solution.py:263
  59.4 0.1 collective-permute-start.13
  59.5 0.0 collective-permute-done.4.relayed
  59.5 2.9 %shard_map.110 = (bf16[256,4096]{1,0:T(8,128)(2,1)}, f32[256,256]{1,0:T(8,128)S(1)}) custom-call(bf16[256,512]{1,0:T(8,128)(2,1)S(1)} %copy-done.4, bf16[64,256]{1,0:T(8,128)(2,1)S(1)} %get-tuple-element.46.grad_rank.refs_1_, s32[1,256]{1,0:T(1,128)S(1)} %get-tuple-element.42.deal.refs_2_.refs_1_, ...), custom_call_target="tpu_custom_call" | custom-call | tf_op jit(solution)/shard_map/pallas_call | solution.py:263
  62.4 0.0 collective-permute-done.13.low_got
  62.5 0.3 shard_map.116
  62.7 1.0 %collective-permute-start.18 = (bf16[128,256]{1,0:T(8,128)(2,1)S(1)}, bf16[128,256]{1,0:T(8,128)(2,1)S(1)}, u32[]{:S(2)}, u32[]{:S(2)}) collective-permute-start(bf16[128,256]{1,0:T(8,128)(2,1)S(1)} %get-tuple-element.64.refs_3_), channel_id=1, source_target_pairs={{0,2},{2,0},{1,3},{3,1},{4,6},{6,4},{5,7},{7,5},{8,10},{10,8},{9,1... | collective-permute-start | bytes 196616 | tf_op jit(solution)/shard_map/ppermute | solution.py:444
  63.8 0.0 collective-permute-done.15.refs_1_
  63.8 0.0 collective-permute-done.12.refs_4_.refs_5_
  63.8 0.0 collective-permute-done.16.refs_2_
  63.8 0.2 shard_map.118
  64.0 0.1 collective-permute-start.17
  64.0 2.9 %shard_map.113 = (bf16[256,4096]{1,0:T(8,128)(2,1)}, f32[256,256]{1,0:T(8,128)S(1)}) custom-call(bf16[256,512]{1,0:T(8,128)(2,1)S(1)} %copy-done.4, bf16[64,256]{1,0:T(8,128)(2,1)S(1)} %get-tuple-element.46.grad_rank.refs_1_, s32[1,256]{1,0:T(1,128)S(1)} %get-tuple-element.42.deal.refs_2_.refs_1_, ...), custom_call_target="tpu_custom_call", output_to_operand_aliasing={{0}: (13, {})} | custom-call | tf_op jit(solution)/shard_map/pallas_call | solution.py:263
  67.0 0.1 shard_map.117
  67.1 0.3 collective-permute-start.14
  67.3 0.0 collective-permute-done.18.got
  67.4 1.9 %collective-permute-start.19 = (bf16[32,256]{1,0:T(8,128)(2,1)S(1)}, bf16[32,256]{1,0:T(8,128)(2,1)S(1)}, u32[]{:S(2)}, u32[]{:S(2)}) collective-permute-start(bf16[32,256]{1,0:T(8,128)(2,1)S(1)} %get-tuple-element.69), channel_id=1, source_target_pairs={{0,4},{4,0},{8,12},{12,8},{1,5},{5,1},{9,13},{13,9},{2,6},{6,2},{1... | collective-permute-start | bytes 49160 | tf_op jit(solution)/shard_map/ppermute | solution.py:449
  69.3 0.5 collective-permute-start.20
  69.8 2.0 %collective-permute-start.21 = (bf16[32,256]{1,0:T(8,128)(2,1)S(1)}, bf16[32,256]{1,0:T(8,128)(2,1)S(1)}, u32[]{:S(2)}, u32[]{:S(2)}) collective-permute-start(bf16[32,256]{1,0:T(8,128)(2,1)S(1)} %get-tuple-element.71), channel_id=1, source_target_pairs={{0,12},{4,8},{8,4},{12,0},{1,13},{5,9},{9,5},{13,1},{2,14},{6,10},... | collective-permute-start | bytes 49160 | tf_op jit(solution)/shard_map/ppermute | solution.py:449
  71.8 1.0 %collective-permute-done.19.one = bf16[32,256]{1,0:T(8,128)(2,1)S(1)} collective-permute-done((bf16[32,256]{1,0:T(8,128)(2,1)S(1)}, bf16[32,256]{1,0:T(8,128)(2,1)S(1)}, u32[]{:S(2)}, u32[]{:S(2)}) %collective-permute-start.19) | collective-permute-done | bytes 16416 | tf_op jit(solution)/shard_map/ppermute | solution.py:449
  72.8 1.1 %collective-permute-done.20.two = bf16[32,256]{1,0:T(8,128)(2,1)S(1)} collective-permute-done((bf16[32,256]{1,0:T(8,128)(2,1)S(1)}, bf16[32,256]{1,0:T(8,128)(2,1)S(1)}, u32[]{:S(2)}, u32[]{:S(2)}) %collective-permute-start.20) | collective-permute-done | bytes 16416 | tf_op jit(solution)/shard_map/ppermute | solution.py:449
  73.9 1.4 %collective-permute-done.21.three = bf16[32,256]{1,0:T(8,128)(2,1)S(1)} collective-permute-done((bf16[32,256]{1,0:T(8,128)(2,1)S(1)}, bf16[32,256]{1,0:T(8,128)(2,1)S(1)}, u32[]{:S(2)}, u32[]{:S(2)}) %collective-permute-start.21) | collective-permute-done | bytes 16416 | tf_op jit(solution)/shard_map/ppermute | solution.py:449
  75.3 0.0 collective-permute-done.17.last
  75.3 0.0 collective-permute-done.14.base_got
  75.3 0.9 %shard_map.120 = (bf16[256,256]{1,0:T(8,128)(2,1)}, f32[32,4096]{1,0:T(8,128)}, f32[32,256]{1,0:T(8,128)}) custom-call(f32[256,256]{1,0:T(8,128)S(1)} %get-tuple-element.60.base_keep, f32[256,256]{1,0:T(8,128)S(1)} %collective-permute-done.14.base_got, f32[32,4096]{1,0:T(8,128)S(1)} %get-tuple-element.65.mine, ...), custom_call_target="tpu_custom_call" | custom-call | flops 17250000896 | tf_op jit(solution)/shard_map/pallas_call | solution.py:263
  (15 shorter events, 0.0 us)
Async XLA Ops:
  0.6 6.4 %copy-start.6 = (s32[256,1]{0,1:T(1,128)S(1)}, s32[256,1]{0,1:T(1,128)}, u32[]{:S(2)}) copy-start(s32[256,1]{0,1:T(1,128)} %param.12) | copy-start | bytes 3076
  0.6 6.5 %collective-permute-start = (bf16[64,256]{1,0:T(8,128)(2,1)}, bf16[64,256]{1,0:T(8,128)(2,1)S(1)}, u32[]{:S(2)}, u32[]{:S(2)}) collective-permute-start(bf16[64,256]{1,0:T(8,128)(2,1)} %bitcast.12), channel_id=1, source_target_pairs={{0,4},{4,0},{8,12},{12,8},{1,5},{5,1},{9,13},{13,9},{2,6},{6,2},{1... | collective-permute-start | bytes 98312 | tf_op jit(solution)/shard_map/ppermute | solution.py:342
  3.7 1.6 %copy-start.1 = (bf16[4096,256]{1,0:T(8,128)(2,1)S(1)}, bf16[4096,256]{1,0:T(8,128)(2,1)}, u32[]{:S(2)}) copy-start(bf16[4096,256]{1,0:T(8,128)(2,1)} %refs_12_.1) | copy-start | bytes 6291460
  5.3 1.7 %copy-start.3 = (bf16[4,16,4096]{2,1,0:T(8,128)(2,1)S(1)}, bf16[4,16,4096]{2,1,0:T(8,128)(2,1)}, u32[]{:S(2)}) copy-start(bf16[4,16,4096]{2,1,0:T(8,128)(2,1)} %param.10) | copy-start | bytes 1572868
  5.3 1.7 %copy-start.4 = (bf16[256,512]{1,0:T(8,128)(2,1)S(1)}, bf16[256,512]{1,0:T(8,128)(2,1)}, u32[]{:S(2)}) copy-start(bf16[256,512]{1,0:T(8,128)(2,1)} %refs_0_.7) | copy-start | bytes 786436
  5.3 1.7 %copy-start.5 = (bf16[4,16,256]{2,1,0:T(8,128)(2,1)S(1)}, bf16[4,16,256]{2,1,0:T(8,128)(2,1)}, u32[]{:S(2)}) copy-start(bf16[4,16,256]{2,1,0:T(8,128)(2,1)} %param.11) | copy-start | bytes 98308
  5.3 1.7 %copy-start.7 = (s32[256]{0:T(256)S(1)}, s32[256]{0:T(256)}, u32[]{:S(2)}) copy-start(s32[256]{0:T(256)} %param.13) | copy-start | bytes 3076
  5.4 13.4 %collective-permute-start.3 = (bf16[1024,256]{1,0:T(8,128)(2,1)S(1)}, bf16[1024,256]{1,0:T(8,128)(2,1)S(1)}, u32[]{:S(2)}, u32[]{:S(2)}) collective-permute-start(bf16[1024,256]{1,0:T(8,128)(2,1)S(1)} %get-tuple-element.44), channel_id=1, source_target_pairs={{0,2},{2,0},{1,3},{3,1},{4,6},{6,4},{5,7},{7,5},{8,10},{10,8},{9,1... | collective-permute-start | bytes 1572872 | tf_op jit(solution)/shard_map/ppermute | solution.py:359
  7.2 5.9 %collective-permute-start.1 = (bf16[128,256]{1,0:T(8,128)(2,1)S(1)}, bf16[128,256]{1,0:T(8,128)(2,1)S(1)}, u32[]{:S(2)}, u32[]{:S(2)}) collective-permute-start(bf16[128,256]{1,0:T(8,128)(2,1)S(1)} %shard_map.103.near), channel_id=1, source_target_pairs={{0,8},{4,12},{8,0},{12,4},{1,9},{5,13},{9,1},{13,5},{2,10},{6,14},... | collective-permute-start | bytes 196616 | tf_op jit(solution)/shard_map/ppermute | solution.py:350
  13.1 5.8 %copy-start = (bf16[256,4096]{1,0:T(8,128)(2,1)S(1)}, bf16[256,4096]{1,0:T(8,128)(2,1)}, u32[]{:S(2)}) copy-start(bf16[256,4096]{1,0:T(8,128)(2,1)} %refs_0_.9) | copy-start | bytes 6291460
  13.4 8.0 %copy-start.2 = (bf16[4096,256]{1,0:T(8,128)(2,1)S(1)}, bf16[4096,256]{1,0:T(8,128)(2,1)}, u32[]{:S(2)}) copy-start(bf16[4096,256]{1,0:T(8,128)(2,1)} %refs_12_.1) | copy-start | bytes 6291460
  13.4 4.8 %collective-permute-start.2 = (f32[64,256]{1,0:T(8,128)S(1)}, f32[64,256]{1,0:T(8,128)S(1)}, u32[]{:S(2)}, u32[]{:S(2)}) collective-permute-start(f32[64,256]{1,0:T(8,128)S(1)} %shard_map.104.refs_0_), channel_id=1, source_target_pairs={{0,1},{1,0},{2,3},{3,2},{4,5},{5,4},{6,7},{7,6},{8,9},{9,8},{10,11... | collective-permute-start | bytes 196616 | tf_op jit(solution)/shard_map/ppermute | solution.py:365
  13.5 10.5 %collective-permute-start.6 = (bf16[64,4096]{1,0:T(8,128)(2,1)S(1)}, bf16[64,4096]{1,0:T(8,128)(2,1)S(1)}, u32[]{:S(2)}, u32[]{:S(2)}) collective-permute-start(bf16[64,4096]{1,0:T(8,128)(2,1)S(1)} %bitcast.7), channel_id=1, source_target_pairs={{4,8},{8,4},{5,9},{9,5},{6,10},{10,6},{7,11},{11,7},{20,24},{24,20... | collective-permute-start | bytes 1572872 | tf_op jit(solution)/shard_map/ppermute | solution.py:372
  14.3 15.9 %collective-permute-start.5 = (bf16[64,4096]{1,0:T(8,128)(2,1)S(1)}, bf16[64,4096]{1,0:T(8,128)(2,1)S(1)}, u32[]{:S(2)}, u32[]{:S(2)}) collective-permute-start(bf16[64,4096]{1,0:T(8,128)(2,1)S(1)} %bitcast.8), channel_id=1, source_target_pairs={{0,4},{4,0},{8,12},{12,8},{1,5},{5,1},{9,13},{13,9},{2,6},{6,2},{1... | collective-permute-start | bytes 1572872 | tf_op jit(solution)/shard_map/ppermute | solution.py:371
  19.9 12.8 %collective-permute-start.7 = (bf16[64,4096]{1,0:T(8,128)(2,1)S(1)}, bf16[64,4096]{1,0:T(8,128)(2,1)S(1)}, u32[]{:S(2)}, u32[]{:S(2)}) collective-permute-start(bf16[64,4096]{1,0:T(8,128)(2,1)S(1)} %get-tuple-element.45.refs_2_), channel_id=1, source_target_pairs={{0,2},{2,0},{1,3},{3,1},{4,6},{6,4},{5,7},{7,5},{8,10},{10,8},{9,1... | collective-permute-start | bytes 1572872 | tf_op jit(solution)/shard_map/ppermute | solution.py:373
  30.2 10.2 %collective-permute-start.9 = (bf16[64,4096]{1,0:T(8,128)(2,1)S(1)}, bf16[64,4096]{1,0:T(8,128)(2,1)S(1)}, u32[]{:S(2)}, u32[]{:S(2)}) collective-permute-start(bf16[64,4096]{1,0:T(8,128)(2,1)S(1)} %collective-permute-done.5.refs_6_.refs_1_.refs_4_), channel_id=1, source_target_pairs={{4,8},{8,4},{5,9},{9,5},{6,10},{10,6},{7,11},{11,7},{20,24},{24,20... | collective-permute-start | bytes 1572872 | tf_op jit(solution)/shard_map/ppermute | solution.py:393
  33.6 12.7 %collective-permute-start.8 = (bf16[64,4096]{1,0:T(8,128)(2,1)S(1)}, bf16[64,4096]{1,0:T(8,128)(2,1)S(1)}, u32[]{:S(2)}, u32[]{:S(2)}) collective-permute-start(bf16[64,4096]{1,0:T(8,128)(2,1)S(1)} %get-tuple-element.49), channel_id=1, source_target_pairs={{0,4},{4,0},{8,12},{12,8},{1,5},{5,1},{9,13},{13,9},{2,6},{6,2},{1... | collective-permute-start | bytes 1572872 | tf_op jit(solution)/shard_map/ppermute | solution.py:392
  35.1 24.4 %collective-permute-start.4 = (bf16[1024,256]{1,0:T(8,128)(2,1)S(1)}, bf16[1024,256]{1,0:T(8,128)(2,1)S(1)}, u32[]{:S(2)}, u32[]{:S(2)}) collective-permute-start(bf16[1024,256]{1,0:T(8,128)(2,1)S(1)} %collective-permute-done.3.refs_4_.direct), channel_id=1, source_target_pairs={{0,16},{16,0},{1,17},{17,1},{2,18},{18,2},{3,19},{19,3},{4,20},{20... | collective-permute-start | bytes 1572872 | tf_op jit(solution)/shard_map/ppermute | solution.py:383
  36.6 14.9 %collective-permute-start.11 = (bf16[1024,256]{1,0:T(8,128)(2,1)S(1)}, bf16[1024,256]{1,0:T(8,128)(2,1)S(1)}, u32[]{:S(2)}, u32[]{:S(2)}) collective-permute-start(bf16[1024,256]{1,0:T(8,128)(2,1)S(1)} %get-tuple-element.55), channel_id=1, source_target_pairs={{0,2},{2,0},{1,3},{3,1},{4,6},{6,4},{5,7},{7,5},{8,10},{10,8},{9,1... | collective-permute-start | bytes 1572872 | tf_op jit(solution)/shard_map/ppermute | solution.py:391
  37.6 26.2 %collective-permute-start.15 = (bf16[64,4096]{1,0:T(8,128)(2,1)S(1)}, bf16[64,4096]{1,0:T(8,128)(2,1)S(1)}, u32[]{:S(2)}, u32[]{:S(2)}) collective-permute-start(bf16[64,4096]{1,0:T(8,128)(2,1)S(1)} %get-tuple-element.63), channel_id=1, source_target_pairs={{0,2},{2,0},{1,3},{3,1},{4,6},{6,4},{5,7},{7,5},{8,10},{10,8},{9,1... | collective-permute-start | bytes 1572872 | tf_op jit(solution)/shard_map/ppermute | solution.py:403
  40.4 17.8 %collective-permute-start.10 = (bf16[64,4096]{1,0:T(8,128)(2,1)S(1)}, bf16[64,4096]{1,0:T(8,128)(2,1)S(1)}, u32[]{:S(2)}, u32[]{:S(2)}) collective-permute-start(bf16[64,4096]{1,0:T(8,128)(2,1)S(1)} %collective-permute-done.9.refs_4_.refs_2_.refs_9_.refs_3_), channel_id=1, source_target_pairs={{4,0},{8,12},{5,1},{9,13},{6,2},{10,14},{7,3},{11,15},{20,16},{24,... | collective-permute-start | bytes 1572872 | tf_op jit(solution)/shard_map/ppermute | solution.py:405
  51.5 12.3 %collective-permute-start.12 = (bf16[1024,256]{1,0:T(8,128)(2,1)S(1)}, bf16[1024,256]{1,0:T(8,128)(2,1)S(1)}, u32[]{:S(2)}, u32[]{:S(2)}) collective-permute-start(bf16[1024,256]{1,0:T(8,128)(2,1)S(1)} %collective-permute-done.11.refs_3_), channel_id=1, source_target_pairs={{0,16},{16,0},{1,17},{17,1},{2,18},{18,2},{3,19},{19,3},{4,20},{20... | collective-permute-start | bytes 1572872 | tf_op jit(solution)/shard_map/ppermute | solution.py:406
  52.0 11.8 %collective-permute-start.16 = (bf16[64,4096]{1,0:T(8,128)(2,1)S(1)}, bf16[64,4096]{1,0:T(8,128)(2,1)S(1)}, u32[]{:S(2)}, u32[]{:S(2)}) collective-permute-start(bf16[64,4096]{1,0:T(8,128)(2,1)S(1)} %shard_map.112), channel_id=1, source_target_pairs={{4,8},{8,4},{5,9},{9,5},{6,10},{10,6},{7,11},{11,7},{20,24},{24,20... | collective-permute-start | bytes 1572872 | tf_op jit(solution)/shard_map/ppermute | solution.py:404
  59.4 3.0 %collective-permute-start.13 = (f32[64,256]{1,0:T(8,128)S(1)}, f32[64,256]{1,0:T(8,128)S(1)}, u32[]{:S(2)}, u32[]{:S(2)}) collective-permute-start(f32[64,256]{1,0:T(8,128)S(1)} %shard_map.115.low), channel_id=1, source_target_pairs={{0,1},{1,0},{2,3},{3,2},{4,5},{5,4},{6,7},{7,6},{8,9},{9,8},{10,11... | collective-permute-start | bytes 196616 | tf_op jit(solution)/shard_map/ppermute | solution.py:410
  62.7 4.6 %collective-permute-start.18 = (bf16[128,256]{1,0:T(8,128)(2,1)S(1)}, bf16[128,256]{1,0:T(8,128)(2,1)S(1)}, u32[]{:S(2)}, u32[]{:S(2)}) collective-permute-start(bf16[128,256]{1,0:T(8,128)(2,1)S(1)} %get-tuple-element.64.refs_3_), channel_id=1, source_target_pairs={{0,2},{2,0},{1,3},{3,1},{4,6},{6,4},{5,7},{7,5},{8,10},{10,8},{9,1... | collective-permute-start | bytes 196616 | tf_op jit(solution)/shard_map/ppermute | solution.py:444
  64.0 11.4 %collective-permute-start.17 = (bf16[32,4096]{1,0:T(8,128)(2,1)S(1)}, bf16[32,4096]{1,0:T(8,128)(2,1)S(1)}, u32[]{:S(2)}, u32[]{:S(2)}) collective-permute-start(bf16[32,4096]{1,0:T(8,128)(2,1)S(1)} %get-tuple-element.66), channel_id=1, source_target_pairs={{0,4},{4,0},{8,12},{12,8},{1,5},{5,1},{9,13},{13,9},{2,6},{6,2},{1... | collective-permute-start | bytes 786440 | tf_op jit(solution)/shard_map/ppermute | solution.py:443
  67.1 8.3 %collective-permute-start.14 = (f32[256,256]{1,0:T(8,128)S(1)}, f32[256,256]{1,0:T(8,128)S(1)}, u32[]{:S(2)}, u32[]{:S(2)}) collective-permute-start(f32[256,256]{1,0:T(8,128)S(1)} %get-tuple-element.61), channel_id=1, source_target_pairs={{0,1},{1,0},{2,3},{3,2},{4,5},{5,4},{6,7},{7,6},{8,9},{9,8},{10,11... | collective-permute-start | bytes 786440 | tf_op jit(solution)/shard_map/ppermute | solution.py:452
  67.4 5.4 %collective-permute-start.19 = (bf16[32,256]{1,0:T(8,128)(2,1)S(1)}, bf16[32,256]{1,0:T(8,128)(2,1)S(1)}, u32[]{:S(2)}, u32[]{:S(2)}) collective-permute-start(bf16[32,256]{1,0:T(8,128)(2,1)S(1)} %get-tuple-element.69), channel_id=1, source_target_pairs={{0,4},{4,0},{8,12},{12,8},{1,5},{5,1},{9,13},{13,9},{2,6},{6,2},{1... | collective-permute-start | bytes 49160 | tf_op jit(solution)/shard_map/ppermute | solution.py:449
  69.3 4.6 %collective-permute-start.20 = (bf16[32,256]{1,0:T(8,128)(2,1)S(1)}, bf16[32,256]{1,0:T(8,128)(2,1)S(1)}, u32[]{:S(2)}, u32[]{:S(2)}) collective-permute-start(bf16[32,256]{1,0:T(8,128)(2,1)S(1)} %get-tuple-element.70), channel_id=1, source_target_pairs={{0,8},{4,12},{8,0},{12,4},{1,9},{5,13},{9,1},{13,5},{2,10},{6,14},... | collective-permute-start | bytes 49160 | tf_op jit(solution)/shard_map/ppermute | solution.py:449
  69.8 5.5 %collective-permute-start.21 = (bf16[32,256]{1,0:T(8,128)(2,1)S(1)}, bf16[32,256]{1,0:T(8,128)(2,1)S(1)}, u32[]{:S(2)}, u32[]{:S(2)}) collective-permute-start(bf16[32,256]{1,0:T(8,128)(2,1)S(1)} %get-tuple-element.71), channel_id=1, source_target_pairs={{0,12},{4,8},{8,4},{12,0},{1,13},{5,9},{9,5},{13,1},{2,14},{6,10},... | collective-permute-start | bytes 49160 | tf_op jit(solution)/shard_map/ppermute | solution.py:449

commit v5 on v4

--- a/solution.py
+++ b/solution.py
@@ -23,6 +23,7 @@
 NEAR_US = 6
 UP_US = 4
 LAST_US = 15
+MARK_US = 3
 FIRST_SHARE = 4
 WHOLE = pl.BlockSpec(memory_space=pltpu.VMEM)
 ANY = pl.BlockSpec(memory_space=pl.ANY)
@@ -311,6 +312,10 @@
     down_out[...] = mine[...] + last[...].astype(F32)
 
 
+def mark_kernel(out):
+    out[...] = jnp.zeros(out.shape, out.dtype)
+
+
 def add_kernel(one, two, out):
     out[...] = (one[...].astype(F32) + two[...].astype(F32)).astype(BF16)
 
@@ -399,7 +404,7 @@
         functools.partial(low_kernel, rank, (2,), (2,)),
         narrow, tokens, deal, job, down_cross, swapped, low_near,
     )
-    far_sum = call(add_kernel, span_wide, far, swapped, after=(down_cross2, low_near,), us=SUM_US)
+    far_sum = call(add_kernel, span_wide, far, swapped, after=(down_cross2, low_near, relay_first), us=SUM_US)
     got_near = lax.ppermute(ordered(send_near, far), "fsdp", swap(2))
     cross = lax.ppermute(far_sum, "dp", middle)
     down_out2 = lax.ppermute(ordered(down_cross2, far), "dp", outward)
@@ -436,9 +441,10 @@
 
     input_first, other_first = base(0, got_first, relay_first)
     input_gradient, other_second = base(first_rows, got_second, relay_second, input_first)
+    crossed = call(mark_kernel, struct((8, 128), F32), after=(cross,), us=MARK_US)
     next_sum, mine_sum = call(
         near_kernel, (half_wide, struct((half, width), F32)),
-        near_kept, got_near, cross, after=(up_away, other_first, relay_second), us=NEAR_US,
+        near_kept, got_near, cross, after=(up_away, other_first, relay_second, crossed), us=NEAR_US,
     )
     last = lax.ppermute(next_sum, "dp", swap(4))
     up_got = lax.ppermute(up_away, "fsdp", swap(2))

time: 76.5 us -> 76.4 us (level)
  starting transfers between devices: 27.7 us -> 28.8 us
  waiting for transfers between devices: 29.7 us -> 28.6 us
    ppermute x1, waiting for transfers between devices: 5.04 us -> 0.01 us  [gather_adapters(): got_second = lax.ppermute(ordered(weight_second, got_far), 'fsdp', swap(2))]
    ppermute x1, waiting for transfers between devices: 4.41 us -> 7.41 us  [gather_adapters(): down_out2 = lax.ppermute(ordered(down_cross2, far), 'dp', outward)]
    ppermute x1, waiting for transfers between devices: 4.58 us -> 7.13 us  [gather_adapters(): swapped = lax.ppermute(far_swap, 'dp', swap(4))]
    ppermute x1, waiting for transfers between devices: 6.26 us -> 4.68 us  [gather_adapters(): down_next = lax.ppermute(down_sent, 'dp', swap(4))]
    ppermute x1, starting transfers between devices: 0.51 us -> 1.52 us  [gather_adapters(): relay_second = lax.ppermute(ordered(got_second, far_sum), 'rep', swap(2))]
    pallas_call x19 -> x20, Pallas kernels: 16.3 us -> 16.3 us  [call(): pl.pallas_call(kernel, out_shape=out_shape, in_specs=(in_specs or [WHOLE]...]
  transfers between devices with their start and end apart: 22 -> 22, of which waited for: 10 -> 9; matrix products, arithmetic and copies ran while one was open for 0% -> 0% of each run, Pallas kernels for 20% -> 20%
where the time goes in v5:
time: 76.4 us; the launch traced here: 76.2 us
  starting transfers between devices  28.8 us (38%)
  waiting for transfers between devices  28.6 us (37%)
  Pallas kernels  16.3 us (21%)
  local copies, waits for them, and re-layouts  1.62 us (2%)
  between operations  0.91 us (1%)
    pallas_call x20, Pallas kernels, call(): pl.pallas_call(kernel, out_shape=out_shape, in_specs=(in_specs or [WHOLE]...  16.3 us
    ppermute x1, waiting for transfers between devices, gather_adapters(): down_out2 = lax.ppermute(ordered(down_cross2, far), 'dp', outward)  7.41 us
    ppermute x1, waiting for transfers between devices, gather_adapters(): swapped = lax.ppermute(far_swap, 'dp', swap(4))  7.13 us
    ppermute x1, waiting for transfers between devices, gather_adapters(): down_next = lax.ppermute(down_sent, 'dp', swap(4))  4.68 us
    ppermute x3, starting transfers between devices, gather_adapters(): lax.ppermute(sent, 'dp', swap(4, k + 1))  4.45 us
    ppermute x1, starting transfers between devices, gather_adapters(): down_next = lax.ppermute(down_sent, 'dp', swap(4))  3.86 us
    ppermute x3, waiting for transfers between devices, gather_adapters(): lax.ppermute(sent, 'dp', swap(4, k + 1))  3.47 us
    ppermute x1, waiting for transfers between devices, gather_adapters(): ups = (up_pair, lax.ppermute(up_pair, 'dp', swap(4, 2)))  3.28 us
  transfers between devices with their start and end apart: 22, of which 9 were waited for; matrix products, arithmetic and copies ran while one was open for 0% of the time, Pallas kernels for 20%

profile of v5, /device:TPU:0, one launch (start us, length us, event | category | flops | bytes accessed | tf_op | source)
XLA Modules:
  0.0 76.2 jit_solution(4722876787944467117)
XLA Ops:
  0.6 3.1 %collective-permute-start = (bf16[64,256]{1,0:T(8,128)(2,1)}, bf16[64,256]{1,0:T(8,128)(2,1)S(1)}, u32[]{:S(2)}, u32[]{:S(2)}) collective-permute-start(bf16[64,256]{1,0:T(8,128)(2,1)} %bitcast.12), channel_id=1, source_target_pairs={{0,4},{4,0},{8,12},{12,8},{1,5},{5,1},{9,13},{13,9},{2,6},{6,2},{1... | collective-permute-start | bytes 98312 | tf_op jit(solution)/shard_map/ppermute | solution.py:347
  3.7 1.6 %copy-done.1 = bf16[4096,256]{1,0:T(8,128)(2,1)S(1)} copy-done((bf16[4096,256]{1,0:T(8,128)(2,1)S(1)}, bf16[4096,256]{1,0:T(8,128)(2,1)}, u32[]{:S(2)}) %copy-start.1) | copy-done | bytes 2097176
  5.3 0.1 shard_map.105
  5.4 1.6 %collective-permute-start.3 = (bf16[1024,256]{1,0:T(8,128)(2,1)S(1)}, bf16[1024,256]{1,0:T(8,128)(2,1)S(1)}, u32[]{:S(2)}, u32[]{:S(2)}) collective-permute-start(bf16[1024,256]{1,0:T(8,128)(2,1)S(1)} %get-tuple-element.44), channel_id=1, source_target_pairs={{0,2},{2,0},{1,3},{3,1},{4,6},{6,4},{5,7},{7,5},{8,10},{10,8},{9,1... | collective-permute-start | bytes 1572872 | tf_op jit(solution)/shard_map/ppermute | solution.py:364
  7.0 0.0 copy-done.6
  7.0 0.1 shard_map.102
  7.1 0.0 collective-permute-done.refs_1_
  7.2 2.7 %collective-permute-start.1 = (bf16[128,256]{1,0:T(8,128)(2,1)S(1)}, bf16[128,256]{1,0:T(8,128)(2,1)S(1)}, u32[]{:S(2)}, u32[]{:S(2)}) collective-permute-start(bf16[128,256]{1,0:T(8,128)(2,1)S(1)} %shard_map.103.near), channel_id=1, source_target_pairs={{0,8},{4,12},{8,0},{12,4},{1,9},{5,13},{9,1},{13,5},{2,10},{6,14},... | collective-permute-start | bytes 196616 | tf_op jit(solution)/shard_map/ppermute | solution.py:355
  9.8 3.3 %collective-permute-done.1.far = bf16[128,256]{1,0:T(8,128)(2,1)S(1)} collective-permute-done((bf16[128,256]{1,0:T(8,128)(2,1)S(1)}, bf16[128,256]{1,0:T(8,128)(2,1)S(1)}, u32[]{:S(2)}, u32[]{:S(2)}) %collective-permute-start.1) | collective-permute-done | bytes 65568 | tf_op jit(solution)/shard_map/ppermute | solution.py:355
  13.1 0.3 shard_map.104.refs_0_
  13.4 0.0 copy-start.2
  13.4 0.1 collective-permute-start.2
  13.5 0.8 %collective-permute-start.6 = (bf16[64,4096]{1,0:T(8,128)(2,1)S(1)}, bf16[64,4096]{1,0:T(8,128)(2,1)S(1)}, u32[]{:S(2)}, u32[]{:S(2)}) collective-permute-start(bf16[64,4096]{1,0:T(8,128)(2,1)S(1)} %bitcast.7), channel_id=1, source_target_pairs={{4,8},{8,4},{5,9},{9,5},{6,10},{10,6},{7,11},{11,7},{20,24},{24,20... | collective-permute-start | bytes 1572872 | tf_op jit(solution)/shard_map/ppermute | solution.py:377
  14.3 3.9 %collective-permute-start.5 = (bf16[64,4096]{1,0:T(8,128)(2,1)S(1)}, bf16[64,4096]{1,0:T(8,128)(2,1)S(1)}, u32[]{:S(2)}, u32[]{:S(2)}) collective-permute-start(bf16[64,4096]{1,0:T(8,128)(2,1)S(1)} %bitcast.8), channel_id=1, source_target_pairs={{0,4},{4,0},{8,12},{12,8},{1,5},{5,1},{9,13},{13,9},{2,6},{6,2},{1... | collective-permute-start | bytes 1572872 | tf_op jit(solution)/shard_map/ppermute | solution.py:376
  18.2 0.0 collective-permute-done.2.refs_1_
  18.2 0.7 collective-permute-done.3.refs_4_.direct
  18.9 1.0 %shard_map.106 = (bf16[64,256]{1,0:T(8,128)(2,1)S(1)}, bf16[64,4096]{1,0:T(8,128)(2,1)S(1)}, bf16[64,4096]{1,0:T(8,128)(2,1)S(1)}) custom-call(f32[64,256]{1,0:T(8,128)S(1)} %shard_map.104.refs_0_, f32[64,256]{1,0:T(8,128)S(1)} %collective-permute-done.2.refs_1_, s32[1,256]{1,0:T(1,128)S(1)} %get-tuple-element.42.deal.refs_2_.refs_1_, ...), custom_call_target="tpu_custom_call" | custom-call | flops 6899999744 | tf_op jit(solution)/shard_map/pallas_call | solution.py:264
  19.9 1.6 %collective-permute-start.7 = (bf16[64,4096]{1,0:T(8,128)(2,1)S(1)}, bf16[64,4096]{1,0:T(8,128)(2,1)S(1)}, u32[]{:S(2)}, u32[]{:S(2)}) collective-permute-start(bf16[64,4096]{1,0:T(8,128)(2,1)S(1)} %get-tuple-element.45.refs_2_), channel_id=1, source_target_pairs={{0,2},{2,0},{1,3},{3,1},{4,6},{6,4},{5,7},{7,5},{8,10},{10,8},{9,1... | collective-permute-start | bytes 1572872 | tf_op jit(solution)/shard_map/ppermute | solution.py:378
  21.4 1.6 %shard_map.107.refs_5_.own = f32[256,256]{1,0:T(8,128)S(1)} custom-call(bf16[256,4096]{1,0:T(8,128)(2,1)S(1)} %copy-done, bf16[4096,256]{1,0:T(8,128)(2,1)S(1)} %copy-done.2, bf16[64,4096]{1,0:T(8,128)(2,1)S(1)} %get-tuple-element.45.refs_2_), custom_call_target="tpu_custom_call" | custom-call | tf_op jit(solution)/shard_map/pallas_call | solution.py:264
  23.1 1.6 %collective-permute-start.4 = (bf16[1024,256]{1,0:T(8,128)(2,1)S(1)}, bf16[1024,256]{1,0:T(8,128)(2,1)S(1)}, u32[]{:S(2)}, u32[]{:S(2)}) collective-permute-start(bf16[1024,256]{1,0:T(8,128)(2,1)S(1)} %collective-permute-done.3.refs_4_.direct), channel_id=1, source_target_pairs={{0,16},{16,0},{1,17},{17,1},{2,18},{18,2},{3,19},{19,3},{4,20},{20... | collective-permute-start | bytes 1572872 | tf_op jit(solution)/shard_map/ppermute | solution.py:388
  24.7 0.8 %shard_map.108.refs_7_.refs_0_ = f32[64,4096]{1,0:T(8,128)S(1)} custom-call(bf16[64,256]{1,0:T(8,128)(2,1)S(1)} %get-tuple-element.46.grad_rank.refs_1_, s32[1,256]{1,0:T(1,128)S(1)} %get-tuple-element.42.deal.refs_2_.refs_1_, bf16[256,4096]{1,0:T(8,128)(2,1)S(1)} %copy-done), custom_call_target="tpu_custom_call" | custom-call | tf_op jit(solution)/shard_map/pallas_call | solution.py:264
  25.5 0.0 collective-permute-done.6.refs_4_.refs_2_.refs_7_.refs_3_
  25.5 4.7 %collective-permute-done.5.refs_6_.refs_1_.refs_4_ = bf16[64,4096]{1,0:T(8,128)(2,1)S(1)} collective-permute-done((bf16[64,4096]{1,0:T(8,128)(2,1)S(1)}, bf16[64,4096]{1,0:T(8,128)(2,1)S(1)}, u32[]{:S(2)}, u32[]{:S(2)}) %collective-permute-start.5) | collective-permute-done | bytes 524320 | tf_op jit(solution)/shard_map/ppermute | solution.py:376
  30.2 0.7 collective-permute-start.9
  30.9 1.8 %collective-permute-done.7.refs_0_ = bf16[64,4096]{1,0:T(8,128)(2,1)S(1)} collective-permute-done((bf16[64,4096]{1,0:T(8,128)(2,1)S(1)}, bf16[64,4096]{1,0:T(8,128)(2,1)S(1)}, u32[]{:S(2)}, u32[]{:S(2)}) %collective-permute-start.7) | collective-permute-done | bytes 524320 | tf_op jit(solution)/shard_map/ppermute | solution.py:378
  32.7 0.9 %shard_map.109 = (bf16[64,4096]{1,0:T(8,128)(2,1)S(1)}, bf16[64,4096]{1,0:T(8,128)(2,1)S(1)}) custom-call(bf16[64,4096]{1,0:T(8,128)(2,1)S(1)} %collective-permute-done.7.refs_0_, bf16[64,256]{1,0:T(8,128)(2,1)S(1)} %get-tuple-element.46.grad_rank.refs_1_, s32[1,256]{1,0:T(1,128)S(1)} %get-tuple-element.42.deal.refs_2_.refs_1_, ...), custom_call_target="tpu_custom_call" | custom-call | flops 6899999744 | tf_op jit(solution)/shard_map/pallas_call | solution.py:264
  33.6 1.5 %collective-permute-start.8 = (bf16[64,4096]{1,0:T(8,128)(2,1)S(1)}, bf16[64,4096]{1,0:T(8,128)(2,1)S(1)}, u32[]{:S(2)}, u32[]{:S(2)}) collective-permute-start(bf16[64,4096]{1,0:T(8,128)(2,1)S(1)} %get-tuple-element.49), channel_id=1, source_target_pairs={{0,4},{4,0},{8,12},{12,8},{1,5},{5,1},{9,13},{13,9},{2,6},{6,2},{1... | collective-permute-start | bytes 1572872 | tf_op jit(solution)/shard_map/ppermute | solution.py:397
  35.1 1.0 %collective-permute-start.11 = (bf16[1024,256]{1,0:T(8,128)(2,1)S(1)}, bf16[1024,256]{1,0:T(8,128)(2,1)S(1)}, u32[]{:S(2)}, u32[]{:S(2)}) collective-permute-start(bf16[1024,256]{1,0:T(8,128)(2,1)S(1)} %get-tuple-element.55), channel_id=1, source_target_pairs={{0,2},{2,0},{1,3},{3,1},{4,6},{6,4},{5,7},{7,5},{8,10},{10,8},{9,1... | collective-permute-start | bytes 1572872 | tf_op jit(solution)/shard_map/ppermute | solution.py:396
  36.1 1.8 %shard_map.111.refs_3_.refs_5_ = f32[64,256]{1,0:T(8,128)S(1)} custom-call(bf16[256,4096]{1,0:T(8,128)(2,1)S(1)} %copy-done, s32[1,256]{1,0:T(1,128)S(1)} %get-tuple-element.42.deal.refs_2_.refs_1_, s32[1,256]{1,0:T(1,128)S(1)} %get-tuple-element.43.job.refs_2_, bf16[64,4096]{1,0:T(8,128)(2,1)S(1)} %bitcast.9, ...), custom_call_target="tpu_custom_call" | custom-call | tf_op jit(solution)/shard_map/pallas_call | solution.py:264
  37.9 0.0 collective-permute-done.9.refs_4_.refs_2_.refs_9_.refs_3_
  37.9 1.3 %collective-permute-start.10 = (bf16[64,4096]{1,0:T(8,128)(2,1)S(1)}, bf16[64,4096]{1,0:T(8,128)(2,1)S(1)}, u32[]{:S(2)}, u32[]{:S(2)}) collective-permute-start(bf16[64,4096]{1,0:T(8,128)(2,1)S(1)} %collective-permute-done.9.refs_4_.refs_2_.refs_9_.refs_3_), channel_id=1, source_target_pairs={{4,0},{8,12},{5,1},{9,13},{6,2},{10,14},{7,3},{11,15},{20,16},{24,... | collective-permute-start | bytes 1572872 | tf_op jit(solution)/shard_map/ppermute | solution.py:410
  39.2 0.0 collective-permute-done.4.relayed.refs_4_
  39.2 7.1 %collective-permute-done.8.refs_3_.refs_1_.refs_8_.refs_4_ = bf16[64,4096]{1,0:T(8,128)(2,1)S(1)} collective-permute-done((bf16[64,4096]{1,0:T(8,128)(2,1)S(1)}, bf16[64,4096]{1,0:T(8,128)(2,1)S(1)}, u32[]{:S(2)}, u32[]{:S(2)}) %collective-permute-start.8) | collective-permute-done | bytes 524320 | tf_op jit(solution)/shard_map/ppermute | solution.py:397
  46.3 0.1 shard_map.112
  46.4 0.7 collective-permute-start.16
  47.1 1.0 %collective-permute-start.15 = (bf16[64,4096]{1,0:T(8,128)(2,1)S(1)}, bf16[64,4096]{1,0:T(8,128)(2,1)S(1)}, u32[]{:S(2)}, u32[]{:S(2)}) collective-permute-start(bf16[64,4096]{1,0:T(8,128)(2,1)S(1)} %get-tuple-element.63), channel_id=1, source_target_pairs={{0,2},{2,0},{1,3},{3,1},{4,6},{6,4},{5,7},{7,5},{8,10},{10,8},{9,1... | collective-permute-start | bytes 1572872 | tf_op jit(solution)/shard_map/ppermute | solution.py:408
  48.2 0.0 collective-permute-done.11.refs_3_
  48.2 1.5 %collective-permute-start.12 = (bf16[1024,256]{1,0:T(8,128)(2,1)S(1)}, bf16[1024,256]{1,0:T(8,128)(2,1)S(1)}, u32[]{:S(2)}, u32[]{:S(2)}) collective-permute-start(bf16[1024,256]{1,0:T(8,128)(2,1)S(1)} %collective-permute-done.11.refs_3_), channel_id=1, source_target_pairs={{0,16},{16,0},{1,17},{17,1},{2,18},{18,2},{3,19},{19,3},{4,20},{20... | collective-permute-start | bytes 1572872 | tf_op jit(solution)/shard_map/ppermute | solution.py:411
  49.7 1.2 %shard_map.114.refs_5_ = f32[64,256]{1,0:T(8,128)S(1)} custom-call(bf16[256,4096]{1,0:T(8,128)(2,1)S(1)} %copy-done, s32[1,256]{1,0:T(1,128)S(1)} %get-tuple-element.42.deal.refs_2_.refs_1_, s32[1,256]{1,0:T(1,128)S(1)} %get-tuple-element.43.job.refs_2_, bf16[64,4096]{1,0:T(8,128)(2,1)S(1)} %collective-permute-done.6.refs_4_.refs_2_.refs_7_.refs_3_, ...), custom_call_target="tpu_custom_call" | custom-call | tf_op jit(solution)/shard_map/pallas_call | solution.py:264
  50.8 7.4 %collective-permute-done.10.refs_5_.refs_10_.refs_4_ = bf16[64,4096]{1,0:T(8,128)(2,1)S(1)} collective-permute-done((bf16[64,4096]{1,0:T(8,128)(2,1)S(1)}, bf16[64,4096]{1,0:T(8,128)(2,1)S(1)}, u32[]{:S(2)}, u32[]{:S(2)}) %collective-permute-start.10) | collective-permute-done | bytes 524320 | tf_op jit(solution)/shard_map/ppermute | solution.py:410
  58.3 1.2 %shard_map.115.low = f32[64,256]{1,0:T(8,128)S(1)} custom-call(bf16[256,4096]{1,0:T(8,128)(2,1)S(1)} %copy-done, s32[1,256]{1,0:T(1,128)S(1)} %get-tuple-element.42.deal.refs_2_.refs_1_, s32[1,256]{1,0:T(1,128)S(1)} %get-tuple-element.43.job.refs_2_, bf16[64,4096]{1,0:T(8,128)(2,1)S(1)} %collective-permute-done.9.refs_4_.refs_2_.refs_9_.refs_3_, ...), custom_call_target="tpu_custom_call" | custom-call | tf_op jit(solution)/shard_map/pallas_call | solution.py:264
  59.4 0.1 collective-permute-start.13
  59.5 2.9 %shard_map.110 = (bf16[256,4096]{1,0:T(8,128)(2,1)}, f32[256,256]{1,0:T(8,128)S(1)}) custom-call(bf16[256,512]{1,0:T(8,128)(2,1)S(1)} %copy-done.4, bf16[64,256]{1,0:T(8,128)(2,1)S(1)} %get-tuple-element.46.grad_rank.refs_1_, s32[1,256]{1,0:T(1,128)S(1)} %get-tuple-element.42.deal.refs_2_.refs_1_, ...), custom_call_target="tpu_custom_call" | custom-call | tf_op jit(solution)/shard_map/pallas_call | solution.py:264
  62.4 0.0 collective-permute-done.13.low_got
  62.4 0.3 shard_map.116
  62.7 1.0 %collective-permute-start.18 = (bf16[128,256]{1,0:T(8,128)(2,1)S(1)}, bf16[128,256]{1,0:T(8,128)(2,1)S(1)}, u32[]{:S(2)}, u32[]{:S(2)}) collective-permute-start(bf16[128,256]{1,0:T(8,128)(2,1)S(1)} %get-tuple-element.64.refs_3_), channel_id=1, source_target_pairs={{0,2},{2,0},{1,3},{3,1},{4,6},{6,4},{5,7},{7,5},{8,10},{10,8},{9,1... | collective-permute-start | bytes 196616 | tf_op jit(solution)/shard_map/ppermute | solution.py:450
  63.8 0.0 collective-permute-done.16.refs_0_.refs_2_
  63.8 0.0 collective-permute-done.15.refs_1_
  63.8 0.0 collective-permute-done.12.refs_4_.refs_5_
  63.8 0.2 shard_map.119
  64.0 0.1 collective-permute-start.17
  64.0 2.9 %shard_map.113 = (bf16[256,4096]{1,0:T(8,128)(2,1)}, f32[256,256]{1,0:T(8,128)S(1)}) custom-call(bf16[256,512]{1,0:T(8,128)(2,1)S(1)} %copy-done.4, bf16[64,256]{1,0:T(8,128)(2,1)S(1)} %get-tuple-element.46.grad_rank.refs_1_, s32[1,256]{1,0:T(1,128)S(1)} %get-tuple-element.42.deal.refs_2_.refs_1_, ...), custom_call_target="tpu_custom_call", output_to_operand_aliasing={{0}: (13, {})} | custom-call | tf_op jit(solution)/shard_map/pallas_call | solution.py:264
  67.0 0.1 shard_map.117
  67.1 0.3 collective-permute-start.14
  67.3 0.0 collective-permute-done.18.got
  67.4 1.9 %collective-permute-start.19 = (bf16[32,256]{1,0:T(8,128)(2,1)S(1)}, bf16[32,256]{1,0:T(8,128)(2,1)S(1)}, u32[]{:S(2)}, u32[]{:S(2)}) collective-permute-start(bf16[32,256]{1,0:T(8,128)(2,1)S(1)} %get-tuple-element.69), channel_id=1, source_target_pairs={{0,4},{4,0},{8,12},{12,8},{1,5},{5,1},{9,13},{13,9},{2,6},{6,2},{1... | collective-permute-start | bytes 49160 | tf_op jit(solution)/shard_map/ppermute | solution.py:455
  69.2 0.5 collective-permute-start.20
  69.8 2.1 %collective-permute-start.21 = (bf16[32,256]{1,0:T(8,128)(2,1)S(1)}, bf16[32,256]{1,0:T(8,128)(2,1)S(1)}, u32[]{:S(2)}, u32[]{:S(2)}) collective-permute-start(bf16[32,256]{1,0:T(8,128)(2,1)S(1)} %get-tuple-element.71), channel_id=1, source_target_pairs={{0,12},{4,8},{8,4},{12,0},{1,13},{5,9},{9,5},{13,1},{2,14},{6,10},... | collective-permute-start | bytes 49160 | tf_op jit(solution)/shard_map/ppermute | solution.py:455
  71.8 1.0 %collective-permute-done.19.one = bf16[32,256]{1,0:T(8,128)(2,1)S(1)} collective-permute-done((bf16[32,256]{1,0:T(8,128)(2,1)S(1)}, bf16[32,256]{1,0:T(8,128)(2,1)S(1)}, u32[]{:S(2)}, u32[]{:S(2)}) %collective-permute-start.19) | collective-permute-done | bytes 16416 | tf_op jit(solution)/shard_map/ppermute | solution.py:455
  72.8 1.1 %collective-permute-done.20.two = bf16[32,256]{1,0:T(8,128)(2,1)S(1)} collective-permute-done((bf16[32,256]{1,0:T(8,128)(2,1)S(1)}, bf16[32,256]{1,0:T(8,128)(2,1)S(1)}, u32[]{:S(2)}, u32[]{:S(2)}) %collective-permute-start.20) | collective-permute-done | bytes 16416 | tf_op jit(solution)/shard_map/ppermute | solution.py:455
  73.9 1.4 %collective-permute-done.21.three = bf16[32,256]{1,0:T(8,128)(2,1)S(1)} collective-permute-done((bf16[32,256]{1,0:T(8,128)(2,1)S(1)}, bf16[32,256]{1,0:T(8,128)(2,1)S(1)}, u32[]{:S(2)}, u32[]{:S(2)}) %collective-permute-start.21) | collective-permute-done | bytes 16416 | tf_op jit(solution)/shard_map/ppermute | solution.py:455
  75.3 0.0 collective-permute-done.17.last
  75.3 0.0 collective-permute-done.14.base_got
  75.3 0.9 %shard_map.121 = (bf16[256,256]{1,0:T(8,128)(2,1)}, f32[32,4096]{1,0:T(8,128)}, f32[32,256]{1,0:T(8,128)}) custom-call(f32[256,256]{1,0:T(8,128)S(1)} %get-tuple-element.60.base_keep, f32[256,256]{1,0:T(8,128)S(1)} %collective-permute-done.14.base_got, f32[32,4096]{1,0:T(8,128)S(1)} %get-tuple-element.65.mine, ...), custom_call_target="tpu_custom_call" | custom-call | flops 17250000896 | tf_op jit(solution)/shard_map/pallas_call | solution.py:264
  (16 shorter events, 0.0 us)
Async XLA Ops:
  0.6 6.4 %copy-start.6 = (s32[256,1]{0,1:T(1,128)S(1)}, s32[256,1]{0,1:T(1,128)}, u32[]{:S(2)}) copy-start(s32[256,1]{0,1:T(1,128)} %param.12) | copy-start | bytes 3076
  0.6 6.5 %collective-permute-start = (bf16[64,256]{1,0:T(8,128)(2,1)}, bf16[64,256]{1,0:T(8,128)(2,1)S(1)}, u32[]{:S(2)}, u32[]{:S(2)}) collective-permute-start(bf16[64,256]{1,0:T(8,128)(2,1)} %bitcast.12), channel_id=1, source_target_pairs={{0,4},{4,0},{8,12},{12,8},{1,5},{5,1},{9,13},{13,9},{2,6},{6,2},{1... | collective-permute-start | bytes 98312 | tf_op jit(solution)/shard_map/ppermute | solution.py:347
  3.7 1.6 %copy-start.1 = (bf16[4096,256]{1,0:T(8,128)(2,1)S(1)}, bf16[4096,256]{1,0:T(8,128)(2,1)}, u32[]{:S(2)}) copy-start(bf16[4096,256]{1,0:T(8,128)(2,1)} %refs_12_.1) | copy-start | bytes 6291460
  5.3 1.7 %copy-start.3 = (bf16[4,16,4096]{2,1,0:T(8,128)(2,1)S(1)}, bf16[4,16,4096]{2,1,0:T(8,128)(2,1)}, u32[]{:S(2)}) copy-start(bf16[4,16,4096]{2,1,0:T(8,128)(2,1)} %param.10) | copy-start | bytes 1572868
  5.3 1.7 %copy-start.4 = (bf16[256,512]{1,0:T(8,128)(2,1)S(1)}, bf16[256,512]{1,0:T(8,128)(2,1)}, u32[]{:S(2)}) copy-start(bf16[256,512]{1,0:T(8,128)(2,1)} %refs_0_.7) | copy-start | bytes 786436
  5.3 1.7 %copy-start.5 = (bf16[4,16,256]{2,1,0:T(8,128)(2,1)S(1)}, bf16[4,16,256]{2,1,0:T(8,128)(2,1)}, u32[]{:S(2)}) copy-start(bf16[4,16,256]{2,1,0:T(8,128)(2,1)} %param.11) | copy-start | bytes 98308
  5.3 1.7 %copy-start.7 = (s32[256]{0:T(256)S(1)}, s32[256]{0:T(256)}, u32[]{:S(2)}) copy-start(s32[256]{0:T(256)} %param.13) | copy-start | bytes 3076
  5.4 13.4 %collective-permute-start.3 = (bf16[1024,256]{1,0:T(8,128)(2,1)S(1)}, bf16[1024,256]{1,0:T(8,128)(2,1)S(1)}, u32[]{:S(2)}, u32[]{:S(2)}) collective-permute-start(bf16[1024,256]{1,0:T(8,128)(2,1)S(1)} %get-tuple-element.44), channel_id=1, source_target_pairs={{0,2},{2,0},{1,3},{3,1},{4,6},{6,4},{5,7},{7,5},{8,10},{10,8},{9,1... | collective-permute-start | bytes 1572872 | tf_op jit(solution)/shard_map/ppermute | solution.py:364
  7.2 5.9 %collective-permute-start.1 = (bf16[128,256]{1,0:T(8,128)(2,1)S(1)}, bf16[128,256]{1,0:T(8,128)(2,1)S(1)}, u32[]{:S(2)}, u32[]{:S(2)}) collective-permute-start(bf16[128,256]{1,0:T(8,128)(2,1)S(1)} %shard_map.103.near), channel_id=1, source_target_pairs={{0,8},{4,12},{8,0},{12,4},{1,9},{5,13},{9,1},{13,5},{2,10},{6,14},... | collective-permute-start | bytes 196616 | tf_op jit(solution)/shard_map/ppermute | solution.py:355
  13.1 5.8 %copy-start = (bf16[256,4096]{1,0:T(8,128)(2,1)S(1)}, bf16[256,4096]{1,0:T(8,128)(2,1)}, u32[]{:S(2)}) copy-start(bf16[256,4096]{1,0:T(8,128)(2,1)} %refs_0_.9) | copy-start | bytes 6291460
  13.4 8.0 %copy-start.2 = (bf16[4096,256]{1,0:T(8,128)(2,1)S(1)}, bf16[4096,256]{1,0:T(8,128)(2,1)}, u32[]{:S(2)}) copy-start(bf16[4096,256]{1,0:T(8,128)(2,1)} %refs_12_.1) | copy-start | bytes 6291460
  13.4 4.8 %collective-permute-start.2 = (f32[64,256]{1,0:T(8,128)S(1)}, f32[64,256]{1,0:T(8,128)S(1)}, u32[]{:S(2)}, u32[]{:S(2)}) collective-permute-start(f32[64,256]{1,0:T(8,128)S(1)} %shard_map.104.refs_0_), channel_id=1, source_target_pairs={{0,1},{1,0},{2,3},{3,2},{4,5},{5,4},{6,7},{7,6},{8,9},{9,8},{10,11... | collective-permute-start | bytes 196616 | tf_op jit(solution)/shard_map/ppermute | solution.py:370
  13.5 12.0 %collective-permute-start.6 = (bf16[64,4096]{1,0:T(8,128)(2,1)S(1)}, bf16[64,4096]{1,0:T(8,128)(2,1)S(1)}, u32[]{:S(2)}, u32[]{:S(2)}) collective-permute-start(bf16[64,4096]{1,0:T(8,128)(2,1)S(1)} %bitcast.7), channel_id=1, source_target_pairs={{4,8},{8,4},{5,9},{9,5},{6,10},{10,6},{7,11},{11,7},{20,24},{24,20... | collective-permute-start | bytes 1572872 | tf_op jit(solution)/shard_map/ppermute | solution.py:377
  14.3 15.9 %collective-permute-start.5 = (bf16[64,4096]{1,0:T(8,128)(2,1)S(1)}, bf16[64,4096]{1,0:T(8,128)(2,1)S(1)}, u32[]{:S(2)}, u32[]{:S(2)}) collective-permute-start(bf16[64,4096]{1,0:T(8,128)(2,1)S(1)} %bitcast.8), channel_id=1, source_target_pairs={{0,4},{4,0},{8,12},{12,8},{1,5},{5,1},{9,13},{13,9},{2,6},{6,2},{1... | collective-permute-start | bytes 1572872 | tf_op jit(solution)/shard_map/ppermute | solution.py:376
  19.9 12.8 %collective-permute-start.7 = (bf16[64,4096]{1,0:T(8,128)(2,1)S(1)}, bf16[64,4096]{1,0:T(8,128)(2,1)S(1)}, u32[]{:S(2)}, u32[]{:S(2)}) collective-permute-start(bf16[64,4096]{1,0:T(8,128)(2,1)S(1)} %get-tuple-element.45.refs_2_), channel_id=1, source_target_pairs={{0,2},{2,0},{1,3},{3,1},{4,6},{6,4},{5,7},{7,5},{8,10},{10,8},{9,1... | collective-permute-start | bytes 1572872 | tf_op jit(solution)/shard_map/ppermute | solution.py:378
  23.1 16.1 %collective-permute-start.4 = (bf16[1024,256]{1,0:T(8,128)(2,1)S(1)}, bf16[1024,256]{1,0:T(8,128)(2,1)S(1)}, u32[]{:S(2)}, u32[]{:S(2)}) collective-permute-start(bf16[1024,256]{1,0:T(8,128)(2,1)S(1)} %collective-permute-done.3.refs_4_.direct), channel_id=1, source_target_pairs={{0,16},{16,0},{1,17},{17,1},{2,18},{18,2},{3,19},{19,3},{4,20},{20... | collective-permute-start | bytes 1572872 | tf_op jit(solution)/shard_map/ppermute | solution.py:388
  30.2 7.7 %collective-permute-start.9 = (bf16[64,4096]{1,0:T(8,128)(2,1)S(1)}, bf16[64,4096]{1,0:T(8,128)(2,1)S(1)}, u32[]{:S(2)}, u32[]{:S(2)}) collective-permute-start(bf16[64,4096]{1,0:T(8,128)(2,1)S(1)} %collective-permute-done.5.refs_6_.refs_1_.refs_4_), channel_id=1, source_target_pairs={{4,8},{8,4},{5,9},{9,5},{6,10},{10,6},{7,11},{11,7},{20,24},{24,20... | collective-permute-start | bytes 1572872 | tf_op jit(solution)/shard_map/ppermute | solution.py:398
  33.6 12.7 %collective-permute-start.8 = (bf16[64,4096]{1,0:T(8,128)(2,1)S(1)}, bf16[64,4096]{1,0:T(8,128)(2,1)S(1)}, u32[]{:S(2)}, u32[]{:S(2)}) collective-permute-start(bf16[64,4096]{1,0:T(8,128)(2,1)S(1)} %get-tuple-element.49), channel_id=1, source_target_pairs={{0,4},{4,0},{8,12},{12,8},{1,5},{5,1},{9,13},{13,9},{2,6},{6,2},{1... | collective-permute-start | bytes 1572872 | tf_op jit(solution)/shard_map/ppermute | solution.py:397
  35.1 13.1 %collective-permute-start.11 = (bf16[1024,256]{1,0:T(8,128)(2,1)S(1)}, bf16[1024,256]{1,0:T(8,128)(2,1)S(1)}, u32[]{:S(2)}, u32[]{:S(2)}) collective-permute-start(bf16[1024,256]{1,0:T(8,128)(2,1)S(1)} %get-tuple-element.55), channel_id=1, source_target_pairs={{0,2},{2,0},{1,3},{3,1},{4,6},{6,4},{5,7},{7,5},{8,10},{10,8},{9,1... | collective-permute-start | bytes 1572872 | tf_op jit(solution)/shard_map/ppermute | solution.py:396
  37.9 20.4 %collective-permute-start.10 = (bf16[64,4096]{1,0:T(8,128)(2,1)S(1)}, bf16[64,4096]{1,0:T(8,128)(2,1)S(1)}, u32[]{:S(2)}, u32[]{:S(2)}) collective-permute-start(bf16[64,4096]{1,0:T(8,128)(2,1)S(1)} %collective-permute-done.9.refs_4_.refs_2_.refs_9_.refs_3_), channel_id=1, source_target_pairs={{4,0},{8,12},{5,1},{9,13},{6,2},{10,14},{7,3},{11,15},{20,16},{24,... | collective-permute-start | bytes 1572872 | tf_op jit(solution)/shard_map/ppermute | solution.py:410
  46.4 17.3 %collective-permute-start.16 = (bf16[64,4096]{1,0:T(8,128)(2,1)S(1)}, bf16[64,4096]{1,0:T(8,128)(2,1)S(1)}, u32[]{:S(2)}, u32[]{:S(2)}) collective-permute-start(bf16[64,4096]{1,0:T(8,128)(2,1)S(1)} %shard_map.112), channel_id=1, source_target_pairs={{4,8},{8,4},{5,9},{9,5},{6,10},{10,6},{7,11},{11,7},{20,24},{24,20... | collective-permute-start | bytes 1572872 | tf_op jit(solution)/shard_map/ppermute | solution.py:409
  47.1 16.6 %collective-permute-start.15 = (bf16[64,4096]{1,0:T(8,128)(2,1)S(1)}, bf16[64,4096]{1,0:T(8,128)(2,1)S(1)}, u32[]{:S(2)}, u32[]{:S(2)}) collective-permute-start(bf16[64,4096]{1,0:T(8,128)(2,1)S(1)} %get-tuple-element.63), channel_id=1, source_target_pairs={{0,2},{2,0},{1,3},{3,1},{4,6},{6,4},{5,7},{7,5},{8,10},{10,8},{9,1... | collective-permute-start | bytes 1572872 | tf_op jit(solution)/shard_map/ppermute | solution.py:408
  48.2 15.6 %collective-permute-start.12 = (bf16[1024,256]{1,0:T(8,128)(2,1)S(1)}, bf16[1024,256]{1,0:T(8,128)(2,1)S(1)}, u32[]{:S(2)}, u32[]{:S(2)}) collective-permute-start(bf16[1024,256]{1,0:T(8,128)(2,1)S(1)} %collective-permute-done.11.refs_3_), channel_id=1, source_target_pairs={{0,16},{16,0},{1,17},{17,1},{2,18},{18,2},{3,19},{19,3},{4,20},{20... | collective-permute-start | bytes 1572872 | tf_op jit(solution)/shard_map/ppermute | solution.py:411
  59.4 3.0 %collective-permute-start.13 = (f32[64,256]{1,0:T(8,128)S(1)}, f32[64,256]{1,0:T(8,128)S(1)}, u32[]{:S(2)}, u32[]{:S(2)}) collective-permute-start(f32[64,256]{1,0:T(8,128)S(1)} %shard_map.115.low), channel_id=1, source_target_pairs={{0,1},{1,0},{2,3},{3,2},{4,5},{5,4},{6,7},{7,6},{8,9},{9,8},{10,11... | collective-permute-start | bytes 196616 | tf_op jit(solution)/shard_map/ppermute | solution.py:415
  62.7 4.6 %collective-permute-start.18 = (bf16[128,256]{1,0:T(8,128)(2,1)S(1)}, bf16[128,256]{1,0:T(8,128)(2,1)S(1)}, u32[]{:S(2)}, u32[]{:S(2)}) collective-permute-start(bf16[128,256]{1,0:T(8,128)(2,1)S(1)} %get-tuple-element.64.refs_3_), channel_id=1, source_target_pairs={{0,2},{2,0},{1,3},{3,1},{4,6},{6,4},{5,7},{7,5},{8,10},{10,8},{9,1... | collective-permute-start | bytes 196616 | tf_op jit(solution)/shard_map/ppermute | solution.py:450
  64.0 11.3 %collective-permute-start.17 = (bf16[32,4096]{1,0:T(8,128)(2,1)S(1)}, bf16[32,4096]{1,0:T(8,128)(2,1)S(1)}, u32[]{:S(2)}, u32[]{:S(2)}) collective-permute-start(bf16[32,4096]{1,0:T(8,128)(2,1)S(1)} %get-tuple-element.66), channel_id=1, source_target_pairs={{0,4},{4,0},{8,12},{12,8},{1,5},{5,1},{9,13},{13,9},{2,6},{6,2},{1... | collective-permute-start | bytes 786440 | tf_op jit(solution)/shard_map/ppermute | solution.py:449
  67.1 8.2 %collective-permute-start.14 = (f32[256,256]{1,0:T(8,128)S(1)}, f32[256,256]{1,0:T(8,128)S(1)}, u32[]{:S(2)}, u32[]{:S(2)}) collective-permute-start(f32[256,256]{1,0:T(8,128)S(1)} %get-tuple-element.61), channel_id=1, source_target_pairs={{0,1},{1,0},{2,3},{3,2},{4,5},{5,4},{6,7},{7,6},{8,9},{9,8},{10,11... | collective-permute-start | bytes 786440 | tf_op jit(solution)/shard_map/ppermute | solution.py:458
  67.4 5.4 %collective-permute-start.19 = (bf16[32,256]{1,0:T(8,128)(2,1)S(1)}, bf16[32,256]{1,0:T(8,128)(2,1)S(1)}, u32[]{:S(2)}, u32[]{:S(2)}) collective-permute-start(bf16[32,256]{1,0:T(8,128)(2,1)S(1)} %get-tuple-element.69), channel_id=1, source_target_pairs={{0,4},{4,0},{8,12},{12,8},{1,5},{5,1},{9,13},{13,9},{2,6},{6,2},{1... | collective-permute-start | bytes 49160 | tf_op jit(solution)/shard_map/ppermute | solution.py:455
  69.2 4.6 %collective-permute-start.20 = (bf16[32,256]{1,0:T(8,128)(2,1)S(1)}, bf16[32,256]{1,0:T(8,128)(2,1)S(1)}, u32[]{:S(2)}, u32[]{:S(2)}) collective-permute-start(bf16[32,256]{1,0:T(8,128)(2,1)S(1)} %get-tuple-element.70), channel_id=1, source_target_pairs={{0,8},{4,12},{8,0},{12,4},{1,9},{5,13},{9,1},{13,5},{2,10},{6,14},... | collective-permute-start | bytes 49160 | tf_op jit(solution)/shard_map/ppermute | solution.py:455
  69.8 5.5 %collective-permute-start.21 = (bf16[32,256]{1,0:T(8,128)(2,1)S(1)}, bf16[32,256]{1,0:T(8,128)(2,1)S(1)}, u32[]{:S(2)}, u32[]{:S(2)}) collective-permute-start(bf16[32,256]{1,0:T(8,128)(2,1)S(1)} %get-tuple-element.71), channel_id=1, source_target_pairs={{0,12},{4,8},{8,4},{12,0},{1,13},{5,9},{9,5},{13,1},{2,14},{6,10},... | collective-permute-start | bytes 49160 | tf_op jit(solution)/shard_map/ppermute | solution.py:455

commit v6 on v5

--- a/solution.py
+++ b/solution.py
@@ -444,7 +444,7 @@
     crossed = call(mark_kernel, struct((8, 128), F32), after=(cross,), us=MARK_US)
     next_sum, mine_sum = call(
         near_kernel, (half_wide, struct((half, width), F32)),
-        near_kept, got_near, cross, after=(up_away, other_first, relay_second, crossed), us=NEAR_US,
+        near_kept, got_near, cross, after=(relay_second, crossed), us=NEAR_US,
     )
     last = lax.ppermute(next_sum, "dp", swap(4))
     up_got = lax.ppermute(up_away, "fsdp", swap(2))

time: 76.4 us -> 76.4 us (level)
  no operation moved by 1% of the time
where the time goes in v6:
time: 76.4 us; the launch traced here: 76.2 us
  starting transfers between devices  28.8 us (38%)
  waiting for transfers between devices  28.6 us (37%)
  Pallas kernels  16.3 us (21%)
  local copies, waits for them, and re-layouts  1.62 us (2%)
  between operations  0.9 us (1%)
    pallas_call x20, Pallas kernels, call(): pl.pallas_call(kernel, out_shape=out_shape, in_specs=(in_specs or [WHOLE]...  16.3 us
    ppermute x1, waiting for transfers between devices, gather_adapters(): down_out2 = lax.ppermute(ordered(down_cross2, far), 'dp', outward)  7.41 us
    ppermute x1, waiting for transfers between devices, gather_adapters(): swapped = lax.ppermute(far_swap, 'dp', swap(4))  7.13 us
    ppermute x1, waiting for transfers between devices, gather_adapters(): down_next = lax.ppermute(down_sent, 'dp', swap(4))  4.68 us
    ppermute x3, starting transfers between devices, gather_adapters(): lax.ppermute(sent, 'dp', swap(4, k + 1))  4.45 us
    ppermute x1, starting transfers between devices, gather_adapters(): down_next = lax.ppermute(down_sent, 'dp', swap(4))  3.86 us
    ppermute x3, waiting for transfers between devices, gather_adapters(): lax.ppermute(sent, 'dp', swap(4, k + 1))  3.47 us
    ppermute x1, waiting for transfers between devices, gather_adapters(): ups = (up_pair, lax.ppermute(up_pair, 'dp', swap(4, 2)))  3.28 us
  transfers between devices with their start and end apart: 22, of which 9 were waited for; matrix products, arithmetic and copies ran while one was open for 0% of the time, Pallas kernels for 20%

profile of v6, /device:TPU:0, one launch (start us, length us, event | category | flops | bytes accessed | tf_op | source)
XLA Modules:
  0.0 76.2 jit_solution(8567701583499309695)
XLA Ops:
  0.6 3.1 %collective-permute-start = (bf16[64,256]{1,0:T(8,128)(2,1)}, bf16[64,256]{1,0:T(8,128)(2,1)S(1)}, u32[]{:S(2)}, u32[]{:S(2)}) collective-permute-start(bf16[64,256]{1,0:T(8,128)(2,1)} %bitcast.12), channel_id=1, source_target_pairs={{0,4},{4,0},{8,12},{12,8},{1,5},{5,1},{9,13},{13,9},{2,6},{6,2},{1... | collective-permute-start | bytes 98312 | tf_op jit(solution)/shard_map/ppermute | solution.py:347
  3.7 1.6 %copy-done.1 = bf16[4096,256]{1,0:T(8,128)(2,1)S(1)} copy-done((bf16[4096,256]{1,0:T(8,128)(2,1)S(1)}, bf16[4096,256]{1,0:T(8,128)(2,1)}, u32[]{:S(2)}) %copy-start.1) | copy-done | bytes 2097176
  5.3 0.1 shard_map.105
  5.4 1.6 %collective-permute-start.3 = (bf16[1024,256]{1,0:T(8,128)(2,1)S(1)}, bf16[1024,256]{1,0:T(8,128)(2,1)S(1)}, u32[]{:S(2)}, u32[]{:S(2)}) collective-permute-start(bf16[1024,256]{1,0:T(8,128)(2,1)S(1)} %get-tuple-element.44), channel_id=1, source_target_pairs={{0,2},{2,0},{1,3},{3,1},{4,6},{6,4},{5,7},{7,5},{8,10},{10,8},{9,1... | collective-permute-start | bytes 1572872 | tf_op jit(solution)/shard_map/ppermute | solution.py:364
  7.0 0.0 copy-done.3
  7.0 0.1 shard_map.102
  7.1 0.0 collective-permute-done.refs_1_
  7.2 2.7 %collective-permute-start.1 = (bf16[128,256]{1,0:T(8,128)(2,1)S(1)}, bf16[128,256]{1,0:T(8,128)(2,1)S(1)}, u32[]{:S(2)}, u32[]{:S(2)}) collective-permute-start(bf16[128,256]{1,0:T(8,128)(2,1)S(1)} %shard_map.103.near), channel_id=1, source_target_pairs={{0,8},{4,12},{8,0},{12,4},{1,9},{5,13},{9,1},{13,5},{2,10},{6,14},... | collective-permute-start | bytes 196616 | tf_op jit(solution)/shard_map/ppermute | solution.py:355
  9.8 3.3 %collective-permute-done.1.far = bf16[128,256]{1,0:T(8,128)(2,1)S(1)} collective-permute-done((bf16[128,256]{1,0:T(8,128)(2,1)S(1)}, bf16[128,256]{1,0:T(8,128)(2,1)S(1)}, u32[]{:S(2)}, u32[]{:S(2)}) %collective-permute-start.1) | collective-permute-done | bytes 65568 | tf_op jit(solution)/shard_map/ppermute | solution.py:355
  13.1 0.3 shard_map.104.refs_0_
  13.4 0.0 copy-start.2
  13.4 0.1 collective-permute-start.2
  13.5 0.8 %collective-permute-start.6 = (bf16[64,4096]{1,0:T(8,128)(2,1)S(1)}, bf16[64,4096]{1,0:T(8,128)(2,1)S(1)}, u32[]{:S(2)}, u32[]{:S(2)}) collective-permute-start(bf16[64,4096]{1,0:T(8,128)(2,1)S(1)} %bitcast.7), channel_id=1, source_target_pairs={{4,8},{8,4},{5,9},{9,5},{6,10},{10,6},{7,11},{11,7},{20,24},{24,20... | collective-permute-start | bytes 1572872 | tf_op jit(solution)/shard_map/ppermute | solution.py:377
  14.3 3.9 %collective-permute-start.5 = (bf16[64,4096]{1,0:T(8,128)(2,1)S(1)}, bf16[64,4096]{1,0:T(8,128)(2,1)S(1)}, u32[]{:S(2)}, u32[]{:S(2)}) collective-permute-start(bf16[64,4096]{1,0:T(8,128)(2,1)S(1)} %bitcast.8), channel_id=1, source_target_pairs={{0,4},{4,0},{8,12},{12,8},{1,5},{5,1},{9,13},{13,9},{2,6},{6,2},{1... | collective-permute-start | bytes 1572872 | tf_op jit(solution)/shard_map/ppermute | solution.py:376
  18.2 0.0 collective-permute-done.2.refs_1_
  18.2 0.7 collective-permute-done.3.refs_4_.direct
  18.9 1.0 %shard_map.106 = (bf16[64,256]{1,0:T(8,128)(2,1)S(1)}, bf16[64,4096]{1,0:T(8,128)(2,1)S(1)}, bf16[64,4096]{1,0:T(8,128)(2,1)S(1)}) custom-call(f32[64,256]{1,0:T(8,128)S(1)} %shard_map.104.refs_0_, f32[64,256]{1,0:T(8,128)S(1)} %collective-permute-done.2.refs_1_, s32[1,256]{1,0:T(1,128)S(1)} %get-tuple-element.42.deal.refs_2_.refs_1_, ...), custom_call_target="tpu_custom_call" | custom-call | flops 6899999744 | tf_op jit(solution)/shard_map/pallas_call | solution.py:264
  19.9 1.6 %collective-permute-start.7 = (bf16[64,4096]{1,0:T(8,128)(2,1)S(1)}, bf16[64,4096]{1,0:T(8,128)(2,1)S(1)}, u32[]{:S(2)}, u32[]{:S(2)}) collective-permute-start(bf16[64,4096]{1,0:T(8,128)(2,1)S(1)} %get-tuple-element.45.refs_2_), channel_id=1, source_target_pairs={{0,2},{2,0},{1,3},{3,1},{4,6},{6,4},{5,7},{7,5},{8,10},{10,8},{9,1... | collective-permute-start | bytes 1572872 | tf_op jit(solution)/shard_map/ppermute | solution.py:378
  21.4 1.6 %shard_map.107.refs_5_.own = f32[256,256]{1,0:T(8,128)S(1)} custom-call(bf16[256,4096]{1,0:T(8,128)(2,1)S(1)} %copy-done, bf16[4096,256]{1,0:T(8,128)(2,1)S(1)} %copy-done.2, bf16[64,4096]{1,0:T(8,128)(2,1)S(1)} %get-tuple-element.45.refs_2_), custom_call_target="tpu_custom_call" | custom-call | tf_op jit(solution)/shard_map/pallas_call | solution.py:264
  23.1 1.6 %collective-permute-start.4 = (bf16[1024,256]{1,0:T(8,128)(2,1)S(1)}, bf16[1024,256]{1,0:T(8,128)(2,1)S(1)}, u32[]{:S(2)}, u32[]{:S(2)}) collective-permute-start(bf16[1024,256]{1,0:T(8,128)(2,1)S(1)} %collective-permute-done.3.refs_4_.direct), channel_id=1, source_target_pairs={{0,16},{16,0},{1,17},{17,1},{2,18},{18,2},{3,19},{19,3},{4,20},{20... | collective-permute-start | bytes 1572872 | tf_op jit(solution)/shard_map/ppermute | solution.py:388
  24.7 0.8 %shard_map.108.refs_7_.refs_0_ = f32[64,4096]{1,0:T(8,128)S(1)} custom-call(bf16[64,256]{1,0:T(8,128)(2,1)S(1)} %get-tuple-element.46.grad_rank.refs_1_, s32[1,256]{1,0:T(1,128)S(1)} %get-tuple-element.42.deal.refs_2_.refs_1_, bf16[256,4096]{1,0:T(8,128)(2,1)S(1)} %copy-done), custom_call_target="tpu_custom_call" | custom-call | tf_op jit(solution)/shard_map/pallas_call | solution.py:264
  25.5 0.0 collective-permute-done.6.refs_4_.refs_2_.refs_7_.refs_3_
  25.5 4.7 %collective-permute-done.5.refs_6_.refs_1_.refs_4_ = bf16[64,4096]{1,0:T(8,128)(2,1)S(1)} collective-permute-done((bf16[64,4096]{1,0:T(8,128)(2,1)S(1)}, bf16[64,4096]{1,0:T(8,128)(2,1)S(1)}, u32[]{:S(2)}, u32[]{:S(2)}) %collective-permute-start.5) | collective-permute-done | bytes 524320 | tf_op jit(solution)/shard_map/ppermute | solution.py:376
  30.2 0.7 collective-permute-start.9
  30.9 1.8 %collective-permute-done.7.refs_0_ = bf16[64,4096]{1,0:T(8,128)(2,1)S(1)} collective-permute-done((bf16[64,4096]{1,0:T(8,128)(2,1)S(1)}, bf16[64,4096]{1,0:T(8,128)(2,1)S(1)}, u32[]{:S(2)}, u32[]{:S(2)}) %collective-permute-start.7) | collective-permute-done | bytes 524320 | tf_op jit(solution)/shard_map/ppermute | solution.py:378
  32.7 0.9 %shard_map.109 = (bf16[64,4096]{1,0:T(8,128)(2,1)S(1)}, bf16[64,4096]{1,0:T(8,128)(2,1)S(1)}) custom-call(bf16[64,4096]{1,0:T(8,128)(2,1)S(1)} %collective-permute-done.7.refs_0_, bf16[64,256]{1,0:T(8,128)(2,1)S(1)} %get-tuple-element.46.grad_rank.refs_1_, s32[1,256]{1,0:T(1,128)S(1)} %get-tuple-element.42.deal.refs_2_.refs_1_, ...), custom_call_target="tpu_custom_call" | custom-call | flops 6899999744 | tf_op jit(solution)/shard_map/pallas_call | solution.py:264
  33.6 1.5 %collective-permute-start.8 = (bf16[64,4096]{1,0:T(8,128)(2,1)S(1)}, bf16[64,4096]{1,0:T(8,128)(2,1)S(1)}, u32[]{:S(2)}, u32[]{:S(2)}) collective-permute-start(bf16[64,4096]{1,0:T(8,128)(2,1)S(1)} %get-tuple-element.49), channel_id=1, source_target_pairs={{0,4},{4,0},{8,12},{12,8},{1,5},{5,1},{9,13},{13,9},{2,6},{6,2},{1... | collective-permute-start | bytes 1572872 | tf_op jit(solution)/shard_map/ppermute | solution.py:397
  35.1 1.0 %collective-permute-start.11 = (bf16[1024,256]{1,0:T(8,128)(2,1)S(1)}, bf16[1024,256]{1,0:T(8,128)(2,1)S(1)}, u32[]{:S(2)}, u32[]{:S(2)}) collective-permute-start(bf16[1024,256]{1,0:T(8,128)(2,1)S(1)} %get-tuple-element.55), channel_id=1, source_target_pairs={{0,2},{2,0},{1,3},{3,1},{4,6},{6,4},{5,7},{7,5},{8,10},{10,8},{9,1... | collective-permute-start | bytes 1572872 | tf_op jit(solution)/shard_map/ppermute | solution.py:396
  36.1 1.8 %shard_map.111.refs_3_.refs_5_ = f32[64,256]{1,0:T(8,128)S(1)} custom-call(bf16[256,4096]{1,0:T(8,128)(2,1)S(1)} %copy-done, s32[1,256]{1,0:T(1,128)S(1)} %get-tuple-element.42.deal.refs_2_.refs_1_, s32[1,256]{1,0:T(1,128)S(1)} %get-tuple-element.43.job.refs_2_, bf16[64,4096]{1,0:T(8,128)(2,1)S(1)} %bitcast.9, ...), custom_call_target="tpu_custom_call" | custom-call | tf_op jit(solution)/shard_map/pallas_call | solution.py:264
  37.9 0.0 collective-permute-done.9.refs_4_.refs_2_.refs_9_.refs_3_
  37.9 1.3 %collective-permute-start.10 = (bf16[64,4096]{1,0:T(8,128)(2,1)S(1)}, bf16[64,4096]{1,0:T(8,128)(2,1)S(1)}, u32[]{:S(2)}, u32[]{:S(2)}) collective-permute-start(bf16[64,4096]{1,0:T(8,128)(2,1)S(1)} %collective-permute-done.9.refs_4_.refs_2_.refs_9_.refs_3_), channel_id=1, source_target_pairs={{4,0},{8,12},{5,1},{9,13},{6,2},{10,14},{7,3},{11,15},{20,16},{24,... | collective-permute-start | bytes 1572872 | tf_op jit(solution)/shard_map/ppermute | solution.py:410
  39.2 0.0 collective-permute-done.4.relayed.refs_4_
  39.2 7.1 %collective-permute-done.8.refs_3_.refs_1_.refs_8_.refs_4_ = bf16[64,4096]{1,0:T(8,128)(2,1)S(1)} collective-permute-done((bf16[64,4096]{1,0:T(8,128)(2,1)S(1)}, bf16[64,4096]{1,0:T(8,128)(2,1)S(1)}, u32[]{:S(2)}, u32[]{:S(2)}) %collective-permute-start.8) | collective-permute-done | bytes 524320 | tf_op jit(solution)/shard_map/ppermute | solution.py:397
  46.3 0.1 shard_map.112
  46.4 0.7 collective-permute-start.16
  47.1 1.0 %collective-permute-start.15 = (bf16[64,4096]{1,0:T(8,128)(2,1)S(1)}, bf16[64,4096]{1,0:T(8,128)(2,1)S(1)}, u32[]{:S(2)}, u32[]{:S(2)}) collective-permute-start(bf16[64,4096]{1,0:T(8,128)(2,1)S(1)} %get-tuple-element.63), channel_id=1, source_target_pairs={{0,2},{2,0},{1,3},{3,1},{4,6},{6,4},{5,7},{7,5},{8,10},{10,8},{9,1... | collective-permute-start | bytes 1572872 | tf_op jit(solution)/shard_map/ppermute | solution.py:408
  48.2 0.0 collective-permute-done.11.refs_3_
  48.2 1.5 %collective-permute-start.12 = (bf16[1024,256]{1,0:T(8,128)(2,1)S(1)}, bf16[1024,256]{1,0:T(8,128)(2,1)S(1)}, u32[]{:S(2)}, u32[]{:S(2)}) collective-permute-start(bf16[1024,256]{1,0:T(8,128)(2,1)S(1)} %collective-permute-done.11.refs_3_), channel_id=1, source_target_pairs={{0,16},{16,0},{1,17},{17,1},{2,18},{18,2},{3,19},{19,3},{4,20},{20... | collective-permute-start | bytes 1572872 | tf_op jit(solution)/shard_map/ppermute | solution.py:411
  49.7 1.2 %shard_map.114.refs_5_ = f32[64,256]{1,0:T(8,128)S(1)} custom-call(bf16[256,4096]{1,0:T(8,128)(2,1)S(1)} %copy-done, s32[1,256]{1,0:T(1,128)S(1)} %get-tuple-element.42.deal.refs_2_.refs_1_, s32[1,256]{1,0:T(1,128)S(1)} %get-tuple-element.43.job.refs_2_, bf16[64,4096]{1,0:T(8,128)(2,1)S(1)} %collective-permute-done.6.refs_4_.refs_2_.refs_7_.refs_3_, ...), custom_call_target="tpu_custom_call" | custom-call | tf_op jit(solution)/shard_map/pallas_call | solution.py:264
  50.8 7.4 %collective-permute-done.10.refs_5_.refs_10_.refs_4_ = bf16[64,4096]{1,0:T(8,128)(2,1)S(1)} collective-permute-done((bf16[64,4096]{1,0:T(8,128)(2,1)S(1)}, bf16[64,4096]{1,0:T(8,128)(2,1)S(1)}, u32[]{:S(2)}, u32[]{:S(2)}) %collective-permute-start.10) | collective-permute-done | bytes 524320 | tf_op jit(solution)/shard_map/ppermute | solution.py:410
  58.3 1.2 %shard_map.115.low = f32[64,256]{1,0:T(8,128)S(1)} custom-call(bf16[256,4096]{1,0:T(8,128)(2,1)S(1)} %copy-done, s32[1,256]{1,0:T(1,128)S(1)} %get-tuple-element.42.deal.refs_2_.refs_1_, s32[1,256]{1,0:T(1,128)S(1)} %get-tuple-element.43.job.refs_2_, bf16[64,4096]{1,0:T(8,128)(2,1)S(1)} %collective-permute-done.9.refs_4_.refs_2_.refs_9_.refs_3_, ...), custom_call_target="tpu_custom_call" | custom-call | tf_op jit(solution)/shard_map/pallas_call | solution.py:264
  59.4 0.1 collective-permute-start.13
  59.5 2.9 %shard_map.110 = (bf16[256,4096]{1,0:T(8,128)(2,1)}, f32[256,256]{1,0:T(8,128)S(1)}) custom-call(bf16[256,512]{1,0:T(8,128)(2,1)S(1)} %copy-done.4, bf16[64,256]{1,0:T(8,128)(2,1)S(1)} %get-tuple-element.46.grad_rank.refs_1_, s32[1,256]{1,0:T(1,128)S(1)} %get-tuple-element.42.deal.refs_2_.refs_1_, ...), custom_call_target="tpu_custom_call" | custom-call | tf_op jit(solution)/shard_map/pallas_call | solution.py:264
  62.4 0.0 collective-permute-done.13.low_got
  62.4 0.3 shard_map.116
  62.7 1.0 %collective-permute-start.18 = (bf16[128,256]{1,0:T(8,128)(2,1)S(1)}, bf16[128,256]{1,0:T(8,128)(2,1)S(1)}, u32[]{:S(2)}, u32[]{:S(2)}) collective-permute-start(bf16[128,256]{1,0:T(8,128)(2,1)S(1)} %get-tuple-element.67), channel_id=1, source_target_pairs={{0,2},{2,0},{1,3},{3,1},{4,6},{6,4},{5,7},{7,5},{8,10},{10,8},{9,1... | collective-permute-start | bytes 196616 | tf_op jit(solution)/shard_map/ppermute | solution.py:450
  63.8 0.0 collective-permute-done.16.refs_0_.refs_2_
  63.8 0.0 collective-permute-done.15.refs_1_
  63.8 0.0 collective-permute-done.12.refs_4_.refs_3_
  63.8 0.2 shard_map.119
  64.0 0.1 collective-permute-start.17
  64.0 2.9 %shard_map.113 = (bf16[256,4096]{1,0:T(8,128)(2,1)}, f32[256,256]{1,0:T(8,128)S(1)}) custom-call(bf16[256,512]{1,0:T(8,128)(2,1)S(1)} %copy-done.4, bf16[64,256]{1,0:T(8,128)(2,1)S(1)} %get-tuple-element.46.grad_rank.refs_1_, s32[1,256]{1,0:T(1,128)S(1)} %get-tuple-element.42.deal.refs_2_.refs_1_, ...), custom_call_target="tpu_custom_call", output_to_operand_aliasing={{0}: (13, {})} | custom-call | tf_op jit(solution)/shard_map/pallas_call | solution.py:264
  67.0 0.1 shard_map.117
  67.1 0.3 collective-permute-start.14
  67.3 0.0 collective-permute-done.18.got
  67.4 1.9 %collective-permute-start.19 = (bf16[32,256]{1,0:T(8,128)(2,1)S(1)}, bf16[32,256]{1,0:T(8,128)(2,1)S(1)}, u32[]{:S(2)}, u32[]{:S(2)}) collective-permute-start(bf16[32,256]{1,0:T(8,128)(2,1)S(1)} %get-tuple-element.69), channel_id=1, source_target_pairs={{0,4},{4,0},{8,12},{12,8},{1,5},{5,1},{9,13},{13,9},{2,6},{6,2},{1... | collective-permute-start | bytes 49160 | tf_op jit(solution)/shard_map/ppermute | solution.py:455
  69.2 0.5 collective-permute-start.20
  69.8 2.1 %collective-permute-start.21 = (bf16[32,256]{1,0:T(8,128)(2,1)S(1)}, bf16[32,256]{1,0:T(8,128)(2,1)S(1)}, u32[]{:S(2)}, u32[]{:S(2)}) collective-permute-start(bf16[32,256]{1,0:T(8,128)(2,1)S(1)} %get-tuple-element.71), channel_id=1, source_target_pairs={{0,12},{4,8},{8,4},{12,0},{1,13},{5,9},{9,5},{13,1},{2,14},{6,10},... | collective-permute-start | bytes 49160 | tf_op jit(solution)/shard_map/ppermute | solution.py:455
  71.8 1.0 %collective-permute-done.19.one = bf16[32,256]{1,0:T(8,128)(2,1)S(1)} collective-permute-done((bf16[32,256]{1,0:T(8,128)(2,1)S(1)}, bf16[32,256]{1,0:T(8,128)(2,1)S(1)}, u32[]{:S(2)}, u32[]{:S(2)}) %collective-permute-start.19) | collective-permute-done | bytes 16416 | tf_op jit(solution)/shard_map/ppermute | solution.py:455
  72.8 1.1 %collective-permute-done.20.two = bf16[32,256]{1,0:T(8,128)(2,1)S(1)} collective-permute-done((bf16[32,256]{1,0:T(8,128)(2,1)S(1)}, bf16[32,256]{1,0:T(8,128)(2,1)S(1)}, u32[]{:S(2)}, u32[]{:S(2)}) %collective-permute-start.20) | collective-permute-done | bytes 16416 | tf_op jit(solution)/shard_map/ppermute | solution.py:455
  73.9 1.4 %collective-permute-done.21.three = bf16[32,256]{1,0:T(8,128)(2,1)S(1)} collective-permute-done((bf16[32,256]{1,0:T(8,128)(2,1)S(1)}, bf16[32,256]{1,0:T(8,128)(2,1)S(1)}, u32[]{:S(2)}, u32[]{:S(2)}) %collective-permute-start.21) | collective-permute-done | bytes 16416 | tf_op jit(solution)/shard_map/ppermute | solution.py:455
  75.3 0.0 collective-permute-done.17.last
  75.3 0.0 collective-permute-done.14.base_got
  75.3 0.9 %shard_map.121 = (bf16[256,256]{1,0:T(8,128)(2,1)}, f32[32,4096]{1,0:T(8,128)}, f32[32,256]{1,0:T(8,128)}) custom-call(f32[256,256]{1,0:T(8,128)S(1)} %get-tuple-element.60.base_keep, f32[256,256]{1,0:T(8,128)S(1)} %collective-permute-done.14.base_got, f32[32,4096]{1,0:T(8,128)S(1)} %get-tuple-element.64.mine, ...), custom_call_target="tpu_custom_call" | custom-call | flops 17250000896 | tf_op jit(solution)/shard_map/pallas_call | solution.py:264
  (16 shorter events, 0.0 us)
Async XLA Ops:
  0.6 6.4 %copy-start.6 = (s32[256,1]{0,1:T(1,128)S(1)}, s32[256,1]{0,1:T(1,128)}, u32[]{:S(2)}) copy-start(s32[256,1]{0,1:T(1,128)} %param.12) | copy-start | bytes 3076
  0.6 6.5 %collective-permute-start = (bf16[64,256]{1,0:T(8,128)(2,1)}, bf16[64,256]{1,0:T(8,128)(2,1)S(1)}, u32[]{:S(2)}, u32[]{:S(2)}) collective-permute-start(bf16[64,256]{1,0:T(8,128)(2,1)} %bitcast.12), channel_id=1, source_target_pairs={{0,4},{4,0},{8,12},{12,8},{1,5},{5,1},{9,13},{13,9},{2,6},{6,2},{1... | collective-permute-start | bytes 98312 | tf_op jit(solution)/shard_map/ppermute | solution.py:347
  3.7 1.6 %copy-start.1 = (bf16[4096,256]{1,0:T(8,128)(2,1)S(1)}, bf16[4096,256]{1,0:T(8,128)(2,1)}, u32[]{:S(2)}) copy-start(bf16[4096,256]{1,0:T(8,128)(2,1)} %refs_12_.1) | copy-start | bytes 6291460
  5.3 1.7 %copy-start.3 = (bf16[4,16,4096]{2,1,0:T(8,128)(2,1)S(1)}, bf16[4,16,4096]{2,1,0:T(8,128)(2,1)}, u32[]{:S(2)}) copy-start(bf16[4,16,4096]{2,1,0:T(8,128)(2,1)} %param.10) | copy-start | bytes 1572868
  5.3 1.7 %copy-start.4 = (bf16[256,512]{1,0:T(8,128)(2,1)S(1)}, bf16[256,512]{1,0:T(8,128)(2,1)}, u32[]{:S(2)}) copy-start(bf16[256,512]{1,0:T(8,128)(2,1)} %refs_0_.7) | copy-start | bytes 786436
  5.3 1.7 %copy-start.5 = (bf16[4,16,256]{2,1,0:T(8,128)(2,1)S(1)}, bf16[4,16,256]{2,1,0:T(8,128)(2,1)}, u32[]{:S(2)}) copy-start(bf16[4,16,256]{2,1,0:T(8,128)(2,1)} %param.11) | copy-start | bytes 98308
  5.3 1.7 %copy-start.7 = (s32[256]{0:T(256)S(1)}, s32[256]{0:T(256)}, u32[]{:S(2)}) copy-start(s32[256]{0:T(256)} %param.13) | copy-start | bytes 3076
  5.4 13.4 %collective-permute-start.3 = (bf16[1024,256]{1,0:T(8,128)(2,1)S(1)}, bf16[1024,256]{1,0:T(8,128)(2,1)S(1)}, u32[]{:S(2)}, u32[]{:S(2)}) collective-permute-start(bf16[1024,256]{1,0:T(8,128)(2,1)S(1)} %get-tuple-element.44), channel_id=1, source_target_pairs={{0,2},{2,0},{1,3},{3,1},{4,6},{6,4},{5,7},{7,5},{8,10},{10,8},{9,1... | collective-permute-start | bytes 1572872 | tf_op jit(solution)/shard_map/ppermute | solution.py:364
  7.2 5.9 %collective-permute-start.1 = (bf16[128,256]{1,0:T(8,128)(2,1)S(1)}, bf16[128,256]{1,0:T(8,128)(2,1)S(1)}, u32[]{:S(2)}, u32[]{:S(2)}) collective-permute-start(bf16[128,256]{1,0:T(8,128)(2,1)S(1)} %shard_map.103.near), channel_id=1, source_target_pairs={{0,8},{4,12},{8,0},{12,4},{1,9},{5,13},{9,1},{13,5},{2,10},{6,14},... | collective-permute-start | bytes 196616 | tf_op jit(solution)/shard_map/ppermute | solution.py:355
  13.1 5.8 %copy-start = (bf16[256,4096]{1,0:T(8,128)(2,1)S(1)}, bf16[256,4096]{1,0:T(8,128)(2,1)}, u32[]{:S(2)}) copy-start(bf16[256,4096]{1,0:T(8,128)(2,1)} %refs_0_.9) | copy-start | bytes 6291460
  13.4 8.0 %copy-start.2 = (bf16[4096,256]{1,0:T(8,128)(2,1)S(1)}, bf16[4096,256]{1,0:T(8,128)(2,1)}, u32[]{:S(2)}) copy-start(bf16[4096,256]{1,0:T(8,128)(2,1)} %refs_12_.1) | copy-start | bytes 6291460
  13.4 4.8 %collective-permute-start.2 = (f32[64,256]{1,0:T(8,128)S(1)}, f32[64,256]{1,0:T(8,128)S(1)}, u32[]{:S(2)}, u32[]{:S(2)}) collective-permute-start(f32[64,256]{1,0:T(8,128)S(1)} %shard_map.104.refs_0_), channel_id=1, source_target_pairs={{0,1},{1,0},{2,3},{3,2},{4,5},{5,4},{6,7},{7,6},{8,9},{9,8},{10,11... | collective-permute-start | bytes 196616 | tf_op jit(solution)/shard_map/ppermute | solution.py:370
  13.5 12.0 %collective-permute-start.6 = (bf16[64,4096]{1,0:T(8,128)(2,1)S(1)}, bf16[64,4096]{1,0:T(8,128)(2,1)S(1)}, u32[]{:S(2)}, u32[]{:S(2)}) collective-permute-start(bf16[64,4096]{1,0:T(8,128)(2,1)S(1)} %bitcast.7), channel_id=1, source_target_pairs={{4,8},{8,4},{5,9},{9,5},{6,10},{10,6},{7,11},{11,7},{20,24},{24,20... | collective-permute-start | bytes 1572872 | tf_op jit(solution)/shard_map/ppermute | solution.py:377
  14.3 15.9 %collective-permute-start.5 = (bf16[64,4096]{1,0:T(8,128)(2,1)S(1)}, bf16[64,4096]{1,0:T(8,128)(2,1)S(1)}, u32[]{:S(2)}, u32[]{:S(2)}) collective-permute-start(bf16[64,4096]{1,0:T(8,128)(2,1)S(1)} %bitcast.8), channel_id=1, source_target_pairs={{0,4},{4,0},{8,12},{12,8},{1,5},{5,1},{9,13},{13,9},{2,6},{6,2},{1... | collective-permute-start | bytes 1572872 | tf_op jit(solution)/shard_map/ppermute | solution.py:376
  19.9 12.8 %collective-permute-start.7 = (bf16[64,4096]{1,0:T(8,128)(2,1)S(1)}, bf16[64,4096]{1,0:T(8,128)(2,1)S(1)}, u32[]{:S(2)}, u32[]{:S(2)}) collective-permute-start(bf16[64,4096]{1,0:T(8,128)(2,1)S(1)} %get-tuple-element.45.refs_2_), channel_id=1, source_target_pairs={{0,2},{2,0},{1,3},{3,1},{4,6},{6,4},{5,7},{7,5},{8,10},{10,8},{9,1... | collective-permute-start | bytes 1572872 | tf_op jit(solution)/shard_map/ppermute | solution.py:378
  23.1 16.1 %collective-permute-start.4 = (bf16[1024,256]{1,0:T(8,128)(2,1)S(1)}, bf16[1024,256]{1,0:T(8,128)(2,1)S(1)}, u32[]{:S(2)}, u32[]{:S(2)}) collective-permute-start(bf16[1024,256]{1,0:T(8,128)(2,1)S(1)} %collective-permute-done.3.refs_4_.direct), channel_id=1, source_target_pairs={{0,16},{16,0},{1,17},{17,1},{2,18},{18,2},{3,19},{19,3},{4,20},{20... | collective-permute-start | bytes 1572872 | tf_op jit(solution)/shard_map/ppermute | solution.py:388
  30.2 7.7 %collective-permute-start.9 = (bf16[64,4096]{1,0:T(8,128)(2,1)S(1)}, bf16[64,4096]{1,0:T(8,128)(2,1)S(1)}, u32[]{:S(2)}, u32[]{:S(2)}) collective-permute-start(bf16[64,4096]{1,0:T(8,128)(2,1)S(1)} %collective-permute-done.5.refs_6_.refs_1_.refs_4_), channel_id=1, source_target_pairs={{4,8},{8,4},{5,9},{9,5},{6,10},{10,6},{7,11},{11,7},{20,24},{24,20... | collective-permute-start | bytes 1572872 | tf_op jit(solution)/shard_map/ppermute | solution.py:398
  33.6 12.7 %collective-permute-start.8 = (bf16[64,4096]{1,0:T(8,128)(2,1)S(1)}, bf16[64,4096]{1,0:T(8,128)(2,1)S(1)}, u32[]{:S(2)}, u32[]{:S(2)}) collective-permute-start(bf16[64,4096]{1,0:T(8,128)(2,1)S(1)} %get-tuple-element.49), channel_id=1, source_target_pairs={{0,4},{4,0},{8,12},{12,8},{1,5},{5,1},{9,13},{13,9},{2,6},{6,2},{1... | collective-permute-start | bytes 1572872 | tf_op jit(solution)/shard_map/ppermute | solution.py:397
  35.1 13.1 %collective-permute-start.11 = (bf16[1024,256]{1,0:T(8,128)(2,1)S(1)}, bf16[1024,256]{1,0:T(8,128)(2,1)S(1)}, u32[]{:S(2)}, u32[]{:S(2)}) collective-permute-start(bf16[1024,256]{1,0:T(8,128)(2,1)S(1)} %get-tuple-element.55), channel_id=1, source_target_pairs={{0,2},{2,0},{1,3},{3,1},{4,6},{6,4},{5,7},{7,5},{8,10},{10,8},{9,1... | collective-permute-start | bytes 1572872 | tf_op jit(solution)/shard_map/ppermute | solution.py:396
  37.9 20.4 %collective-permute-start.10 = (bf16[64,4096]{1,0:T(8,128)(2,1)S(1)}, bf16[64,4096]{1,0:T(8,128)(2,1)S(1)}, u32[]{:S(2)}, u32[]{:S(2)}) collective-permute-start(bf16[64,4096]{1,0:T(8,128)(2,1)S(1)} %collective-permute-done.9.refs_4_.refs_2_.refs_9_.refs_3_), channel_id=1, source_target_pairs={{4,0},{8,12},{5,1},{9,13},{6,2},{10,14},{7,3},{11,15},{20,16},{24,... | collective-permute-start | bytes 1572872 | tf_op jit(solution)/shard_map/ppermute | solution.py:410
  46.4 17.3 %collective-permute-start.16 = (bf16[64,4096]{1,0:T(8,128)(2,1)S(1)}, bf16[64,4096]{1,0:T(8,128)(2,1)S(1)}, u32[]{:S(2)}, u32[]{:S(2)}) collective-permute-start(bf16[64,4096]{1,0:T(8,128)(2,1)S(1)} %shard_map.112), channel_id=1, source_target_pairs={{4,8},{8,4},{5,9},{9,5},{6,10},{10,6},{7,11},{11,7},{20,24},{24,20... | collective-permute-start | bytes 1572872 | tf_op jit(solution)/shard_map/ppermute | solution.py:409
  47.1 16.6 %collective-permute-start.15 = (bf16[64,4096]{1,0:T(8,128)(2,1)S(1)}, bf16[64,4096]{1,0:T(8,128)(2,1)S(1)}, u32[]{:S(2)}, u32[]{:S(2)}) collective-permute-start(bf16[64,4096]{1,0:T(8,128)(2,1)S(1)} %get-tuple-element.63), channel_id=1, source_target_pairs={{0,2},{2,0},{1,3},{3,1},{4,6},{6,4},{5,7},{7,5},{8,10},{10,8},{9,1... | collective-permute-start | bytes 1572872 | tf_op jit(solution)/shard_map/ppermute | solution.py:408
  48.2 15.6 %collective-permute-start.12 = (bf16[1024,256]{1,0:T(8,128)(2,1)S(1)}, bf16[1024,256]{1,0:T(8,128)(2,1)S(1)}, u32[]{:S(2)}, u32[]{:S(2)}) collective-permute-start(bf16[1024,256]{1,0:T(8,128)(2,1)S(1)} %collective-permute-done.11.refs_3_), channel_id=1, source_target_pairs={{0,16},{16,0},{1,17},{17,1},{2,18},{18,2},{3,19},{19,3},{4,20},{20... | collective-permute-start | bytes 1572872 | tf_op jit(solution)/shard_map/ppermute | solution.py:411
  59.4 3.0 %collective-permute-start.13 = (f32[64,256]{1,0:T(8,128)S(1)}, f32[64,256]{1,0:T(8,128)S(1)}, u32[]{:S(2)}, u32[]{:S(2)}) collective-permute-start(f32[64,256]{1,0:T(8,128)S(1)} %shard_map.115.low), channel_id=1, source_target_pairs={{0,1},{1,0},{2,3},{3,2},{4,5},{5,4},{6,7},{7,6},{8,9},{9,8},{10,11... | collective-permute-start | bytes 196616 | tf_op jit(solution)/shard_map/ppermute | solution.py:415
  62.7 4.6 %collective-permute-start.18 = (bf16[128,256]{1,0:T(8,128)(2,1)S(1)}, bf16[128,256]{1,0:T(8,128)(2,1)S(1)}, u32[]{:S(2)}, u32[]{:S(2)}) collective-permute-start(bf16[128,256]{1,0:T(8,128)(2,1)S(1)} %get-tuple-element.67), channel_id=1, source_target_pairs={{0,2},{2,0},{1,3},{3,1},{4,6},{6,4},{5,7},{7,5},{8,10},{10,8},{9,1... | collective-permute-start | bytes 196616 | tf_op jit(solution)/shard_map/ppermute | solution.py:450
  64.0 11.3 %collective-permute-start.17 = (bf16[32,4096]{1,0:T(8,128)(2,1)S(1)}, bf16[32,4096]{1,0:T(8,128)(2,1)S(1)}, u32[]{:S(2)}, u32[]{:S(2)}) collective-permute-start(bf16[32,4096]{1,0:T(8,128)(2,1)S(1)} %get-tuple-element.65), channel_id=1, source_target_pairs={{0,4},{4,0},{8,12},{12,8},{1,5},{5,1},{9,13},{13,9},{2,6},{6,2},{1... | collective-permute-start | bytes 786440 | tf_op jit(solution)/shard_map/ppermute | solution.py:449
  67.1 8.2 %collective-permute-start.14 = (f32[256,256]{1,0:T(8,128)S(1)}, f32[256,256]{1,0:T(8,128)S(1)}, u32[]{:S(2)}, u32[]{:S(2)}) collective-permute-start(f32[256,256]{1,0:T(8,128)S(1)} %get-tuple-element.61), channel_id=1, source_target_pairs={{0,1},{1,0},{2,3},{3,2},{4,5},{5,4},{6,7},{7,6},{8,9},{9,8},{10,11... | collective-permute-start | bytes 786440 | tf_op jit(solution)/shard_map/ppermute | solution.py:458
  67.4 5.4 %collective-permute-start.19 = (bf16[32,256]{1,0:T(8,128)(2,1)S(1)}, bf16[32,256]{1,0:T(8,128)(2,1)S(1)}, u32[]{:S(2)}, u32[]{:S(2)}) collective-permute-start(bf16[32,256]{1,0:T(8,128)(2,1)S(1)} %get-tuple-element.69), channel_id=1, source_target_pairs={{0,4},{4,0},{8,12},{12,8},{1,5},{5,1},{9,13},{13,9},{2,6},{6,2},{1... | collective-permute-start | bytes 49160 | tf_op jit(solution)/shard_map/ppermute | solution.py:455
  69.2 4.6 %collective-permute-start.20 = (bf16[32,256]{1,0:T(8,128)(2,1)S(1)}, bf16[32,256]{1,0:T(8,128)(2,1)S(1)}, u32[]{:S(2)}, u32[]{:S(2)}) collective-permute-start(bf16[32,256]{1,0:T(8,128)(2,1)S(1)} %get-tuple-element.70), channel_id=1, source_target_pairs={{0,8},{4,12},{8,0},{12,4},{1,9},{5,13},{9,1},{13,5},{2,10},{6,14},... | collective-permute-start | bytes 49160 | tf_op jit(solution)/shard_map/ppermute | solution.py:455
  69.8 5.5 %collective-permute-start.21 = (bf16[32,256]{1,0:T(8,128)(2,1)S(1)}, bf16[32,256]{1,0:T(8,128)(2,1)S(1)}, u32[]{:S(2)}, u32[]{:S(2)}) collective-permute-start(bf16[32,256]{1,0:T(8,128)(2,1)S(1)} %get-tuple-element.71), channel_id=1, source_target_pairs={{0,12},{4,8},{8,4},{12,0},{1,13},{5,9},{9,5},{13,1},{2,14},{6,10},... | collective-permute-start | bytes 49160 | tf_op jit(solution)/shard_map/ppermute | solution.py:455
